TPU v7x, 32 devices: a whole 2x2x4 slice. The times are simulated.
32 devices in a mesh: gx: 4 (over x, core), gy: 4 (over z), gz: 2 (over y).
Axes of the slice: x: 2, y: 2, z: 4, core: 2. Of those that a mesh axis runs over, the one named last changes fastest.
Arguments:
- initial_wind: float32 [3, 64, 512, 1024], P(None, 'gz', 'gx', 'gy'), may hold values from -4 to 4
- building_mask: int32 [64, 512, 1024], P('gz', 'gx', 'gy'), may hold values 0 or 1
- surface_flags: int32 [512, 1024], P('gx', 'gy'), may hold values from 0 to 3
- scalars: float32 [4, 64, 512, 1024], P(None, 'gz', 'gx', 'gy'), may hold values from 0 to 2
Outputs:
- corrected_wind: float32 [3, 64, 512, 1024], P(None, 'gz', 'gx', 'gy')
- transported: float32 [4, 64, 512, 1024], P(None, 'gz', 'gx', 'gy')
Inputs may be any that keep to these rules, and one draw needn't show every extreme that they name: `building_mask`: 1 marks a building cell.
All inputs are finite; a program needn't handle non-finite values. No bound on the sum of `building_mask` on one device may be relied on, other than what follows from the above.
Results may differ from a plain program's by a relative error of at most 0.0003.
Values sent between devices are 32-bit elements; how exact they have to be, the bound alone decides.
No kernel may reach another device: no remote copies, remote signals or barrier semaphores. Data moves between devices by JAX's collectives and lax.ppermute only.
A program may use at most 512 MiB of HBM per device.

v0:
```python
import math

import jax
import jax.numpy as jnp
from jax import lax
from jax.sharding import PartitionSpec as P

TIME_STEP = 0.2
ANISOTROPY = 4.0
DEPOSIT = (
    (0.0, 0.25, 0.75, 1.5),
    (0.0, 0.5, 1.0, 2.0),
    (0.1, 0.4, 0.8, 1.6),
    (0.0, 0.15, 1.25, 2.5),
)


def with_halo(block, sides, width):
    for axis, dim in sides:
        count = lax.axis_size(axis)
        forward = [(i, i + 1) for i in range(count - 1)]
        backward = [(target, source) for source, target in forward]
        low = lax.ppermute(
            lax.slice_in_dim(block, block.shape[dim] - width, None, axis=dim), axis, forward
        )
        high = lax.ppermute(lax.slice_in_dim(block, 0, width, axis=dim), axis, backward)
        block = jnp.concatenate([low, block, high], axis=dim)
    return block


def basis_table(sine_kind, extent, spectral, spatial):
    wavenumber = spectral[:, None]
    position = spatial[None, :]
    if sine_kind:
        phase_index = (wavenumber + 1) * (2 * position + 1) % (4 * extent)
        weight = jnp.where(
            wavenumber == extent - 1, math.sqrt(1.0 / extent), math.sqrt(2.0 / extent)
        )
        return weight * jnp.sin(phase_index.astype(jnp.float32) * (math.pi / (2 * extent)))
    phase_index = wavenumber * (2 * position + 1) % (4 * extent)
    weight = jnp.where(wavenumber == 0, math.sqrt(1.0 / extent), math.sqrt(2.0 / extent))
    return weight * jnp.cos(phase_index.astype(jnp.float32) * (math.pi / (2 * extent)))


def eigenvalues(sine_kind, extent, spectral):
    offset_one = 1 if sine_kind else 0
    half_angle = (spectral + offset_one).astype(jnp.float32) * (math.pi / (2 * extent))
    return 4.0 * jnp.sin(half_angle) ** 2


def denominator(index_z, index_x, index_y, total_z, total_x, total_y):
    return (
        eigenvalues(True, total_x, index_x)[None, :, None]
        + eigenvalues(True, total_y, index_y)[None, None, :]
        + ANISOTROPY * eigenvalues(False, total_z, index_z)[:, None, None]
    )


def contract(grid_field, matrix, direction):
    if direction == 0:
        return jnp.einsum("ka,abc->kbc", matrix, grid_field, precision=lax.Precision.HIGHEST)
    if direction == 1:
        return jnp.einsum("kb,abc->akc", matrix, grid_field, precision=lax.Precision.HIGHEST)
    return jnp.einsum("kc,abc->abk", matrix, grid_field, precision=lax.Precision.HIGHEST)


def limiter_ratio(demand, supply):
    binding = demand > supply
    return jnp.where(binding, supply / jnp.where(binding, demand, 1.0), 1.0)


def ground_factor(surface_flags):
    deposit_rates = 1.0 - TIME_STEP * jnp.asarray(DEPOSIT, dtype=jnp.float32)
    factor = jnp.zeros((deposit_rates.shape[0],) + surface_flags.shape, jnp.float32)
    for surface in range(4):
        factor = factor + jnp.where(
            surface_flags[None] == surface, deposit_rates[:, surface][:, None, None], 0.0
        )
    return factor


def y_edges(values):
    return jnp.stack([values[:, :, :, 0], values[:, :, :, -1]], axis=1)


def rim_layers(padded, edges):
    lower_z = padded[:, 0, 1:-1, :]
    upper_z = padded[:, -1, 1:-1, :]
    inner = padded[:, 1:-1]
    lower_x = inner[:, :, 0, :]
    upper_x = inner[:, :, -1, :]
    return {1: (lower_z, upper_z), 2: (lower_x, upper_x), 3: (edges[:, 0], edges[:, 3])}


def rim_part(rims, begin, end):
    return {key: (pair[0][begin:end], pair[1][begin:end]) for key, pair in rims.items()}


def first_layer(values, direction):
    return lax.index_in_dim(values, 0, direction, keepdims=False)


def after_cell(values, upper, direction):
    extent = values.shape[direction]
    return jnp.concatenate(
        [lax.slice_in_dim(values, 1, extent, axis=direction), jnp.expand_dims(upper, direction)],
        axis=direction,
    )


def before_cell(values, lower, direction):
    extent = values.shape[direction]
    return jnp.concatenate(
        [
            jnp.expand_dims(lower, direction),
            lax.slice_in_dim(values, 0, extent - 1, axis=direction),
        ],
        axis=direction,
    )


def along_x(grid_field, matrix):

    def transform_pencil(pencil_part):
        return contract(pencil_part, matrix, 1)

    pencil = transform_pencil(
        lax.all_to_all(grid_field, "gx", split_axis=0, concat_axis=1, tiled=True)
    )
    return lax.all_to_all(pencil, "gx", split_axis=1, concat_axis=0, tiled=True)


def along_y(grid_field, matrix):

    def transform_pencil(pencil_part):
        return contract(pencil_part, matrix, 2)

    pencil = transform_pencil(
        lax.all_to_all(grid_field, "gy", split_axis=0, concat_axis=2, tiled=True)
    )
    return lax.all_to_all(pencil, "gy", split_axis=2, concat_axis=0, tiled=True)


def along_z(grid_field, matrix):

    def transform_pencil(pencil_part):
        return contract(pencil_part, matrix, 0)

    pencil = transform_pencil(
        lax.all_to_all(grid_field, "gz", split_axis=1, concat_axis=0, tiled=True)
    )
    return lax.all_to_all(pencil, "gz", split_axis=0, concat_axis=1, tiled=True)


def body(initial_wind, building_mask, surface_flags, scalars):
    local_z, local_x, local_y = building_mask.shape
    devices_x = lax.axis_size("gx")
    devices_y = lax.axis_size("gy")
    devices_z = lax.axis_size("gz")
    total_x = local_x * devices_x
    total_y = local_y * devices_y
    total_z = local_z * devices_z
    spatial_axes = (2, 3, 1)
    correction_gains = (0.5, 0.5, 0.5 * ANISOTROPY)
    scalar_count = scalars.shape[0]
    openness = 1.0 - building_mask.astype(jnp.float32)
    cell_data = jnp.concatenate([initial_wind, openness[None]], 0)
    cell_padded = with_halo(cell_data, (("gx", 2), ("gz", 1)), 1)
    cell_edge = with_halo(y_edges(cell_data), (("gy", 1),), 1)
    cell_rims = rim_layers(cell_padded, cell_edge)
    open_cells = cell_data[3:4]
    face_open = []
    open_lower = []
    masked = []
    masked_lower = []
    divergence = jnp.zeros((1, local_z, local_x, local_y), jnp.float32)
    for component in range(3):
        direction = spatial_axes[component]
        open_low, open_high = (cell_rims[direction][0][3:4], cell_rims[direction][1][3:4])
        wind_low = cell_rims[direction][0][component : component + 1]
        open_faces = open_cells * after_cell(open_cells, open_high, direction)
        masked_part = cell_data[component : component + 1] * open_faces
        open_face_low = open_low * first_layer(open_cells, direction)
        masked_low = wind_low * open_face_low
        divergence = divergence + (masked_part - before_cell(masked_part, masked_low, direction))
        face_open.append(open_faces)
        open_lower.append(open_face_low)
        masked.append(masked_part)
        masked_lower.append(masked_low)
    waves_z = jnp.arange(total_z, dtype=jnp.int32)
    waves_x = jnp.arange(total_x, dtype=jnp.int32)
    waves_y = jnp.arange(total_y, dtype=jnp.int32)
    cosine_z = basis_table(False, total_z, waves_z, waves_z)
    sine_x = basis_table(True, total_x, waves_x, waves_x)
    sine_y = basis_table(True, total_y, waves_y, waves_y)
    source = divergence[0]
    spectrum = along_z(along_y(along_x(source, sine_x), sine_y), cosine_z)
    index_z = lax.axis_index("gz") * local_z + jnp.arange(local_z, dtype=jnp.int32)
    index_x = lax.axis_index("gx") * local_x + jnp.arange(local_x, dtype=jnp.int32)
    index_y = lax.axis_index("gy") * local_y + jnp.arange(local_y, dtype=jnp.int32)
    solved = 2.0 * spectrum / denominator(index_z, index_x, index_y, total_z, total_x, total_y)
    multiplier = along_x(along_y(along_z(solved, cosine_z.T), sine_y.T), sine_x.T)
    mult_cells = multiplier[None]
    mult_padded = with_halo(mult_cells, (("gx", 2), ("gz", 1)), 1)
    mult_edge = with_halo(y_edges(mult_cells), (("gy", 1),), 1)
    mult_rims = rim_layers(mult_padded, mult_edge)
    winds = []
    winds_lower = []
    for component in range(3):
        direction = spatial_axes[component]
        mult_low, mult_high = mult_rims[direction]
        gain = correction_gains[component]
        gradient = after_cell(mult_cells, mult_high, direction) - mult_cells
        winds.append((masked[component] + gain * gradient) * face_open[component])
        low_gradient = first_layer(mult_cells, direction) - mult_low
        winds_lower.append((masked_lower[component] + gain * low_gradient) * open_lower[component])
    corrected_wind = jnp.concatenate(winds, 0)
    conc_padded = with_halo(scalars, (("gx", 2), ("gz", 1)), 1)
    conc_edge = with_halo(y_edges(scalars), (("gy", 1),), 1)
    conc_rims = rim_layers(conc_padded, conc_edge)
    anti_parts = []
    anti_before = []
    anti_lower = []
    change = jnp.zeros(scalars.shape, jnp.float32)
    for component in range(3):
        direction = spatial_axes[component]
        conc_low, conc_high = conc_rims[direction]
        velocity = winds[component]
        velocity_low = winds_lower[component]
        downwind = after_cell(scalars, conc_high, direction)
        upwind_flux = jnp.maximum(velocity, 0.0) * scalars + jnp.minimum(velocity, 0.0) * downwind
        anti_flux = 0.5 * velocity * (scalars + downwind) - upwind_flux
        first_conc = first_layer(scalars, direction)
        upwind_low = (
            jnp.maximum(velocity_low, 0.0) * conc_low + jnp.minimum(velocity_low, 0.0) * first_conc
        )
        anti_low = 0.5 * velocity_low * (conc_low + first_conc) - upwind_low
        change = change + (upwind_flux - before_cell(upwind_flux, upwind_low, direction))
        anti_parts.append(anti_flux)
        anti_lower.append(anti_low)
        anti_before.append(before_cell(anti_flux, anti_low, direction))
    trial_value = scalars - TIME_STEP * change
    trial_padded = with_halo(trial_value, (("gx", 2), ("gz", 1)), 1)
    trial_edge = with_halo(y_edges(trial_value), (("gy", 1),), 1)
    trial_rims = rim_layers(trial_padded, trial_edge)
    upper_bound = jnp.maximum(scalars, trial_value)
    lower_bound = jnp.minimum(scalars, trial_value)
    ceiling = upper_bound
    bottom = lower_bound
    for component in range(3):
        direction = spatial_axes[component]
        conc_low, conc_high = conc_rims[direction]
        trial_low, trial_high = trial_rims[direction]
        ceiling = jnp.maximum(
            ceiling, after_cell(upper_bound, jnp.maximum(conc_high, trial_high), direction)
        )
        ceiling = jnp.maximum(
            ceiling, before_cell(upper_bound, jnp.maximum(conc_low, trial_low), direction)
        )
        bottom = jnp.minimum(
            bottom, after_cell(lower_bound, jnp.minimum(conc_high, trial_high), direction)
        )
        bottom = jnp.minimum(
            bottom, before_cell(lower_bound, jnp.minimum(conc_low, trial_low), direction)
        )
    inflow = jnp.zeros(scalars.shape, jnp.float32)
    outflow = jnp.zeros(scalars.shape, jnp.float32)
    for component in range(3):
        anti_flux = anti_parts[component]
        before = anti_before[component]
        inflow = inflow + (jnp.maximum(before, 0.0) - jnp.minimum(anti_flux, 0.0))
        outflow = outflow + (jnp.maximum(anti_flux, 0.0) - jnp.minimum(before, 0.0))
    ratio_up = limiter_ratio(TIME_STEP * inflow, ceiling - trial_value)
    ratio_down = limiter_ratio(TIME_STEP * outflow, trial_value - bottom)
    ratios = jnp.concatenate([ratio_up, ratio_down], 0)
    ratio_padded = with_halo(ratios, (("gx", 2), ("gz", 1)), 1)
    ratio_edge = with_halo(y_edges(ratios), (("gy", 1),), 1)
    ratio_rims = rim_layers(ratio_padded, ratio_edge)
    up_rims = rim_part(ratio_rims, 0, scalar_count)
    down_rims = rim_part(ratio_rims, scalar_count, 2 * scalar_count)
    correction = jnp.zeros(scalars.shape, jnp.float32)
    for component in range(3):
        direction = spatial_axes[component]
        anti_flux = anti_parts[component]
        anti_low = anti_lower[component]
        up_low, up_high = up_rims[direction]
        down_low, down_high = down_rims[direction]
        next_up = after_cell(ratio_up, up_high, direction)
        next_down = after_cell(ratio_down, down_high, direction)
        limited = (
            jnp.where(
                anti_flux >= 0.0, jnp.minimum(next_up, ratio_down), jnp.minimum(ratio_up, next_down)
            )
            * anti_flux
        )
        limited_low = (
            jnp.where(
                anti_low >= 0.0,
                jnp.minimum(first_layer(ratio_up, direction), down_low),
                jnp.minimum(up_low, first_layer(ratio_down, direction)),
            )
            * anti_low
        )
        correction = correction + (limited - before_cell(limited, limited_low, direction))
    advected = trial_value - TIME_STEP * correction
    ground = lax.axis_index("gz") * local_z + jnp.arange(local_z, dtype=jnp.int32) == 0
    factors = ground_factor(surface_flags)
    transported = jnp.where(ground[None, :, None, None], advected * factors[:, None], advected)
    return (corrected_wind, transported)


def solution(mesh):
    in_specs = (
        P(None, "gz", "gx", "gy"),
        P("gz", "gx", "gy"),
        P("gx", "gy"),
        P(None, "gz", "gx", "gy"),
    )
    out_specs = (P(None, "gz", "gx", "gy"), P(None, "gz", "gx", "gy"))
    return jax.shard_map(body, mesh=mesh, in_specs=in_specs, out_specs=out_specs, check_vma=False)
```

profile of v0, /device:TPU:5, one launch (start us, length us, event | category | flops | bytes accessed | tf_op | source)
XLA Modules:
  0.0 2373.5 jit_solution(4259825616070363772)
XLA Ops:
  13.3 12.8 copy.1489
  26.0 24.7 %fusion.1 = (f32[4,32,1,256]{2,1,0,3:T(8,128)}, f32[4,32,1,256]{2,1,0,3:T(8,128)}) fusion(f32[3,32,128,256]{2,1,0,3:T(8,128)} %copy.1489, f32[1,32,128,256]{2,1,0,3:T(8,128)} %bitcast.254), kind=kLoop, calls=%fused_computation.10 | loop fusion | flops 65536 | bytes 17039360 | tf_op jit(solution)/shard_map/concatenate | solution.py:167
  129.7 13.7 copy.1504
  143.4 13.6 copy.1505
  157.0 14.1 pad_maximum_fusion.12
  197.6 16.6 fusion.79
  220.6 13.1 fusion.43
  238.8 45.3 %all-to-all-done = f32[32,128,256]{1,2,0:T(8,128)} async-done(((f32[32,128,256]{1,2,0:T(8,128)}), f32[32,128,256]{1,2,0:T(8,128)}, u32[]{:S(2)}, u32[]{:S(2)}) %all-to-all-start) | async-done | bytes 4194336 | tf_op jit(solution)/shard_map/all_to_all | solution.py:128
  284.1 14.6 fusion.59
  304.1 53.2 %all_to_all.204 = f32[8,512,256]{2,0,1:T(8,128)S(1)} all-to-all(f32[8,512,256]{2,0,1:T(8,128)} %copy.1513), channel_id=1, replica_groups=mesh['gx'=4,'gy'=4,'gz'=2] {'gx'}, dimensions={1} | all-to-all | bytes 8388608 | tf_op jit(solution)/shard_map/all_to_all | solution.py:130
  365.9 17.1 fusion.206
  383.0 75.6 %all-to-all-done.2 = f32[32,128,256]{2,1,0:T(8,128)} async-done(((f32[32,128,256]{2,1,0:T(8,128)}), f32[32,128,256]{2,1,0:T(8,128)}, u32[]{:S(2)}, u32[]{:S(2)}) %all-to-all-start.2) | async-done | bytes 4194336 | tf_op jit(solution)/shard_map/all_to_all | solution.py:139
  462.0 14.7 fusion.57
  482.1 98.1 %all_to_all.205 = f32[8,128,1024]{1,0,2:T(8,128)} all-to-all(f32[8,128,1024]{1,0,2:T(8,128)} %copy.1517), channel_id=1, replica_groups=mesh['gx'=4,'gy'=4,'gz'=2] {'gy'}, dimensions={2} | all-to-all | bytes 8388608 | tf_op jit(solution)/shard_map/all_to_all | solution.py:141
  600.1 44.4 %all-to-all-done.4 = f32[32,128,256]{2,0,1:T(8,128)} async-done(((f32[32,128,256]{2,0,1:T(8,128)}), f32[32,128,256]{2,0,1:T(8,128)}, u32[]{:S(2)}, u32[]{:S(2)}) %all-to-all-start.4) | async-done | bytes 4194336 | tf_op jit(solution)/shard_map/all_to_all | solution.py:150
  662.4 43.2 %all-to-all-done.5 = f32[64,64,256]{2,1,0:T(8,128)} async-done(((f32[64,64,256]{2,1,0:T(8,128)}), f32[64,64,256]{2,1,0:T(8,128)}, u32[]{:S(2)}, u32[]{:S(2)}) %all-to-all-start.5) | async-done | bytes 4194336 | tf_op jit(solution)/shard_map/all_to_all | solution.py:152
  712.2 46.3 %all_to_all.206 = f32[32,128,256]{2,0,1:T(8,128)S(1)} all-to-all(f32[32,128,256]{2,0,1:T(8,128)S(1)} %copy.1526), channel_id=1, replica_groups=mesh['gx'=4,'gy'=4,'gz'=2] {'gz'}, dimensions={1} | all-to-all | bytes 8388608 | tf_op jit(solution)/shard_map/all_to_all | solution.py:150
  765.6 45.4 %all_to_all.207 = f32[64,64,256]{2,1,0:T(8,128)S(1)} all-to-all(f32[64,64,256]{2,1,0:T(8,128)S(1)} %copy.1529), channel_id=1, replica_groups=mesh['gx'=4,'gy'=4,'gz'=2] {'gz'}, dimensions={0} | all-to-all | bytes 8388608 | tf_op jit(solution)/shard_map/all_to_all | solution.py:152
  811.4 97.7 %all_to_all.208 = f32[32,128,256]{2,1,0:T(8,128)S(1)} all-to-all(f32[32,128,256]{2,1,0:T(8,128)S(1)} %bitcast.293), channel_id=1, replica_groups=mesh['gx'=4,'gy'=4,'gz'=2] {'gy'}, dimensions={0} | all-to-all | bytes 8388608 | tf_op jit(solution)/shard_map/all_to_all | solution.py:139
  909.7 30.8 %fusion.55 = f32[8,128,1024]{2,1,0:T(8,128)} fusion(f32[8,128,1024]{2,1,0:T(8,128)S(1)} %bitcast.298, s32[1024]{0:T(1024)S(1)} %get-tuple-element.163, s32[1024]{0:T(1024)S(1)} %get-tuple-element.164, f32[1024]{0:T(1024)S(1)} %fusion.143), kind=kOutput, calls=%fused_computation.128 | convolution fusion | flops 12900630528 | bytes 8400896 | tf_op jit(solution)/shard_map/kc,abc->abk/dot_general | solution.py:64
  945.9 97.7 %all_to_all.209 = f32[8,128,1024]{1,0,2:T(8,128)} all-to-all(f32[8,128,1024]{1,0,2:T(8,128)} %copy.1532), channel_id=1, replica_groups=mesh['gx'=4,'gy'=4,'gz'=2] {'gy'}, dimensions={2} | all-to-all | bytes 8388608 | tf_op jit(solution)/shard_map/all_to_all | solution.py:141
  1048.8 55.1 %all_to_all.210 = f32[32,128,256]{2,1,0:T(8,128)} all-to-all(f32[32,128,256]{2,1,0:T(8,128)} %bitcast.296), channel_id=1, replica_groups=mesh['gx'=4,'gy'=4,'gz'=2] {'gx'}, dimensions={0} | all-to-all | bytes 8388608 | tf_op jit(solution)/shard_map/all_to_all | solution.py:128
  1114.6 15.0 convolution_bitcast_fusion
  1141.1 15.2 copy.1574
  1183.4 14.1 slice.547
  1231.2 21.3 copy_dynamic-update-slice_fusion
  1289.6 15.6 multiply_subtract_fusion.3
  1338.9 24.0 %multiply_bitcast_fusion.2 = (f32[32,128,256]{1,2,0:T(8,128)}, f32[1,32,128,256]{2,3,1,0:T(8,128)S(1)}, f32[32,128,256]{1,2,0:T(8,128)}, f32[1,32,128,256]{2,3,1...) fusion(f32[32,1,256]{1,2,0:T(8,128)} %copy.1492, f32[32,127,256]{1,2,0:T(8,128)} %bitcast.279, ...), kind=kLoop, calls=%fused_computation.119 | loop fusion | flops 27262976 | bytes 71303168 | tf_op jit(solution)/shard_map/mul | solution.py:232
  1429.2 61.7 %multiply_subtract_fusion.1 = (f32[4,32,128,256]{3,1,2,0:T(8,128)}, f32[4,32,128,256]{3,1,2,0:T(8,128)}, f32[4,32,128,256]{3,1,2,0:T(8,128)}, f32[4,32,128,256]{3,1,2,0:T(8,128)}, f32[4,32,128,256]{3,1,2,0:T(8,128)}) fusion(f32[4,32,128,1]{3,1,2,0:T(8,128)} %copy.1557, f32[4,32,128,255]{3,1,2,0:T(8,128)} %slice.551, f32[32,128,256]{2,0,1:T(8,128)} %copy.1579, ...), kind=kLoop, calls=%fused_computation.63 | loop fusion | flops 75497472 | bytes 184549376 | tf_op jit(solution)/shard_map/sub | solution.py:232
  1490.9 12.2 slice.550
  1508.0 61.3 %copy_maximum_fusion.2 = (f32[4,32,128,256]{3,1,2,0:T(8,128)}, f32[4,32,128,256]{3,1,2,0:T(8,128)}, f32[4,32,128,256]{3,1,2,0:T(8,128)}) fusion(f32[4,32,128,256]{3,2,1,0:T(8,128)} %param.8, f32[4,32,128,256]{3,1,2,0:T(8,128)} %get-tuple-element.98, f32[4,31,128,256]{3,1,2,0:T(8,128)} %bitcast.273, f32[4,1,128,256]{3,1,2,0:T(1,128)S(1)} %get-tuple-element.39, ...), kind=kLoop, calls=%fused_computation.322 | loop fusion | flops 75497472 | bytes 180355072 | tf_op jit(solution)/shard_map/max | solution.py:246
  1569.3 25.6 %fusion.180 = (f32[4,32,128,255]{3,1,2,0:T(8,128)}, f32[4,32,128,255]{3,1,2,0:T(8,128)}) fusion(f32[4,32,128,256]{3,1,2,0:T(8,128)} %get-tuple-element.34), kind=kLoop, calls=%fused_computation.325 | loop fusion | bytes 66846720 | tf_op jit(solution)/shard_map/slice | solution.py:106
  1606.8 24.6 %fusion.179 = (f32[4,32,127,256]{3,1,2,0:T(8,128)}, f32[4,32,127,256]{3,1,2,0:T(8,128)}) fusion(f32[4,32,128,256]{3,1,2,0:T(8,128)} %get-tuple-element.34), kind=kLoop, calls=%fused_computation.324 | loop fusion | bytes 66584576 | tf_op jit(solution)/shard_map/slice | solution.py:106
  1642.9 16.1 copy_minimum_fusion.2
  1659.0 25.5 %fusion.185 = (f32[4,32,128,255]{3,1,2,0:T(8,128)}, f32[4,32,128,255]{3,1,2,0:T(8,128)}) fusion(f32[4,32,128,256]{3,1,2,0:T(8,128)} %copy_minimum_fusion.2), kind=kLoop, calls=%fused_computation.330 | loop fusion | bytes 66846720 | tf_op jit(solution)/shard_map/slice | solution.py:106
  1684.5 12.1 fusion.187
  1806.8 100.2 %divide_select_fusion.1 = f32[4,32,128,256]{3,1,2,0:T(8,128)} fusion(f32[4,32,128,256]{3,1,2,0:T(8,128)} %get-tuple-element.35, f32[4,31,128,256]{3,1,2,0:T(8,128)} %get-tuple-element.83, f32[4,1,128,256]{3,1,2,0:T(1,128)S(1)} %get-tuple-element.135, f32[4,1,128,256]{3,1,2,0:T(1,128)S(1)} %get-tuple-element.133, f32[4,31,128,256]{3,1,2,0:T(8,128)} %get-tuple-element.82, ...), kind=kLoop, calls=%fused_computation.61 | loop fusion | flops 138412032 | bytes 251658240 | tf_op jit(solution)/shard_map/jit(_where)/select_n | solution.py:69
  1907.0 96.3 %divide_select_fusion = f32[4,32,128,256]{3,1,2,0:T(8,128)} fusion(f32[4,32,128,256]{3,1,2,0:T(8,128)} %get-tuple-element.35, f32[4,31,128,256]{3,1,2,0:T(8,128)} %get-tuple-element.93, f32[4,1,128,256]{3,1,2,0:T(1,128)S(1)} %get-tuple-element.136, f32[4,1,128,256]{3,1,2,0:T(1,128)S(1)} %get-tuple-element.134, f32[4,31,128,256]{3,1,2,0:T(8,128)} %get-tuple-element.92, ...), kind=kLoop, calls=%fused_computation.60 | loop fusion | flops 138412032 | bytes 251658240 | tf_op jit(solution)/shard_map/jit(_where)/select_n | solution.py:69
  2004.5 22.7 pad_maximum_fusion
  2033.2 12.0 copy.1603
  2059.8 12.6 copy.1612
  2072.4 14.4 slice.594
  2086.9 14.3 slice.605
  2169.9 19.2 fusion.30
  2210.6 80.4 %fusion.28 = (f32[4,32,128,256]{3,1,2,0:T(8,128)}, f32[4,32,128,256]{3,1,2,0:T(8,128)}, f32[4,32,128,256]{3,1,2,0:T(8,128)}) fusion(f32[4,32,128,256]{3,1,2,0:T(8,128)} %get-tuple-element.97, f32[4,32,128,256]{3,1,2,0:T(8,128)} %divide_select_fusion, f32[4,1,128,256]{3,1,2,0:T(1,128)S(1)} %copy.1637, f32[4,31,128,256]{3,1,2,0:T(8,128)} %slice.605, ...), kind=kLoop, calls=%fused_computation.56 | loop fusion | flops 88080384 | bytes 234881024 | tf_op jit(solution)/shard_map/mul | solution.py:291
  2291.0 12.1 slice.593
  2309.1 46.4 %multiply_select_fusion = f32[4,32,128,256]{3,1,2,0:T(8,128)} fusion(f32[4,32,128,256]{3,1,2,0:T(8,128)} %get-tuple-element.35, f32[4,32,128,256]{3,1,2,0:T(8,128)} %get-tuple-element.61, f32[4,32,127,256]{3,1,2,0:T(8,128)} %slice.593, f32[4,32,1,256]{3,1,2,0:T(8,128)S(1)} %fusion.104, f32[4,32,128,256]{3,1,2,0:T(8,128)} %get-tuple-element.60, ...), kind=kLoop, calls=%fused_computation.5 | loop fusion | flops 50331648 | bytes 134742048 | tf_op jit(solution)/shard_map/jit(_where)/select_n | solution.py:308
  2355.5 17.7 copy.1613
  (354 shorter events, 690.9 us)
Async XLA Ops:
  62.5 67.1 %collective-permute-start.1 = (f32[4,32,1,256]{3,1,2,0:T(8,128)S(1)}, f32[4,32,1,256]{3,1,2,0:T(8,128)S(1)}, u32[]{:S(2)}, u32[]{:S(2)}) collective-permute-start(f32[4,32,1,256]{3,1,2,0:T(8,128)S(1)} %copy.1493), channel_id=1, source_target_pairs={{0,8},{8,16},{16,24},{1,9},{9,17},{17,25},{2,10},{10,18},{18,26},{... | collective-permute-start | bytes 393224 | tf_op jit(solution)/shard_map/ppermute | solution.py:23
  78.0 65.4 %collective-permute-start = (f32[4,32,1,256]{3,1,2,0:T(8,128)S(1)}, f32[4,32,1,256]{3,1,2,0:T(8,128)S(1)}, u32[]{:S(2)}, u32[]{:S(2)}) collective-permute-start(f32[4,32,1,256]{3,1,2,0:T(8,128)S(1)} %copy.1491), channel_id=1, source_target_pairs={{8,0},{16,8},{24,16},{9,1},{17,9},{25,17},{10,2},{18,10},{26,18},{... | collective-permute-start | bytes 393224 | tf_op jit(solution)/shard_map/ppermute | solution.py:26
  80.8 48.1 %collective-permute-start.2 = (f32[4,1,32,128]{3,2,0,1:T(8,128)S(1)}, f32[4,1,32,128]{3,2,0,1:T(8,128)S(1)}, u32[]{:S(2)}, u32[]{:S(2)}) collective-permute-start(f32[4,1,32,128]{3,2,0,1:T(8,128)S(1)} %get-tuple-element.100), channel_id=1, source_target_pairs={{2,0},{4,2},{6,4},{3,1},{5,3},{7,5},{10,8},{12,10},{14,12},{11,9},... | collective-permute-start | bytes 196616 | tf_op jit(solution)/shard_map/ppermute | solution.py:26
  82.1 46.8 %collective-permute-start.3 = (f32[4,1,32,128]{3,2,0,1:T(8,128)S(1)}, f32[4,1,32,128]{3,2,0,1:T(8,128)S(1)}, u32[]{:S(2)}, u32[]{:S(2)}) collective-permute-start(f32[4,1,32,128]{3,2,0,1:T(8,128)S(1)} %get-tuple-element.99), channel_id=1, source_target_pairs={{0,2},{2,4},{4,6},{1,3},{3,5},{5,7},{8,10},{10,12},{12,14},{9,11},... | collective-permute-start | bytes 196616 | tf_op jit(solution)/shard_map/ppermute | solution.py:23
  128.9 68.7 %copy-start.32 = (f32[1,1,32,128]{3,2,0,1:T(8,128)}, f32[1,1,32,128]{3,2,0,1:T(8,128)S(1)}, u32[]{:S(2)}) copy-start(f32[1,1,32,128]{3,2,0,1:T(8,128)S(1)} %slice.529) | copy-start | bytes 49156
  129.7 50.5 %copy-start.31 = (f32[4,32,1,256]{3,1,2,0:T(8,128)}, f32[4,32,1,256]{3,1,2,0:T(8,128)S(1)}, u32[]{:S(2)}) copy-start(f32[4,32,1,256]{3,1,2,0:T(8,128)S(1)} %collective-permute-done.1) | copy-start | bytes 393220
  172.6 24.7 %collective-permute-start.4 = (f32[4,1,130,256]{3,0,2,1:T(4,128)S(1)}, f32[4,1,130,256]{3,0,2,1:T(4,128)S(1)}, u32[]{:S(2)}, u32[]{:S(2)}) collective-permute-start(f32[4,1,130,256]{3,0,2,1:T(4,128)S(1)} %copy.1506), channel_id=1, source_target_pairs={{1,0},{3,2},{5,4},{7,6},{9,8},{11,10},{13,12},{15,14},{17,16},{19,... | collective-permute-start | bytes 1597448 | tf_op jit(solution)/shard_map/ppermute | solution.py:26
  178.9 39.8 %collective-permute-start.5 = (f32[4,1,130,256]{3,0,2,1:T(4,128)S(1)}, f32[4,1,130,256]{3,0,2,1:T(4,128)S(1)}, u32[]{:S(2)}, u32[]{:S(2)}) collective-permute-start(f32[4,1,130,256]{3,0,2,1:T(4,128)S(1)} %copy.1508), channel_id=1, source_target_pairs={{0,1},{2,3},{4,5},{6,7},{8,9},{10,11},{12,13},{14,15},{16,17},{18,... | collective-permute-start | bytes 1597448 | tf_op jit(solution)/shard_map/ppermute | solution.py:23
  233.7 50.4 %all-to-all-start = ((f32[32,128,256]{1,2,0:T(8,128)}), f32[32,128,256]{1,2,0:T(8,128)}, u32[]{:S(2)}, u32[]{:S(2)}) async-start(f32[32,128,256]{1,2,0:T(8,128)} %fusion.43), calls=%async_computation | async-start | bytes 8388608 | tf_op jit(solution)/shard_map/all_to_all | solution.py:128
  360.6 98.0 %all-to-all-start.2 = ((f32[32,128,256]{2,1,0:T(8,128)}), f32[32,128,256]{2,1,0:T(8,128)}, u32[]{:S(2)}, u32[]{:S(2)}) async-start(f32[32,128,256]{2,1,0:T(8,128)} %bitcast.284), calls=%async_computation.2 | async-start | bytes 8388608 | tf_op jit(solution)/shard_map/all_to_all | solution.py:139
  592.1 52.4 %all-to-all-start.4 = ((f32[32,128,256]{2,0,1:T(8,128)}), f32[32,128,256]{2,0,1:T(8,128)}, u32[]{:S(2)}, u32[]{:S(2)}) async-start(f32[32,128,256]{2,0,1:T(8,128)} %copy.1520), calls=%async_computation.4 | async-start | bytes 8388608 | tf_op jit(solution)/shard_map/all_to_all | solution.py:150
  655.4 50.3 %all-to-all-start.5 = ((f32[64,64,256]{2,1,0:T(8,128)}), f32[64,64,256]{2,1,0:T(8,128)}, u32[]{:S(2)}, u32[]{:S(2)}) async-start(f32[64,64,256]{2,1,0:T(8,128)} %copy.1524), calls=%async_computation.5 | async-start | bytes 8388608 | tf_op jit(solution)/shard_map/all_to_all | solution.py:152
  1135.0 87.4 %all-to-all-start.11 = ((f32[8,512,256]{2,0,1:T(8,128)}), f32[8,512,256]{2,0,1:T(8,128)}, u32[]{:S(2)}, u32[]{:S(2)}) async-start(f32[8,512,256]{2,0,1:T(8,128)} %copy.1536), calls=%async_computation.11 | async-start | bytes 8388608 | tf_op jit(solution)/shard_map/all_to_all | solution.py:130
  1162.4 59.2 %collective-permute-start.11 = (f32[4,32,1,256]{3,1,2,0:T(8,128)S(1)}, f32[4,32,1,256]{3,1,2,0:T(8,128)S(1)}, u32[]{:S(2)}, u32[]{:S(2)}) collective-permute-start(f32[4,32,1,256]{3,1,2,0:T(8,128)S(1)} %slice.549), channel_id=1, source_target_pairs={{0,8},{8,16},{16,24},{1,9},{9,17},{17,25},{2,10},{10,18},{18,26},{... | collective-permute-start | bytes 393224 | tf_op jit(solution)/shard_map/ppermute | solution.py:23
  1180.3 33.8 %collective-permute-start.14 = (f32[4,1,32,128]{3,2,0,1:T(8,128)S(1)}, f32[4,1,32,128]{3,2,0,1:T(8,128)S(1)}, u32[]{:S(2)}, u32[]{:S(2)}) collective-permute-start(f32[4,1,32,128]{3,2,0,1:T(8,128)S(1)} %bitcast.310), channel_id=1, source_target_pairs={{0,2},{2,4},{4,6},{1,3},{3,5},{5,7},{8,10},{10,12},{12,14},{9,11},... | collective-permute-start | bytes 196616 | tf_op jit(solution)/shard_map/ppermute | solution.py:23
  1221.6 59.7 %copy-start.27 = (f32[4,32,1,256]{3,1,2,0:T(8,128)}, f32[4,32,1,256]{3,1,2,0:T(8,128)S(1)}, u32[]{:S(2)}) copy-start(f32[4,32,1,256]{3,1,2,0:T(8,128)S(1)} %collective-permute-done.11) | copy-start | bytes 393220
  1228.7 23.8 %copy-start.4 = (f32[8,4,128,256]{2,3,0,1:T(8,128)S(1)}, f32[8,4,128,256]{2,3,0,1:T(8,128)}, u32[]{:S(2)}) copy-start(f32[8,4,128,256]{2,3,0,1:T(8,128)} %copy.1537) | copy-start | bytes 12582916
  1228.7 41.6 %collective-permute-start.13 = (f32[1,1,32,128]{3,2,1,0:T(8,128)S(1)}, f32[1,1,32,128]{3,2,1,0:T(8,128)S(1)}, u32[]{:S(2)}, u32[]{:S(2)}) collective-permute-start(f32[1,1,32,128]{3,2,1,0:T(8,128)S(1)} %bitcast.322), channel_id=1, source_target_pairs={{0,2},{2,4},{4,6},{1,3},{3,5},{5,7},{8,10},{10,12},{12,14},{9,11},... | collective-permute-start | bytes 49160 | tf_op jit(solution)/shard_map/ppermute | solution.py:23
  1266.4 5.0 collective-permute-start.8
  1269.0 69.9 %collective-permute-start.7 = (f32[1,1,32,128]{3,2,1,0:T(8,128)S(1)}, f32[1,1,32,128]{3,2,1,0:T(8,128)S(1)}, u32[]{:S(2)}, u32[]{:S(2)}) collective-permute-start(f32[1,1,32,128]{3,2,1,0:T(8,128)S(1)} %bitcast.319), channel_id=1, source_target_pairs={{2,0},{4,2},{6,4},{3,1},{5,3},{7,5},{10,8},{12,10},{14,12},{11,9},... | collective-permute-start | bytes 49160 | tf_op jit(solution)/shard_map/ppermute | solution.py:26
  1282.9 46.7 %collective-permute-start.10 = (f32[4,32,1,256]{3,1,2,0:T(8,128)S(1)}, f32[4,32,1,256]{3,1,2,0:T(8,128)S(1)}, u32[]{:S(2)}, u32[]{:S(2)}) collective-permute-start(f32[4,32,1,256]{3,1,2,0:T(8,128)S(1)} %get-tuple-element.85), channel_id=1, source_target_pairs={{8,0},{16,8},{24,16},{9,1},{17,9},{25,17},{10,2},{18,10},{26,18},{... | collective-permute-start | bytes 393224 | tf_op jit(solution)/shard_map/ppermute | solution.py:26
  1287.7 25.4 %collective-permute-start.6 = (f32[1,32,1,256]{3,1,2,0:T(8,128)S(1)}, f32[1,32,1,256]{3,1,2,0:T(8,128)S(1)}, u32[]{:S(2)}, u32[]{:S(2)}) collective-permute-start(f32[1,32,1,256]{3,1,2,0:T(8,128)S(1)} %copy.1538), channel_id=1, source_target_pairs={{8,0},{16,8},{24,16},{9,1},{17,9},{25,17},{10,2},{18,10},{26,18},{... | collective-permute-start | bytes 98312 | tf_op jit(solution)/shard_map/ppermute | solution.py:26
  1311.8 10.3 collective-permute-start.12
  1317.3 20.6 collective-permute-start.9
  1320.8 100.1 %collective-permute-start.16 = (f32[1,1,130,256]{2,3,1,0:T(8,128)S(1)}, f32[1,1,130,256]{2,3,1,0:T(8,128)}, u32[]{:S(2)}, u32[]{:S(2)}) collective-permute-start(f32[1,1,130,256]{2,3,1,0:T(8,128)S(1)} %get-tuple-element.103), channel_id=1, source_target_pairs={{0,1},{2,3},{4,5},{6,7},{8,9},{10,11},{12,13},{14,15},{16,17},{18,... | collective-permute-start | bytes 399368 | tf_op jit(solution)/shard_map/ppermute | solution.py:23
  1329.6 178.4 %copy-start.19 = (f32[4,32,1,256]{3,1,2,0:T(8,128)}, f32[4,32,1,256]{3,1,2,0:T(8,128)S(1)}, u32[]{:S(2)}) copy-start(f32[4,32,1,256]{3,1,2,0:T(8,128)S(1)} %collective-permute-done.10) | copy-start | bytes 393220
  1331.8 96.0 %collective-permute-start.15 = (f32[4,1,130,256]{3,0,2,1:T(4,128)S(1)}, f32[4,1,130,256]{3,0,2,1:T(4,128)S(1)}, u32[]{:S(2)}, u32[]{:S(2)}) collective-permute-start(f32[4,1,130,256]{3,0,2,1:T(4,128)S(1)} %get-tuple-element.71), channel_id=1, source_target_pairs={{1,0},{3,2},{5,4},{7,6},{9,8},{11,10},{13,12},{15,14},{17,16},{19,... | collective-permute-start | bytes 1597448 | tf_op jit(solution)/shard_map/ppermute | solution.py:26
  1336.5 166.6 %collective-permute-start.17 = (f32[4,1,130,256]{3,0,2,1:T(4,128)S(1)}, f32[4,1,130,256]{3,0,2,1:T(4,128)S(1)}, u32[]{:S(2)}, u32[]{:S(2)}) collective-permute-start(f32[4,1,130,256]{3,0,2,1:T(4,128)S(1)} %get-tuple-element.70), channel_id=1, source_target_pairs={{0,1},{2,3},{4,5},{6,7},{8,9},{10,11},{12,13},{14,15},{16,17},{18,... | collective-permute-start | bytes 1597448 | tf_op jit(solution)/shard_map/ppermute | solution.py:23
  1569.3 25.6 %copy-start = (f32[4,32,128,256]{3,1,2,0:T(8,128)S(1)}, f32[4,32,128,256]{3,1,2,0:T(8,128)}, u32[]{:S(2)}) copy-start(f32[4,32,128,256]{3,1,2,0:T(8,128)} %get-tuple-element.34) | copy-start | bytes 50331652
  1606.8 36.1 %slice-start.8 = ((s8[16777216]{0:T(1024)(128)(4,1)}), s8[4194304]{0:T(1024)(128)(4,1)S(1)}, s32[]{:S(2)}) async-start(s8[16777216]{0:T(1024)(128)(4,1)} %bitcast.246), calls=%async_computation.20 | async-start | bytes 8388608
  1606.8 36.1 %slice-start.9 = ((s8[16777216]{0:T(1024)(128)(4,1)}), s8[4194304]{0:T(1024)(128)(4,1)S(1)}, s32[]{:S(2)}) async-start(s8[16777216]{0:T(1024)(128)(4,1)} %bitcast.246), calls=%async_computation.21 | async-start | bytes 8388608
  1606.8 36.1 %slice-start.10 = ((s8[16777216]{0:T(1024)(128)(4,1)}), s8[4194304]{0:T(1024)(128)(4,1)S(1)}, s32[]{:S(2)}) async-start(s8[16777216]{0:T(1024)(128)(4,1)} %bitcast.246), calls=%async_computation.22 | async-start | bytes 8388608
  1659.0 25.5 %copy-start.1 = (f32[4,32,128,256]{3,1,2,0:T(8,128)S(1)}, f32[4,32,128,256]{3,1,2,0:T(8,128)}, u32[]{:S(2)}) copy-start(f32[4,32,128,256]{3,1,2,0:T(8,128)} %copy_minimum_fusion.2) | copy-start | bytes 50331652
  1715.0 32.7 %collective-permute-start.20 = (f32[4,1,32,128]{3,2,0,1:T(8,128)S(1)}, f32[4,1,32,128]{3,2,0,1:T(8,128)S(1)}, u32[]{:S(2)}, u32[]{:S(2)}) collective-permute-start(f32[4,1,32,128]{3,2,0,1:T(8,128)S(1)} %bitcast.308), channel_id=1, source_target_pairs={{2,0},{4,2},{6,4},{3,1},{5,3},{7,5},{10,8},{12,10},{14,12},{11,9},... | collective-permute-start | bytes 196616 | tf_op jit(solution)/shard_map/ppermute | solution.py:26
  1717.3 56.2 %collective-permute-start.18 = (f32[4,32,1,256]{3,1,2,0:T(8,128)S(1)}, f32[4,32,1,256]{3,1,2,0:T(8,128)S(1)}, u32[]{:S(2)}, u32[]{:S(2)}) collective-permute-start(f32[4,32,1,256]{3,1,2,0:T(8,128)S(1)} %get-tuple-element.95), channel_id=1, source_target_pairs={{8,0},{16,8},{24,16},{9,1},{17,9},{25,17},{10,2},{18,10},{26,18},{... | collective-permute-start | bytes 393224 | tf_op jit(solution)/shard_map/ppermute | solution.py:26
  1725.7 40.2 %collective-permute-start.21 = (f32[4,1,32,128]{3,2,0,1:T(8,128)S(1)}, f32[4,1,32,128]{3,2,0,1:T(8,128)S(1)}, u32[]{:S(2)}, u32[]{:S(2)}) collective-permute-start(f32[4,1,32,128]{3,2,0,1:T(8,128)S(1)} %bitcast.314), channel_id=1, source_target_pairs={{0,2},{2,4},{4,6},{1,3},{3,5},{5,7},{8,10},{10,12},{12,14},{9,11},... | collective-permute-start | bytes 196616 | tf_op jit(solution)/shard_map/ppermute | solution.py:23
  1731.0 42.4 %collective-permute-start.19 = (f32[4,32,1,256]{3,1,2,0:T(8,128)S(1)}, f32[4,32,1,256]{3,1,2,0:T(8,128)S(1)}, u32[]{:S(2)}, u32[]{:S(2)}) collective-permute-start(f32[4,32,1,256]{3,1,2,0:T(8,128)S(1)} %get-tuple-element.94), channel_id=1, source_target_pairs={{0,8},{8,16},{16,24},{1,9},{9,17},{17,25},{2,10},{10,18},{18,26},{... | collective-permute-start | bytes 393224 | tf_op jit(solution)/shard_map/ppermute | solution.py:23
  1777.8 28.0 %copy-start.13 = (f32[4,1,128,256]{3,0,2,1:T(4,128)S(1)}, f32[4,1,128,256]{3,0,2,1:T(4,128)}, u32[]{:S(2)}) copy-start(f32[4,1,128,256]{3,0,2,1:T(4,128)} %copy-done.12) | copy-start | bytes 1572868
  1777.8 15.6 collective-permute-start.22
  1791.7 14.0 collective-permute-start.23
  2027.2 133.2 %collective-permute-start.24 = (f32[8,32,1,256]{3,1,2,0:T(8,128)S(1)}, f32[8,32,1,256]{3,1,2,0:T(8,128)S(1)}, u32[]{:S(2)}, u32[]{:S(2)}) collective-permute-start(f32[8,32,1,256]{3,1,2,0:T(8,128)S(1)} %get-tuple-element.65), channel_id=1, source_target_pairs={{8,0},{16,8},{24,16},{9,1},{17,9},{25,17},{10,2},{18,10},{26,18},{... | collective-permute-start | bytes 786440 | tf_op jit(solution)/shard_map/ppermute | solution.py:26
  2029.1 131.2 %collective-permute-start.25 = (f32[8,32,1,256]{3,1,2,0:T(8,128)S(1)}, f32[8,32,1,256]{3,1,2,0:T(8,128)S(1)}, u32[]{:S(2)}, u32[]{:S(2)}) collective-permute-start(f32[8,32,1,256]{3,1,2,0:T(8,128)S(1)} %get-tuple-element.64), channel_id=1, source_target_pairs={{0,8},{8,16},{16,24},{1,9},{9,17},{17,25},{2,10},{10,18},{18,26},{... | collective-permute-start | bytes 786440 | tf_op jit(solution)/shard_map/ppermute | solution.py:23
  2045.2 100.1 %collective-permute-start.27 = (f32[8,1,32,128]{3,2,0,1:T(8,128)S(1)}, f32[8,1,32,128]{3,2,0,1:T(8,128)S(1)}, u32[]{:S(2)}, u32[]{:S(2)}) collective-permute-start(f32[8,1,32,128]{3,2,0,1:T(8,128)S(1)} %bitcast.307), channel_id=1, source_target_pairs={{0,2},{2,4},{4,6},{1,3},{3,5},{5,7},{8,10},{10,12},{12,14},{9,11},... | collective-permute-start | bytes 393224 | tf_op jit(solution)/shard_map/ppermute | solution.py:23
  2072.4 28.8 %slice-start.4 = ((s8[16777216]{0:T(1024)(128)(4,1)}), s8[4194304]{0:T(1024)(128)(4,1)S(1)}, s32[]{:S(2)}) async-start(s8[16777216]{0:T(1024)(128)(4,1)} %bitcast.244), calls=%async_computation.16 | async-start | bytes 8388608
  2072.4 28.8 %slice-start.5 = ((s8[16777216]{0:T(1024)(128)(4,1)}), s8[4194304]{0:T(1024)(128)(4,1)S(1)}, s32[]{:S(2)}) async-start(s8[16777216]{0:T(1024)(128)(4,1)} %bitcast.244), calls=%async_computation.17 | async-start | bytes 8388608
  2144.0 45.0 %collective-permute-start.26 = (f32[8,1,32,128]{3,2,0,1:T(8,128)S(1)}, f32[8,1,32,128]{3,2,0,1:T(8,128)S(1)}, u32[]{:S(2)}, u32[]{:S(2)}) collective-permute-start(f32[8,1,32,128]{3,2,0,1:T(8,128)S(1)} %bitcast.306), channel_id=1, source_target_pairs={{2,0},{4,2},{6,4},{3,1},{5,3},{7,5},{10,8},{12,10},{14,12},{11,9},... | collective-permute-start | bytes 393224 | tf_op jit(solution)/shard_map/ppermute | solution.py:26
  2167.5 40.3 %collective-permute-start.28 = (f32[8,1,130,256]{3,0,2,1:T(8,128)S(1)}, f32[8,1,130,256]{3,0,2,1:T(8,128)}, u32[]{:S(2)}, u32[]{:S(2)}) collective-permute-start(f32[8,1,130,256]{3,0,2,1:T(8,128)S(1)} %copy.1606), channel_id=1, source_target_pairs={{1,0},{3,2},{5,4},{7,6},{9,8},{11,10},{13,12},{15,14},{17,16},{19,... | collective-permute-start | bytes 3194888 | tf_op jit(solution)/shard_map/ppermute | solution.py:26
  2204.1 98.9 %collective-permute-start.29 = (f32[8,1,130,256]{3,0,2,1:T(8,128)S(1)}, f32[8,1,130,256]{3,0,2,1:T(8,128)}, u32[]{:S(2)}, u32[]{:S(2)}) collective-permute-start(f32[8,1,130,256]{3,0,2,1:T(8,128)S(1)} %copy.1609), channel_id=1, source_target_pairs={{0,1},{2,3},{4,5},{6,7},{8,9},{10,11},{12,13},{14,15},{16,17},{18,... | collective-permute-start | bytes 3194888 | tf_op jit(solution)/shard_map/ppermute | solution.py:23
  (46 other events, 565.5 us)
where the time goes:
time: 2390 us; the launch traced here: 2370 us
  local copies, waits for them, and re-layouts  734 us (31%)
  other arithmetic  733 us (31%)
  blocking collectives  493 us (21%)
  waiting for transfers between devices  220 us (9%)
  starting transfers between devices  108 us (5%)
  matrix products  83 us (3%)
    slice x21, local copies, waits for them, and re-layouts, after_cell(): lax.slice_in_dim(values, 1, extent, axis=direction)  207 us
    select_n x2, other arithmetic, limiter_ratio(): return jnp.where(binding, supply / jnp.where(binding, demand, 1.0), 1.0)  196 us
    all_to_all x2, blocking collectives, along_y(): return lax.all_to_all(pencil, 'gy', split_axis=2, concat_axis=0, tiled=True)  196 us
    unnamed x139, local copies, waits for them, and re-layouts  141 us
    all_to_all x1, blocking collectives, along_y(): lax.all_to_all(grid_field, 'gy', split_axis=0, concat_axis=2, tiled=True)  97.7 us
    mul x1, other arithmetic, body(): jnp.where(anti_flux >= 0.0, jnp.minimum(next_up, ratio_down), jnp.minimum...  80.4 us
    all_to_all x1, waiting for transfers between devices, along_y(): lax.all_to_all(grid_field, 'gy', split_axis=0, concat_axis=2, tiled=True)  75.6 us
    slice x8, local copies, waits for them, and re-layouts, y_edges(): return jnp.stack([values[:, :, :, 0], values[:, :, :, -1]], axis=1)  65.1 us
  transfers between devices with their start and end apart: 35, of which 5 were waited for; matrix products, arithmetic and copies ran while one was open for 32% of the time, Pallas kernels for 0%

commit v1 on v0

v1 whole, which is shorter than its diff:
```python
import functools
import math

import jax
import jax.numpy as jnp
import ml_dtypes
import numpy as np
from jax import lax
from jax.experimental import pallas as pl
from jax.experimental.pallas import tpu as pltpu
from jax.sharding import PartitionSpec as P

TIME_STEP = 0.2
ANISOTROPY = 4.0
GAINS = (0.5, 0.5, 0.5 * ANISOTROPY)
DEPOSIT = (
    (0.0, 0.25, 0.75, 1.5),
    (0.0, 0.5, 1.0, 2.0),
    (0.1, 0.4, 0.8, 1.6),
    (0.0, 0.15, 1.25, 2.5),
)
W = 3
RX = 8
LANES = 128
F32 = jnp.float32
BF16 = jnp.bfloat16
VMEM_LIMIT = 60 * 1024 * 1024


def params():
    return pltpu.CompilerParams(
        dimension_semantics=("arbitrary",), vmem_limit_bytes=VMEM_LIMIT
    )


def sine_half(extent):
    k = np.arange(extent)[:, None]
    n = np.arange(extent)[None, :]
    weight = np.where(k == extent - 1, math.sqrt(1.0 / extent), math.sqrt(2.0 / extent))
    return weight * np.sin(np.pi * ((k + 1) * (2 * n + 1) % (4 * extent)) / (2 * extent))


def cosine_half(extent):
    k = np.arange(extent)[:, None]
    n = np.arange(extent)[None, :]
    weight = np.where(k == 0, math.sqrt(1.0 / extent), math.sqrt(2.0 / extent))
    return weight * np.cos(np.pi * (k * (2 * n + 1) % (4 * extent)) / (2 * extent))


def sine_whole(extent):
    k = np.arange(extent)[:, None] + 1
    n = np.arange(extent)[None, :] + 1
    return math.sqrt(2.0 / (extent + 1)) * np.sin(np.pi * (k * n % (2 * extent + 2)) / (extent + 1))


def split_table(table):
    table = np.asarray(table, np.float32)
    high = table.astype(ml_dtypes.bfloat16)
    low = (table - high.astype(np.float32)).astype(ml_dtypes.bfloat16)
    return jnp.asarray(high), jnp.asarray(low)


def split_value(value):
    high = value.astype(BF16)
    return high, (value - high.astype(F32)).astype(BF16)


def mm(left, right):
    return jnp.dot(left, right, preferred_element_type=F32)


def table_left(high, low, value):
    v_high, v_low = split_value(value)
    return mm(high[...], v_high) + (mm(high[...], v_low) + mm(low[...], v_high))


def table_right(value, high, low):
    v_high, v_low = split_value(value)
    return mm(v_high, high[...]) + (mm(v_low, high[...]) + mm(v_high, low[...]))


def full(left, right):
    return jnp.dot(
        left, right, precision=lax.Precision.HIGHEST, preferred_element_type=F32
    )


def lines_kernel(x_ref, *refs):
    tables, o_ref = refs[:-1], refs[-1]
    count, _, rows, lanes = x_ref.shape
    value = x_ref[...].reshape(count * rows, lanes)
    if len(tables) == 2:
        result = table_left(*tables, value)
    else:
        result = full(tables[0][...], value)
    o_ref[...] = result.reshape(o_ref.shape)


def x_lines(blocks, tables, pieces):
    count, layers, rows, lanes = blocks.shape
    total = count * rows
    return pl.pallas_call(
        lines_kernel,
        grid=(layers,),
        in_specs=[
            pl.BlockSpec((count, 1, rows, lanes), lambda i: (0, i, 0, 0)),
        ]
        + [pl.BlockSpec((total, total), lambda i: (0, 0)) for _ in tables],
        out_specs=pl.BlockSpec((pieces, 1, total // pieces, lanes), lambda i: (0, i, 0, 0)),
        out_shape=jax.ShapeDtypeStruct((pieces, layers, total // pieces, lanes), F32),
        compiler_params=params(),
    )(blocks, *tables)


def forward_kernel(x_ref, s_high, s_low, k_high, k_low, lam_ref, ey_ref, ends_ref, b_ref, fl_ref):
    total_z, rows, lanes = x_ref.shape
    value = x_ref[...].reshape(total_z * rows, lanes)
    spectrum = table_left(k_high, k_low, table_right(value, s_high, s_low))
    b_ref[...] = spectrum.reshape(b_ref.shape)
    local = spectrum / (lam_ref[0] + ey_ref[...])
    fl_ref[0] = lax.dot_general(
        ends_ref[...],
        local,
        (((1,), (1,)), ((), ())),
        precision=lax.Precision.HIGHEST,
        preferred_element_type=F32,
    )


def backward_kernel(b_ref, ab_ref, s_ref, k_ref, lam_ref, ey_ref, ends_ref, u_ref):
    total_z, rows, lanes = b_ref.shape
    spectrum = b_ref[...].reshape(total_z * rows, lanes)
    ends = lax.dot_general(
        ab_ref[0],
        ends_ref[...],
        (((0,), (0,)), ((), ())),
        precision=lax.Precision.HIGHEST,
        preferred_element_type=F32,
    )
    solved = (spectrum + ends) / (lam_ref[0] + ey_ref[...])
    u_ref[...] = full(k_ref[...], full(solved, s_ref[...])).reshape(u_ref.shape)


def solve(source, scalars, scalar_z):
    local_z, local_x, local_y = source.shape
    nx, ny, nz = lax.axis_size("gx"), lax.axis_size("gy"), lax.axis_size("gz")
    total_x, total_z = local_x * nx, local_z * nz
    group = nx * nz
    layers = local_z // nx
    part_x = total_x // group
    tiles = part_x // 8
    pair_rows = total_z * 8
    chunk = lax.axis_index("gz") * nx + lax.axis_index("gx")

    e_x = 4.0 * np.sin(np.pi * (np.arange(total_x) + 1) / (2 * total_x)) ** 2
    e_z = 4.0 * np.sin(np.pi * np.arange(total_z) / (2 * total_z)) ** 2
    lam = ANISOTROPY * e_z[:, None] + e_x[None, :]
    lam = lam.reshape(total_z, group, tiles, 8).transpose(1, 2, 0, 3).reshape(group, tiles, pair_rows)
    theta = np.log1p(lam / 2 + np.sqrt(lam + lam * lam / 4))
    whole = np.expm1(-2 * (local_y + 1) * theta)
    alpha = np.exp(-theta) * np.expm1(-2 * local_y * theta) / whole
    beta = np.exp(-local_y * theta) * np.expm1(-2 * theta) / whole
    response = [alpha - beta * beta / (1 + alpha)]
    inverse = [1 / (1 + alpha)]
    for _ in range(1, ny):
        inverse.append(1 / (1 - alpha * response[-1]))
        response.append(alpha + beta * beta * response[-1] * inverse[-1])
    closing = 1 / (1 + response[-1])

    def mine(table):
        return lax.dynamic_index_in_dim(jnp.asarray(table, F32), chunk, 0, keepdims=False)

    basis = sine_whole(local_y)
    e_y = 4.0 * np.sin(np.pi * (np.arange(local_y) + 1) / (2 * (local_y + 1))) ** 2
    ends = np.zeros((8, local_y))
    ends[0], ends[1] = basis[:, 0], basis[:, -1]
    ends = jnp.asarray(ends, F32)
    ey = jnp.asarray(e_y[None, :], F32)
    lam_rows = mine(lam)[:, :, None]
    s_high, s_low = split_table(basis)
    cosine = np.kron(cosine_half(total_z), np.eye(8))
    forward_z = split_table(2.0 * cosine)
    backward_z = jnp.asarray(cosine.T, F32)

    together = lax.optimization_barrier
    source, scalar_z = together((source, scalar_z))
    blocks = source.reshape(nx, layers, local_x, local_y)
    scalar_x = x_halo((scalars,), *scalar_z)
    blocks = lax.all_to_all(blocks, "gx", 0, 0)
    blocks, scalar_x = together((blocks, scalar_x))
    sine_x = sine_half(total_x)
    blocks = x_lines(blocks, split_table(sine_x), group)
    scalar_pack = y_pack((scalars,), *scalar_z, *scalar_x)
    blocks = lax.all_to_all(blocks, ("gz", "gx"), 0, 0)
    blocks, scalar_pack = together((blocks, scalar_pack))
    scalar_y = shift_pair(*scalar_pack, "gy")
    columns = blocks.reshape(total_z, part_x, local_y)

    cube = pl.BlockSpec((total_z, 8, local_y), lambda i: (0, i, 0))
    small = pl.BlockSpec((1, 8, pair_rows), lambda i: (i, 0, 0))
    tables = [
        pl.BlockSpec((local_y, local_y), lambda i: (0, 0)),
        pl.BlockSpec((local_y, local_y), lambda i: (0, 0)),
        pl.BlockSpec((pair_rows, pair_rows), lambda i: (0, 0)),
        pl.BlockSpec((pair_rows, pair_rows), lambda i: (0, 0)),
        pl.BlockSpec((1, pair_rows, 1), lambda i: (i, 0, 0)),
        pl.BlockSpec((1, local_y), lambda i: (0, 0)),
        pl.BlockSpec((8, local_y), lambda i: (0, 0)),
    ]
    spectrum, edge = pl.pallas_call(
        forward_kernel,
        grid=(tiles,),
        in_specs=[cube] + tables,
        out_specs=[cube, small],
        out_shape=[
            jax.ShapeDtypeStruct(columns.shape, F32),
            jax.ShapeDtypeStruct((tiles, 8, pair_rows), F32),
        ],
        compiler_params=params(),
    )(columns, s_high, s_low, *forward_z, lam_rows, ey, ends)

    every = lax.all_gather(edge[:, :2], "gy")
    al, be = mine(alpha), mine(beta)
    re = [mine(r) for r in response]
    inv = [mine(r) for r in inverse]
    first_in = [every[p, :, 0] for p in range(ny)]
    last_in = [every[p, :, 1] for p in range(ny)]
    carried = [last_in[0] - be * first_in[0] * inv[0]]
    for p in range(1, ny):
        prior = carried[-1]
        carried.append(
            last_in[p] + be * (prior + re[p - 1] * (first_in[p] + al * prior) * inv[p])
        )
    first, last = [None] * ny, [None] * ny
    last[ny - 1] = carried[ny - 1] * mine(closing)
    above = -last[ny - 1]
    for p in range(ny - 1, -1, -1):
        if p < ny - 1:
            last[p] = carried[p] + re[p] * above
        if p > 0:
            first[p] = (first_in[p] + al * carried[p - 1] + be * above) * inv[p]
        else:
            first[p] = (first_in[p] + be * above) * inv[p]
        above = first[p]
    below = jnp.stack([-first[0]] + last[:-1])
    above = jnp.stack(first[1:] + [-last[-1]])
    place = lax.axis_index("gy")
    below = lax.dynamic_index_in_dim(below, place, 0, keepdims=False)
    above = lax.dynamic_index_in_dim(above, place, 0, keepdims=False)
    sides = jnp.stack([below, above] + [jnp.zeros_like(below)] * 6, 1)

    columns = pl.pallas_call(
        backward_kernel,
        grid=(tiles,),
        in_specs=[cube, small, tables[0], tables[2]] + tables[4:],
        out_specs=cube,
        out_shape=jax.ShapeDtypeStruct(columns.shape, F32),
        compiler_params=params(),
    )(spectrum, sides, jnp.asarray(basis, F32), backward_z, lam_rows, ey, ends)

    blocks = columns.reshape(group, layers, part_x, local_y)
    blocks = lax.all_to_all(blocks, ("gz", "gx"), 0, 0)
    blocks, scalar_y = together((blocks, scalar_y))
    blocks = x_lines(blocks, (jnp.asarray(sine_x.T, F32),), nx)
    blocks = lax.all_to_all(blocks, "gx", 0, 0)
    return blocks.reshape(local_z, local_x, local_y), scalar_z + scalar_x + scalar_y


def shift_pair(low_part, high_part, axis):
    count = lax.axis_size(axis)
    up = [(i, i + 1) for i in range(count - 1)]
    down = [(target, source) for source, target in up]
    return lax.ppermute(high_part, axis, up), lax.ppermute(low_part, axis, down)


def pack_kernel(groups, span, *refs):
    count = len(groups)
    firsts, finals = refs[:count], refs[count : 2 * count]
    zlf, zll, zhf, zhl, xlf, xll, xhf, xhl, lo_ref, hi_ref = refs[2 * count :]
    step = pl.program_id(0)
    depth = pl.num_programs(0) * span
    rows = firsts[0].shape[2]
    lane = lax.broadcasted_iota(jnp.int32, (1, LANES), 1)

    def packed(k, first, final, old):
        keep = (lane >= W * k) & (lane < W * k + W)
        low = jnp.where(keep, pltpu.roll(first, lax.rem(W * k, LANES), 1), old[0])
        high = jnp.where(keep, pltpu.roll(final, lax.rem(W * k + W, LANES), 1), old[1])
        return low, high

    inner = slice(RX, RX + rows)

    @pl.when(step == 0)
    def _():
        for field in range(sum(groups)):
            for begin, first, final in ((0, xlf, xll), (RX + rows, xhf, xhl)):
                old = (jnp.zeros((RX, LANES), F32),) * 2
                for k in range(first.shape[1]):
                    old = packed(jnp.int32(k), first[field, k], final[field, k], old)
                lo_ref[field, begin : begin + RX, :] = old[0]
                hi_ref[field, begin : begin + RX, :] = old[1]
            old = (jnp.zeros((rows, LANES), F32),) * 2
            for k in range(W):
                old = packed(jnp.int32(k), zlf[field, k], zll[field, k], old)
                old = packed(W + depth + k, zhf[field, k], zhl[field, k], old)
            lo_ref[field, inner, :] = old[0]
            hi_ref[field, inner, :] = old[1]

    field = 0
    for at, size in enumerate(groups):
        for index in range(size):
            old = (lo_ref[field, inner, :], hi_ref[field, inner, :])
            for j in range(span):
                old = packed(
                    W + step * span + j, firsts[at][index, j], finals[at][index, j], old
                )
            lo_ref[field, inner, :] = old[0]
            hi_ref[field, inner, :] = old[1]
            field += 1


def joined(arrays, pick):
    parts = [pick(a) for a in arrays]
    return parts[0] if len(parts) == 1 else jnp.concatenate(parts, 0)


def z_halo(arrays, after=None):
    local_z = arrays[0].shape[1]
    first = joined(arrays, lambda a: a[:, :W])
    final = joined(arrays, lambda a: a[:, local_z - W :])
    if after is not None:
        first, final, _ = lax.optimization_barrier((first, final, after))
    return shift_pair(first, final, "gz")


def x_halo(arrays, z_low, z_high):
    local_x = arrays[0].shape[2]

    def rows(begin):
        cut = lambda a: a[:, :, begin : begin + RX]
        return jnp.concatenate([cut(z_low), joined(arrays, cut), cut(z_high)], 1)

    return shift_pair(rows(0), rows(local_x - RX), "gx")


def y_pack(arrays, z_low, z_high, x_low, x_high):
    local_z, local_x, local_y = arrays[0].shape[1:]
    groups = tuple(a.shape[0] for a in arrays)
    fields = sum(groups)
    final = local_y // LANES - 1
    span = 8

    def edge(shape, at):
        return pl.BlockSpec(shape[:3] + (LANES,), lambda k: (0, 0, 0, at))

    def part(size, at):
        return pl.BlockSpec((size, span, local_x, LANES), lambda k: (0, k, 0, at))

    specs = [part(g, 0) for g in groups] + [part(g, final) for g in groups]
    operands = list(arrays) * 2
    for array in (z_low, z_high, x_low, x_high):
        specs += [edge(array.shape, 0), edge(array.shape, final)]
        operands += [array, array]
    shape = (fields, local_x + 2 * RX, LANES)
    return pl.pallas_call(
        functools.partial(pack_kernel, groups, span),
        grid=(local_z // span,),
        in_specs=specs,
        out_specs=[pl.BlockSpec(shape, lambda k: (0, 0, 0))] * 2,
        out_shape=[jax.ShapeDtypeStruct(shape, F32)] * 2,
        compiler_params=params(),
    )(*operands)


def halos(arrays):
    z_part = z_halo(arrays)
    x_part = x_halo(arrays, *z_part)
    return z_part + x_part + shift_pair(*y_pack(arrays, *z_part, *x_part), "gy")


def halo_specs(fields, local_z, local_x, local_y, plane_of):
    return [
        pl.BlockSpec(
            (fields, 1, local_x, local_y), lambda k: (0, jnp.minimum(plane_of(k), W - 1), 0, 0)
        ),
        pl.BlockSpec(
            (fields, 1, local_x, local_y),
            lambda k: (0, jnp.maximum(plane_of(k) - W - local_z, 0), 0, 0),
        ),
        pl.BlockSpec((fields, 1, RX, local_y), lambda k: (0, plane_of(k), 0, 0)),
        pl.BlockSpec((fields, 1, RX, local_y), lambda k: (0, plane_of(k), 0, 0)),
        pl.BlockSpec((fields, local_x + 2 * RX, LANES), lambda k: (0, 0, 0)),
        pl.BlockSpec((fields, local_x + 2 * RX, LANES), lambda k: (0, 0, 0)),
    ]


def assemble(k, local_z, mains, halo, put):
    z_low, z_high, x_low, x_high, y_low, y_high = halo
    local_x, local_y = z_low.shape[2:]
    every = slice(0, local_x + 2 * RX)
    inner = slice(RX, RX + local_x)
    wide = slice(0, local_y)
    lane = lax.broadcasted_iota(jnp.int32, (1, LANES), 1)
    up = lax.rem(2 * LANES - W * k, LANES)
    down = lax.rem(2 * LANES - W * k - W, LANES)
    field = 0
    for main in mains:
        for index in range(main.shape[0]):

            @pl.when((k >= W) & (k < W + local_z))
            def _():
                put(field, inner, wide, main[index, 0])

            @pl.when(k < W)
            def _():
                put(field, inner, wide, z_low[field, 0])

            @pl.when(k >= W + local_z)
            def _():
                put(field, inner, wide, z_high[field, 0])

            put(field, slice(0, RX), wide, x_low[field, 0])
            put(field, slice(RX + local_x, 2 * RX + local_x), wide, x_high[field, 0])
            put(
                field,
                every,
                slice(local_y, local_y + LANES),
                jnp.where(
                    lane < LANES // 2,
                    pltpu.roll(y_high[field], up, 1),
                    pltpu.roll(y_low[field], down, 1),
                ),
            )
            field += 1


def next_y(value):
    return pltpu.roll(value, value.shape[1] - 1, 1)


def prev_y(value):
    return pltpu.roll(value, 1, 1)


def next_x(value, after):
    row = lax.broadcasted_iota(jnp.int32, value.shape, 0)
    return pltpu.roll(jnp.where(row == 0, after, value), 7, 0)


def prev_x(value, before):
    row = lax.broadcasted_iota(jnp.int32, value.shape, 0)
    return pltpu.roll(jnp.where(row == 7, before, value), 1, 0)


def divergence_kernel(local_z, wind, opened, *refs):
    halo, out, cell, face_z = refs[:6], refs[6], refs[7], refs[8]
    k = pl.program_id(0) + W - 1
    local_x, local_y = out.shape[1:]
    lanes = local_y + LANES
    now, old = lax.rem(k, 2), lax.rem(k + 1, 2)

    def put(field, rows, wide, value):
        cell[now, field, rows, wide] = value

    assemble(k, local_z, (wind, opened), halo, put)
    count = local_x // 8 + 2
    before = jnp.zeros((8, lanes), F32)
    for i in range(count - 1):
        here, after = slice(8 * i, 8 * i + 8), slice(8 * i + 8, 8 * i + 16)
        open_cells = cell[old, 3, here, :]
        flux_x = cell[old, 0, here, :] * (open_cells * next_x(open_cells, cell[old, 3, after, :]))
        flux_y = cell[old, 1, here, :] * (open_cells * next_y(open_cells))
        flux_z = cell[old, 2, here, :] * (open_cells * cell[now, 3, here, :])
        if i > 0:
            total = (flux_x - prev_x(flux_x, before)) + (flux_y - prev_y(flux_y))
            total = total + (flux_z - face_z[here, :])
            out[0, 8 * i - 8 : 8 * i, :] = total[:, :local_y]
        face_z[here, :] = flux_z
        before = flux_x


def divergence(wind, opened, wind_halo):
    local_z, local_x, local_y = wind.shape[1:]
    plane_of = lambda k: k + W - 1
    middle = lambda k: (0, jnp.clip(plane_of(k) - W, 0, local_z - 1), 0, 0)
    lanes = local_y + LANES
    rows = local_x + 2 * RX
    return pl.pallas_call(
        functools.partial(divergence_kernel, local_z),
        grid=(local_z + 2,),
        in_specs=[
            pl.BlockSpec((3, 1, local_x, local_y), middle),
            pl.BlockSpec((1, 1, local_x, local_y), middle),
        ]
        + halo_specs(4, local_z, local_x, local_y, plane_of),
        out_specs=pl.BlockSpec(
            (1, local_x, local_y), lambda k: (jnp.clip(k - 2, 0, local_z - 1), 0, 0)
        ),
        out_shape=jax.ShapeDtypeStruct((local_z, local_x, local_y), F32),
        scratch_shapes=[pltpu.VMEM((2, 4, rows, lanes), F32), pltpu.VMEM((rows, lanes), F32)],
        compiler_params=params(),
    )(wind, opened, *wind_halo)


def limiter(demand, supply):
    binding = demand > supply
    return jnp.where(binding, supply / jnp.where(binding, demand, 1.0), 1.0)


def transport_kernel(local_z, scalar_count, *refs):
    scal, sc_halo = refs[0], refs[1:7]
    wind, opened, wi_halo = refs[7], refs[8], refs[9:15]
    mult, mu_halo = refs[15], refs[16:22]
    factor, wind_out, out = refs[22:25]
    speed, cell, kept = refs[25], refs[26], refs[27:]
    conc, trial, upper, lower, anti, ratio, low_z, lim_z, edge, result = (
        kept[at * scalar_count : (at + 1) * scalar_count] for at in range(10)
    )
    k = pl.program_id(0)
    local_x, local_y = out.shape[2:]
    lanes = local_y + LANES
    count = local_x // 8 + 2
    s0, s1, s2, s3 = (lax.rem(k + 4 - d, 4) for d in range(4))
    now, old = lax.rem(k, 2), lax.rem(k + 1, 2)

    def put_scalar(field, rows, wide, value):
        conc[field][s0, rows, wide] = value

    def put_wind(field, rows, wide, value):
        cell[now, field, rows, wide] = value

    def put_mult(field, rows, wide, value):
        cell[now, 4, rows, wide] = value

    assemble(k, local_z, (scal,), sc_halo, put_scalar)
    assemble(k, local_z, (wind, opened), wi_halo, put_wind)
    assemble(k, local_z, (mult,), mu_halo, put_mult)

    def chunk(i):
        return pl.ds(pl.multiple_of(i * 8, 8), 8)

    def column(i, _):
        here = chunk(i)
        after = chunk(jnp.minimum(i + 1, count - 1))
        before = chunk(jnp.maximum(i - 1, 0))

        cells, multiplier = cell[old, 3, here, :], cell[old, 4, here, :]
        neighbours = (
            (next_x(cells, cell[old, 3, after, :]), next_x(multiplier, cell[old, 4, after, :])),
            (next_y(cells), next_y(multiplier)),
            (cell[now, 3, here, :], cell[now, 4, here, :]),
        )
        speeds, halves, sizes = [], [], []
        for d in range(3):
            open_next, mult_next = neighbours[d]
            face = cells * open_next
            value = (cell[old, d, here, :] * face + GAINS[d] * (mult_next - multiplier)) * face
            speeds.append(value)
            halves.append((0.5 * TIME_STEP) * value)
            sizes.append(jnp.abs(halves[-1]))
        for d in range(3):
            speed[d, here, :] = speeds[d][:, :local_y]

        for s in range(scalar_count):
            c = conc[s][s1, here, :]
            downwind = (next_x(c, conc[s][s1, after, :]), next_y(c), conc[s][s0, here, :])
            antis, lows = [], []
            for d in range(3):
                a = sizes[d] * (downwind[d] - c)
                antis.append(a)
                lows.append(halves[d] * (downwind[d] + c) - a)
            change = (lows[0] - prev_x(lows[0], edge[s][0])) + (lows[1] - prev_y(lows[1]))
            t_new = c - (change + (lows[2] - low_z[s][here, :]))
            u_new, l_new = jnp.maximum(c, t_new), jnp.minimum(c, t_new)

            u, l = upper[s][s2, here, :], lower[s][s2, here, :]
            ceiling = jnp.maximum(
                jnp.maximum(u, u_new),
                jnp.maximum(
                    next_x(u, upper[s][s2, after, :]), prev_x(u, upper[s][s2, before, :])
                ),
            )
            ceiling = jnp.maximum(
                jnp.maximum(ceiling, upper[s][s3, here, :]), jnp.maximum(next_y(u), prev_y(u))
            )
            bottom = jnp.minimum(
                jnp.minimum(l, l_new),
                jnp.minimum(
                    next_x(l, lower[s][s2, after, :]), prev_x(l, lower[s][s2, before, :])
                ),
            )
            bottom = jnp.minimum(
                jnp.minimum(bottom, lower[s][s3, here, :]), jnp.minimum(next_y(l), prev_y(l))
            )
            a_x, a_y, a_z = (anti[s][s2, d, here, :] for d in range(3))
            befores = (
                prev_x(a_x, anti[s][s2, 0, before, :]),
                prev_y(a_y),
                anti[s][s3, 2, here, :],
            )
            inflow, outflow = 0.0, 0.0
            for a, b in zip((a_x, a_y, a_z), befores):
                inflow = inflow + (jnp.maximum(b, 0.0) - jnp.minimum(a, 0.0))
                outflow = outflow + (jnp.maximum(a, 0.0) - jnp.minimum(b, 0.0))
            t_mid = trial[s][s2, here, :]
            up_new = limiter(inflow, ceiling - t_mid)
            down_new = limiter(outflow, t_mid - bottom)

            r_up, r_down = ratio[s][old, 0, here, :], ratio[s][old, 1, here, :]
            nexts = (
                (
                    next_x(r_up, ratio[s][old, 0, after, :]),
                    next_x(r_down, ratio[s][old, 1, after, :]),
                ),
                (next_y(r_up), next_y(r_down)),
                (up_new, down_new),
            )
            limited = []
            for d in range(3):
                a = anti[s][s3, d, here, :]
                share = jnp.where(
                    a >= 0.0, jnp.minimum(nexts[d][0], r_down), jnp.minimum(r_up, nexts[d][1])
                )
                limited.append(share * a)
            moved = limited[0] - prev_x(limited[0], edge[s][1])
            moved = moved + (limited[1] - prev_y(limited[1])) + (limited[2] - lim_z[s][here, :])
            final = trial[s][s3, here, :] - moved

            result[s][here, :] = final[:, :local_y]
            lim_z[s][here, :] = limited[2]
            edge[s][1] = limited[0]
            ratio[s][now, 0, here, :] = up_new
            ratio[s][now, 1, here, :] = down_new
            trial[s][s1, here, :] = t_new
            upper[s][s1, here, :] = u_new
            lower[s][s1, here, :] = l_new
            low_z[s][here, :] = lows[2]
            edge[s][0] = lows[0]
            for d in range(3):
                anti[s][s1, d, here, :] = antis[d]
        return 0

    lax.fori_loop(0, count, column, 0)
    inner = slice(RX, RX + local_x)

    @pl.when((k > W) & (k <= W + local_z))
    def _():
        for d in range(3):
            wind_out[d, 0] = speed[d, inner, :]

    @pl.when(k > 2 * W)
    def _():
        for s in range(scalar_count):
            out[s, 0] = result[s][inner, :]

    @pl.when(k == 2 * W)
    def _():
        for s in range(scalar_count):
            out[s, 0] = result[s][inner, :] * factor[s]


def transport(scalars, sc_halo, wind, opened, wi_halo, mult, mu_halo, factor):
    n, local_z, local_x, local_y = scalars.shape
    same = lambda k: k
    middle = lambda k: (0, jnp.clip(k - W, 0, local_z - 1), 0, 0)
    lanes = local_y + LANES
    rows = local_x + 2 * RX
    plane = (rows, lanes)

    def main(count):
        return [pl.BlockSpec((count, 1, local_x, local_y), middle)]

    def halo(count):
        return halo_specs(count, local_z, local_x, local_y, same)

    return pl.pallas_call(
        functools.partial(transport_kernel, local_z, n),
        grid=(local_z + 2 * W,),
        in_specs=main(n)
        + halo(n)
        + main(3)
        + main(1)
        + halo(4)
        + main(1)
        + halo(1)
        + [pl.BlockSpec((n, local_x, local_y), lambda k: (0, 0, 0))],
        out_specs=[
            pl.BlockSpec(
                (3, 1, local_x, local_y), lambda k: (0, jnp.clip(k - 1 - W, 0, local_z - 1), 0, 0)
            ),
            pl.BlockSpec(
                (n, 1, local_x, local_y), lambda k: (0, jnp.clip(k - 2 * W, 0, local_z - 1), 0, 0)
            ),
        ],
        out_shape=[
            jax.ShapeDtypeStruct((3, local_z, local_x, local_y), F32),
            jax.ShapeDtypeStruct(scalars.shape, F32),
        ],
        scratch_shapes=[pltpu.VMEM((3, rows, local_y), F32), pltpu.VMEM((2, 5) + plane, F32)]
        + [
            pltpu.VMEM(shape, F32)
            for shape in (
                (4,) + plane,
                (4,) + plane,
                (4,) + plane,
                (4,) + plane,
                (4, 3) + plane,
                (2, 2) + plane,
                plane,
                plane,
                (2, 8, lanes),
                (rows, local_y),
            )
            for _ in range(n)
        ],
        compiler_params=params(),
    )(scalars, *sc_halo, wind, opened, *wi_halo, mult, *mu_halo, factor)


def ground_factor(surface_flags):
    rates = 1.0 - TIME_STEP * np.asarray(DEPOSIT, np.float32)
    factor = jnp.zeros((len(DEPOSIT),) + surface_flags.shape, F32)
    for surface in range(4):
        column = jnp.asarray(rates[:, surface], F32)[:, None, None]
        factor = factor + jnp.where(surface_flags[None] == surface, column, 0.0)
    return jnp.where(lax.axis_index("gz") == 0, factor, 1.0)


def body(initial_wind, building_mask, surface_flags, scalars):
    opened = (1.0 - building_mask.astype(F32))[None]
    wind_z = z_halo((initial_wind, opened))
    scalar_z = z_halo((scalars,), wind_z)
    wind_x = x_halo((initial_wind, opened), *wind_z)
    wind_y = shift_pair(*y_pack((initial_wind, opened), *wind_z, *wind_x), "gy")
    wind_halo = wind_z + wind_x + wind_y
    source = divergence(initial_wind, opened, wind_halo)
    multiplier, scalar_halo = solve(source, scalars, scalar_z)
    multiplier = multiplier[None]
    mult_halo = halos((multiplier,))
    corrected, transported = transport(
        scalars,
        scalar_halo,
        initial_wind,
        opened,
        wind_halo,
        multiplier,
        mult_halo,
        ground_factor(surface_flags),
    )
    return (corrected, transported)


def solution(mesh):
    in_specs = (
        P(None, "gz", "gx", "gy"),
        P("gz", "gx", "gy"),
        P("gx", "gy"),
        P(None, "gz", "gx", "gy"),
    )
    out_specs = (P(None, "gz", "gx", "gy"), P(None, "gz", "gx", "gy"))
    return jax.shard_map(body, mesh=mesh, in_specs=in_specs, out_specs=out_specs, check_vma=False)
```

time: 2390 us -> 753 us (0.32)
  other arithmetic: 733 us -> 6.05 us
  local copies, waits for them, and re-layouts: 734 us -> 19.3 us
  blocking collectives: 493 us -> 64.8 us
  Pallas kernels: 0 us -> 402 us
  matrix products: 83 us -> 0 us
  starting transfers between devices: 108 us -> 64.2 us
  waiting for transfers between devices: 220 us -> 193 us
    all_to_all x7 -> x1, blocking collectives: 493 us -> 53.6 us  [solve(): blocks = lax.all_to_all(blocks, 'gx', 0, 0)]
    pallas_call x0 -> x9, Pallas kernels: none -> 402 us  [the longest x1 272 us: transport(): pl.pallas_call(functools.partial(transport_kernel, local_z, n), grid=(loc...]
    slice x64 -> x14, local copies, waits for them, and re-layouts: 383 us -> 11.3 us  [the longest x9 4.33 us: rows(): cut = lambda a: a[:, :, begin:begin + RX]]
    select_n x6 -> x1, other arithmetic: 243 us -> 1.02 us  [ground_factor(): return jnp.where(lax.axis_index('gz') == 0, factor, 1.0)]
    mul x21 -> x0, other arithmetic: 185 us -> none  [the longest x1 80.4 us: body(): jnp.where(anti_flux >= 0.0, jnp.minimum(next_up, ratio_down), jnp.minimum...]
    all_to_all x5 -> x3, waiting for transfers between devices: 208 us -> 64.6 us  [the longest x2 64.6 us: solve(): blocks = lax.all_to_all(blocks, ('gz', 'gx'), 0, 0)]
    unnamed x139 -> x52, local copies, waits for them, and re-layouts: 141 us -> 5.13 us
    ppermute x30 -> x18, waiting for transfers between devices: 11.2 us -> 128 us  [the longest x9 93.2 us: shift_pair(): lax.ppermute(high_part, axis, up)]
  transfers between devices with their start and end apart: 35 -> 21, of which waited for: 5 -> 17; matrix products, arithmetic and copies ran while one was open for 32% -> 2% of each run, Pallas kernels for 0% -> 8%
where the time goes in v1:
time: 753 us; the launch traced here: 750 us
  Pallas kernels  402 us (53%)
  waiting for transfers between devices  193 us (26%)
  blocking collectives  64.8 us (9%)
  starting transfers between devices  64.2 us (9%)
  local copies, waits for them, and re-layouts  19.3 us (3%)
    pallas_call x1, Pallas kernels, transport(): pl.pallas_call(functools.partial(transport_kernel, local_z, n), grid=(loc...  272 us
    ppermute x9, waiting for transfers between devices, shift_pair(): lax.ppermute(high_part, axis, up)  93.2 us
    all_to_all x2, waiting for transfers between devices, solve(): blocks = lax.all_to_all(blocks, ('gz', 'gx'), 0, 0)  64.6 us
    all_to_all x1, blocking collectives, solve(): blocks = lax.all_to_all(blocks, 'gx', 0, 0)  53.6 us
    ppermute x9, waiting for transfers between devices, shift_pair(): lax.ppermute(low_part, axis, down)  35.2 us
    pallas_call x1, Pallas kernels, divergence(): pl.pallas_call(functools.partial(divergence_kernel, local_z), grid=(local...  32.4 us
    pallas_call x3, Pallas kernels, y_pack(): pl.pallas_call(functools.partial(pack_kernel, groups, span), grid=(local_...  29.6 us
    pallas_call x1, Pallas kernels, solve(): pl.pallas_call(backward_kernel, grid=(tiles,), in_specs=[cube, small, tab...  28.8 us
  transfers between devices with their start and end apart: 21, of which 17 were waited for; matrix products, arithmetic and copies ran while one was open for 2% of the time, Pallas kernels for 8%

profile of v1, /device:TPU:5, one launch (start us, length us, event | category | flops | bytes accessed | tf_op | source)
XLA Modules:
  0.0 750.3 jit_solution(11992462213144116007)
XLA Ops:
  0.6 2.0 fusion.35
  5.7 4.2 collective-permute-start.1
  10.0 1.6 fusion.34
  11.5 3.9 fusion.33
  15.4 26.0 %collective-permute-done.refs_4_.refs_5_.refs_0_.refs_9_ = f32[4,3,128,256]{3,2,1,0:T(8,128)S(1)} collective-permute-done((f32[4,3,128,256]{3,2,1,0:T(8,128)S(1)}, f32[4,3,128,256]{3,2,1,0:T(8,128)S(1)}, u32[]{:S(2)}, u32[]{:S(2)}) %collective-permute-start) | collective-permute-done | bytes 1572896 | tf_op jit(solution)/shard_map/ppermute | solution.py:273
  43.7 4.9 collective-permute-start.2
  49.9 5.4 collective-permute-start.7
  55.3 1.9 collective-permute-start.3
  57.3 5.1 collective-permute-done.2.refs_8_.refs_9_.refs_2_.refs_11_
  62.4 11.5 %collective-permute-done.3.refs_10_.refs_11_.refs_3_.refs_12_ = f32[4,38,8,256]{3,2,1,0:T(8,128)S(1)} collective-permute-done((f32[4,38,8,256]{3,2,1,0:T(8,128)S(1)}, f32[4,38,8,256]{3,2,1,0:T(8,128)S(1)}, u32[]{:S(2)}, u32[]{:S(2)}) %collective-permute-start.3) | collective-permute-done | bytes 1245216 | tf_op jit(solution)/shard_map/ppermute | solution.py:273
  74.9 12.2 %shard_map.293 = (f32[4,144,128]{2,1,0:T(8,128)}, f32[4,144,128]{2,1,0:T(8,128)}) custom-call(f32[3,32,128,256]{3,2,1,0:T(8,128)} %refs_7_.1, f32[1,32,128,256]{3,2,1,0:T(8,128)} %copy-done, f32[3,32,128,256]{3,2,1,0:T(8,128)} %refs_7_.1, f32[1,32,128,256]{3,2,1,0:T(8,128)} %copy-done, f32[4,3,128,256]{3,2,1,0:T(8,128)} %copy-done.2, ...), custom_call_target="tpu_custom_call" | custom-call | tf_op jit(solution)/shard_map/pallas_call | solution.py:365
  87.1 3.2 collective-permute-start.4
  91.6 2.6 collective-permute-done.4.refs_4_.refs_13_
  94.3 3.7 collective-permute-done.5.refs_5_.refs_14_
  98.7 32.4 %shard_map.294 = f32[32,128,256]{2,1,0:T(8,128)} custom-call(f32[3,32,128,256]{3,2,1,0:T(8,128)} %refs_7_.1, f32[1,32,128,256]{3,2,1,0:T(8,128)} %copy-done, f32[4,3,128,256]{3,2,1,0:T(8,128)} %copy-done.2, f32[4,3,128,256]{3,2,1,0:T(8,128)} %copy-done.3, f32[4,38,8,256]{3,2,1,0:T(8,128)} %collective-permute-done.2.refs_8_.refs_9_.refs_2_.refs_11_, ...), custom_call_target="tpu_custom_call" | custom-call | tf_op jit(solution)/shard_map/pallas_call | solution.py:488
  131.1 4.9 all-to-all-start
  136.0 1.7 fusion.32
  138.8 2.9 collective-permute-start.8
  141.8 1.9 collective-permute-start.9
  143.8 49.2 %collective-permute-done.8.refs_6_.refs_7_.refs_3_ = f32[4,38,8,256]{3,2,1,0:T(8,128)S(1)} collective-permute-done((f32[4,38,8,256]{3,2,1,0:T(8,128)S(1)}, f32[4,38,8,256]{3,2,1,0:T(8,128)S(1)}, u32[]{:S(2)}, u32[]{:S(2)}) %collective-permute-start.8) | collective-permute-done | bytes 1245216 | tf_op jit(solution)/shard_map/ppermute | solution.py:273
  193.0 1.6 collective-permute-done.9.refs_8_.refs_9_.refs_4_
  194.6 9.4 %shard_map.295 = f32[8,8,64,256]{3,2,1,0:T(8,128)} custom-call(f32[4,8,128,256]{3,2,1,0:T(8,128)} %all-to-all-done.x_ref, bf16[512,512]{1,0:T(8,128)(2,1)} %constant.120.clone.refs_0_, bf16[512,512]{1,0:T(8,128)(2,1)} %constant.121.clone.refs_1_), custom_call_target="tpu_custom_call" | custom-call | tf_op jit(solution)/shard_map/pallas_call | solution.py:102
  204.0 4.6 all-to-all-start.1
  209.5 2.0 copy.50.lam_ref
  211.4 12.3 %shard_map.296 = (f32[4,144,128]{2,1,0:T(8,128)}, f32[4,144,128]{2,1,0:T(8,128)}) custom-call(f32[4,32,128,256]{3,2,1,0:T(8,128)} %refs_0_.7, f32[4,32,128,256]{3,2,1,0:T(8,128)} %refs_0_.7, f32[4,3,128,256]{3,2,1,0:T(8,128)} %copy-done.5, f32[4,3,128,256]{3,2,1,0:T(8,128)} %copy-done.5, f32[4,3,128,256]{3,2,1,0:T(8,128)} %collective-permute-done.7.refs_4_.refs_5_.refs_2_, ...), custom_call_target="tpu_custom_call" | custom-call | tf_op jit(solution)/shard_map/pallas_call | solution.py:365
  223.8 30.5 %all-to-all-done.1 = f32[8,8,64,256]{3,2,1,0:T(8,128)} async-done(((f32[8,8,64,256]{3,2,1,0:T(8,128)}), f32[8,8,64,256]{3,2,1,0:T(8,128)}, u32[]{:S(2)}, u32[]{:S(2)}) %all-to-all-start.1) | async-done | bytes 4194336 | tf_op jit(solution)/shard_map/all_to_all | solution.py:194
  254.3 18.4 %shard_map.297 = (f32[64,64,256]{2,1,0:T(8,128)}, f32[8,8,512]{2,1,0:T(8,128)}) custom-call(f32[64,64,256]{2,1,0:T(8,128)} %bitcast.2.x_ref, bf16[256,256]{1,0:T(8,128)(2,1)} %constant.115.clone.s_high, bf16[256,256]{1,0:T(8,128)(2,1)} %constant.116.clone.s_low, bf16[512,512]{1,0:T(8,128)(2,1)} %constant.117.clone.k_high, ...), custom_call_target="tpu_custom_call" | custom-call | tf_op jit(solution)/shard_map/pallas_call | solution.py:210
  273.6 11.2 %all-gather = f32[32,2,512]{2,1,0:T(2,128)S(1)} all-gather(f32[8,2,512]{2,1,0:T(2,128)S(1)} %slice.131), channel_id=2, replica_groups=mesh['gx'=4,'gy'=4,'gz'=2] {'gy'}, dimensions={0}, use_global_device_ids=true | all-gather | bytes 163840 | tf_op jit(solution)/shard_map/all_gather | solution.py:222
  284.8 1.7 fusion.4
  288.6 28.8 %shard_map.298 = f32[64,64,256]{2,1,0:T(8,128)} custom-call(f32[64,64,256]{2,1,0:T(8,128)} %get-tuple-element.37.b_ref, f32[8,8,512]{2,1,0:T(8,128)} %maximum_maximum_fusion.ab_ref, f32[256,256]{1,0:T(8,128)} %constant.132.clone.s_ref, f32[512,512]{1,0:T(8,128)} %constant.119.clone.k_ref, f32[8,512,1]{2,1,0:T(8,128)} %copy.50.lam_ref, ...), custom_call_target="tpu_custom_call" | custom-call | tf_op jit(solution)/shard_map/pallas_call | solution.py:252
  317.4 10.2 %all-to-all-start.2 = ((f32[8,8,64,256]{3,2,1,0:T(8,128)}), f32[8,8,64,256]{3,2,1,0:T(8,128)}, u32[]{:S(2)}, u32[]{:S(2)}) async-start(f32[8,8,64,256]{3,2,1,0:T(8,128)} %bitcast.96), calls=%async_computation.2 | async-start | bytes 8388608 | tf_op jit(solution)/shard_map/all_to_all | solution.py:262
  327.5 1.4 collective-permute-start.10
  330.2 4.7 collective-permute-done.10.refs_5_
  334.9 3.9 collective-permute-done.11.refs_6_
  338.9 34.1 %all-to-all-done.2.x_ref = f32[8,8,64,256]{3,2,1,0:T(8,128)} async-done(((f32[8,8,64,256]{3,2,1,0:T(8,128)}), f32[8,8,64,256]{3,2,1,0:T(8,128)}, u32[]{:S(2)}, u32[]{:S(2)}) %all-to-all-start.2) | async-done | bytes 4194336 | tf_op jit(solution)/shard_map/all_to_all | solution.py:262
  372.9 11.4 %shard_map.299 = f32[4,8,128,256]{3,2,1,0:T(8,128)} custom-call(f32[8,8,64,256]{3,2,1,0:T(8,128)} %all-to-all-done.2.x_ref, f32[512,512]{1,0:T(8,128)} %constant.133.clone.refs_0_), custom_call_target="tpu_custom_call" | custom-call | tf_op jit(solution)/shard_map/pallas_call | solution.py:102
  384.4 53.6 %all_to_all.20 = f32[4,8,128,256]{3,2,1,0:T(8,128)S(1)} all-to-all(f32[4,8,128,256]{3,2,1,0:T(8,128)} %shard_map.299), channel_id=1, replica_groups=mesh['gx'=4,'gy'=4,'gz'=2] {'gx'}, dimensions={0} | all-to-all | bytes 8388608 | tf_op jit(solution)/shard_map/all_to_all | solution.py:265
  438.1 3.3 collective-permute-start.13
  442.7 6.0 collective-permute-done.13.refs_4_.refs_5_.refs_17_
  448.7 3.8 collective-permute-done.12.refs_2_.refs_3_.refs_16_
  452.6 4.5 collective-permute-start.14
  457.2 1.9 collective-permute-start.15
  459.2 1.7 collective-permute-done.14.refs_6_.refs_7_.refs_18_
  460.9 4.4 collective-permute-done.15.refs_8_.refs_9_.refs_19_
  466.1 5.1 shard_map.300
  471.2 1.4 collective-permute-start.16
  475.0 2.9 collective-permute-done.17.refs_21_
  478.5 271.6 %shard_map.301 = (f32[3,32,128,256]{3,2,1,0:T(8,128)}, f32[4,32,128,256]{3,2,1,0:T(8,128)}) custom-call(f32[4,32,128,256]{3,2,1,0:T(8,128)} %refs_0_.7, f32[4,3,128,256]{3,2,1,0:T(8,128)} %copy-done.5, f32[4,3,128,256]{3,2,1,0:T(8,128)} %collective-permute-done.7.refs_4_.refs_5_.refs_2_, f32[4,38,8,256]{3,2,1,0:T(8,128)} %copy-done.6, ...), custom_call_target="tpu_custom_call" | custom-call | tf_op jit(solution)/shard_map/pallas_call | solution.py:676
  (92 shorter events, 21.4 us)
Async XLA Ops:
  0.6 2.9 copy-start.8
  4.1 5.8 copy-start
  4.3 37.2 %collective-permute-start = (f32[4,3,128,256]{3,2,1,0:T(8,128)S(1)}, f32[4,3,128,256]{3,2,1,0:T(8,128)S(1)}, u32[]{:S(2)}, u32[]{:S(2)}) collective-permute-start(f32[4,3,128,256]{3,2,1,0:T(8,128)S(1)} %pad_maximum_fusion), channel_id=1, source_target_pairs={{0,1},{2,3},{4,5},{6,7},{8,9},{10,11},{12,13},{14,15},{16,17},{18,... | collective-permute-start | bytes 4718600 | tf_op jit(solution)/shard_map/ppermute | solution.py:273
  5.7 36.8 %collective-permute-start.1 = (f32[4,3,128,256]{3,2,1,0:T(8,128)S(1)}, f32[4,3,128,256]{3,2,1,0:T(8,128)S(1)}, u32[]{:S(2)}, u32[]{:S(2)}) collective-permute-start(f32[4,3,128,256]{3,2,1,0:T(8,128)S(1)} %pad_maximum_fusion.1), channel_id=1, source_target_pairs={{1,0},{3,2},{5,4},{7,6},{9,8},{11,10},{13,12},{15,14},{17,16},{19,... | collective-permute-start | bytes 4718600 | tf_op jit(solution)/shard_map/ppermute | solution.py:273
  41.4 1.2 copy-start.2
  42.5 1.2 copy-start.3
  43.7 18.7 %collective-permute-start.2 = (f32[4,38,8,256]{3,2,1,0:T(8,128)S(1)}, f32[4,38,8,256]{3,2,1,0:T(8,128)}, u32[]{:S(2)}, u32[]{:S(2)}) collective-permute-start(f32[4,38,8,256]{3,2,1,0:T(8,128)S(1)} %pad_maximum_fusion.2), channel_id=1, source_target_pairs={{0,8},{8,16},{16,24},{1,9},{9,17},{17,25},{2,10},{10,18},{18,26},{... | collective-permute-start | bytes 3735560 | tf_op jit(solution)/shard_map/ppermute | solution.py:273
  48.6 82.6 %collective-permute-start.6 = (f32[4,3,128,256]{3,2,1,0:T(8,128)}, f32[4,3,128,256]{3,2,1,0:T(8,128)S(1)}, u32[]{:S(2)}, u32[]{:S(2)}) collective-permute-start(f32[4,3,128,256]{3,2,1,0:T(8,128)} %get-tuple-element.26), channel_id=1, source_target_pairs={{0,1},{2,3},{4,5},{6,7},{8,9},{10,11},{12,13},{14,15},{16,17},{18,... | collective-permute-start | bytes 4718600 | tf_op jit(solution)/shard_map/ppermute | solution.py:273
  49.9 81.3 %collective-permute-start.7 = (f32[4,3,128,256]{3,2,1,0:T(8,128)}, f32[4,3,128,256]{3,2,1,0:T(8,128)}, u32[]{:S(2)}, u32[]{:S(2)}) collective-permute-start(f32[4,3,128,256]{3,2,1,0:T(8,128)} %get-tuple-element.27), channel_id=1, source_target_pairs={{1,0},{3,2},{5,4},{7,6},{9,8},{11,10},{13,12},{15,14},{17,16},{19,... | collective-permute-start | bytes 4718600 | tf_op jit(solution)/shard_map/ppermute | solution.py:273
  55.3 18.5 %collective-permute-start.3 = (f32[4,38,8,256]{3,2,1,0:T(8,128)S(1)}, f32[4,38,8,256]{3,2,1,0:T(8,128)S(1)}, u32[]{:S(2)}, u32[]{:S(2)}) collective-permute-start(f32[4,38,8,256]{3,2,1,0:T(8,128)S(1)} %pad_maximum_fusion.3), channel_id=1, source_target_pairs={{8,0},{16,8},{24,16},{9,1},{17,9},{25,17},{10,2},{18,10},{26,18},{... | collective-permute-start | bytes 3735560 | tf_op jit(solution)/shard_map/ppermute | solution.py:273
  73.9 1.1 copy-start.4
  87.1 7.2 collective-permute-start.4
  90.3 7.7 %collective-permute-start.5 = (f32[4,144,128]{2,1,0:T(8,128)}, f32[4,144,128]{2,1,0:T(8,128)S(1)}, u32[]{:S(2)}, u32[]{:S(2)}) collective-permute-start(f32[4,144,128]{2,1,0:T(8,128)} %get-tuple-element.25), channel_id=1, source_target_pairs={{2,0},{4,2},{6,4},{3,1},{5,3},{7,5},{10,8},{12,10},{14,12},{11,9},... | collective-permute-start | bytes 884744 | tf_op jit(solution)/shard_map/ppermute | solution.py:273
  94.3 3.7 copy-start.13
  98.0 0.7 copy-start.14
  131.1 6.6 copy-start.5
  131.1 63.5 %all-to-all-start = ((f32[4,8,128,256]{3,2,1,0:T(8,128)}), f32[4,8,128,256]{3,2,1,0:T(8,128)}, u32[]{:S(2)}, u32[]{:S(2)}) async-start(f32[4,8,128,256]{3,2,1,0:T(8,128)} %bitcast.95), calls=%async_computation | async-start | bytes 8388608 | tf_op jit(solution)/shard_map/all_to_all | solution.py:189
  138.8 54.2 %collective-permute-start.8 = (f32[4,38,8,256]{3,2,1,0:T(8,128)S(1)}, f32[4,38,8,256]{3,2,1,0:T(8,128)S(1)}, u32[]{:S(2)}, u32[]{:S(2)}) collective-permute-start(f32[4,38,8,256]{3,2,1,0:T(8,128)S(1)} %pad_maximum_fusion.4), channel_id=1, source_target_pairs={{0,8},{8,16},{16,24},{1,9},{9,17},{17,25},{2,10},{10,18},{18,26},{... | collective-permute-start | bytes 3735560 | tf_op jit(solution)/shard_map/ppermute | solution.py:273
  141.8 52.8 %collective-permute-start.9 = (f32[4,38,8,256]{3,2,1,0:T(8,128)S(1)}, f32[4,38,8,256]{3,2,1,0:T(8,128)S(1)}, u32[]{:S(2)}, u32[]{:S(2)}) collective-permute-start(f32[4,38,8,256]{3,2,1,0:T(8,128)S(1)} %pad_maximum_fusion.5), channel_id=1, source_target_pairs={{8,0},{16,8},{24,16},{9,1},{17,9},{25,17},{10,2},{18,10},{26,18},{... | collective-permute-start | bytes 3735560 | tf_op jit(solution)/shard_map/ppermute | solution.py:273
  193.0 11.0 %copy-start.6 = (f32[4,38,8,256]{3,2,1,0:T(8,128)}, f32[4,38,8,256]{3,2,1,0:T(8,128)S(1)}, u32[]{:S(2)}) copy-start(f32[4,38,8,256]{3,2,1,0:T(8,128)S(1)} %collective-permute-done.8.refs_6_.refs_7_.refs_3_) | copy-start | bytes 3735556
  194.6 9.4 %copy-start.7 = (f32[4,38,8,256]{3,2,1,0:T(8,128)}, f32[4,38,8,256]{3,2,1,0:T(8,128)S(1)}, u32[]{:S(2)}) copy-start(f32[4,38,8,256]{3,2,1,0:T(8,128)S(1)} %collective-permute-done.9.refs_8_.refs_9_.refs_4_) | copy-start | bytes 3735556
  204.0 50.3 %all-to-all-start.1 = ((f32[8,8,64,256]{3,2,1,0:T(8,128)}), f32[8,8,64,256]{3,2,1,0:T(8,128)}, u32[]{:S(2)}, u32[]{:S(2)}) async-start(f32[8,8,64,256]{3,2,1,0:T(8,128)} %shard_map.295), calls=%async_computation.1 | async-start | bytes 8388608 | tf_op jit(solution)/shard_map/all_to_all | solution.py:194
  317.4 10.2 %copy-start.25 = (f32[4,144,128]{2,1,0:T(8,128)S(1)}, f32[4,144,128]{2,1,0:T(8,128)}, u32[]{:S(2)}) copy-start(f32[4,144,128]{2,1,0:T(8,128)} %get-tuple-element.39) | copy-start | bytes 884740
  317.4 11.6 %copy-start.24 = (f32[4,144,128]{2,1,0:T(8,128)S(1)}, f32[4,144,128]{2,1,0:T(8,128)}, u32[]{:S(2)}) copy-start(f32[4,144,128]{2,1,0:T(8,128)} %get-tuple-element.40) | copy-start | bytes 884740
  317.4 55.6 %all-to-all-start.2 = ((f32[8,8,64,256]{3,2,1,0:T(8,128)}), f32[8,8,64,256]{3,2,1,0:T(8,128)}, u32[]{:S(2)}, u32[]{:S(2)}) async-start(f32[8,8,64,256]{3,2,1,0:T(8,128)} %bitcast.96), calls=%async_computation.2 | async-start | bytes 8388608 | tf_op jit(solution)/shard_map/all_to_all | solution.py:262
  327.5 7.4 collective-permute-start.10
  328.9 9.9 %collective-permute-start.11 = (f32[4,144,128]{2,1,0:T(8,128)S(1)}, f32[4,144,128]{2,1,0:T(8,128)S(1)}, u32[]{:S(2)}, u32[]{:S(2)}) collective-permute-start(f32[4,144,128]{2,1,0:T(8,128)S(1)} %copy-done.24), channel_id=1, source_target_pairs={{2,0},{4,2},{6,4},{3,1},{5,3},{7,5},{10,8},{12,10},{14,12},{11,9},... | collective-permute-start | bytes 884744 | tf_op jit(solution)/shard_map/ppermute | solution.py:273
  334.9 49.4 %copy-start.15 = (f32[4,144,128]{2,1,0:T(8,128)}, f32[4,144,128]{2,1,0:T(8,128)S(1)}, u32[]{:S(2)}) copy-start(f32[4,144,128]{2,1,0:T(8,128)S(1)} %collective-permute-done.10.refs_5_) | copy-start | bytes 884740
  338.9 45.5 %copy-start.16 = (f32[4,144,128]{2,1,0:T(8,128)}, f32[4,144,128]{2,1,0:T(8,128)S(1)}, u32[]{:S(2)}) copy-start(f32[4,144,128]{2,1,0:T(8,128)S(1)} %collective-permute-done.11.refs_6_) | copy-start | bytes 884740
  438.0 4.7 copy-start.1
  438.1 21.0 %copy-start.17 = (s32[128,256]{1,0:T(8,128)S(1)}, s32[128,256]{1,0:T(8,128)}, u32[]{:S(2)}) copy-start(s32[128,256]{1,0:T(8,128)} %param.32) | copy-start | bytes 393220
  438.1 10.6 %collective-permute-start.13 = (f32[1,3,128,256]{3,2,1,0:T(8,128)S(1)}, f32[1,3,128,256]{3,2,1,0:T(8,128)S(1)}, u32[]{:S(2)}, u32[]{:S(2)}) collective-permute-start(f32[1,3,128,256]{3,2,1,0:T(8,128)S(1)} %get-tuple-element.64), channel_id=1, source_target_pairs={{1,0},{3,2},{5,4},{7,6},{9,8},{11,10},{13,12},{15,14},{17,16},{19,... | collective-permute-start | bytes 1179656 | tf_op jit(solution)/shard_map/ppermute | solution.py:273
  441.4 11.2 %collective-permute-start.12 = (f32[1,3,128,256]{3,2,1,0:T(8,128)S(1)}, f32[1,3,128,256]{3,2,1,0:T(8,128)S(1)}, u32[]{:S(2)}, u32[]{:S(2)}) collective-permute-start(f32[1,3,128,256]{3,2,1,0:T(8,128)S(1)} %get-tuple-element.65), channel_id=1, source_target_pairs={{0,1},{2,3},{4,5},{6,7},{8,9},{10,11},{12,13},{14,15},{16,17},{18,... | collective-permute-start | bytes 1179656 | tf_op jit(solution)/shard_map/ppermute | solution.py:273
  448.7 16.7 %copy-start.9 = (f32[1,3,128,256]{3,2,1,0:T(8,128)}, f32[1,3,128,256]{3,2,1,0:T(8,128)S(1)}, u32[]{:S(2)}) copy-start(f32[1,3,128,256]{3,2,1,0:T(8,128)S(1)} %collective-permute-done.13.refs_4_.refs_5_.refs_17_) | copy-start | bytes 1179652
  452.5 12.8 %copy-start.10 = (f32[1,3,128,256]{3,2,1,0:T(8,128)}, f32[1,3,128,256]{3,2,1,0:T(8,128)S(1)}, u32[]{:S(2)}) copy-start(f32[1,3,128,256]{3,2,1,0:T(8,128)S(1)} %collective-permute-done.12.refs_2_.refs_3_.refs_16_) | copy-start | bytes 1179652
  452.6 8.4 %collective-permute-start.14 = (f32[1,38,8,256]{3,2,1,0:T(8,128)S(1)}, f32[1,38,8,256]{3,2,1,0:T(8,128)S(1)}, u32[]{:S(2)}, u32[]{:S(2)}) collective-permute-start(f32[1,38,8,256]{3,2,1,0:T(8,128)S(1)} %pad_maximum_fusion.6), channel_id=1, source_target_pairs={{0,8},{8,16},{16,24},{1,9},{9,17},{17,25},{2,10},{10,18},{18,26},{... | collective-permute-start | bytes 933896 | tf_op jit(solution)/shard_map/ppermute | solution.py:273
  457.2 8.2 %collective-permute-start.15 = (f32[1,38,8,256]{3,2,1,0:T(8,128)S(1)}, f32[1,38,8,256]{3,2,1,0:T(8,128)S(1)}, u32[]{:S(2)}, u32[]{:S(2)}) collective-permute-start(f32[1,38,8,256]{3,2,1,0:T(8,128)S(1)} %pad_maximum_fusion.7), channel_id=1, source_target_pairs={{8,0},{16,8},{24,16},{9,1},{17,9},{25,17},{10,2},{18,10},{26,18},{... | collective-permute-start | bytes 933896 | tf_op jit(solution)/shard_map/ppermute | solution.py:273
  459.2 14.7 %copy-start.20 = (f32[4]{0:T(128)S(1)}, f32[4]{0:T(128)}, u32[]{:S(2)}) copy-start(f32[4]{0:T(128)} %constant.137.clone) | copy-start | bytes 52
  459.2 14.7 %copy-start.21 = (f32[4]{0:T(128)S(1)}, f32[4]{0:T(128)}, u32[]{:S(2)}) copy-start(f32[4]{0:T(128)} %constant.136.clone) | copy-start | bytes 52
  459.2 14.7 %copy-start.22 = (f32[4]{0:T(128)S(1)}, f32[4]{0:T(128)}, u32[]{:S(2)}) copy-start(f32[4]{0:T(128)} %constant.135.clone) | copy-start | bytes 52
  459.2 14.7 %copy-start.23 = (f32[4]{0:T(128)S(1)}, f32[4]{0:T(128)}, u32[]{:S(2)}) copy-start(f32[4]{0:T(128)} %constant.134.clone) | copy-start | bytes 52
  460.9 4.4 copy-start.11
  465.4 0.7 copy-start.12
  471.2 3.7 collective-permute-start.16
  472.6 5.3 collective-permute-start.17
  475.0 2.9 copy-start.18
  477.9 0.6 copy-start.19

commit v2 on v1

--- a/solution.py
+++ b/solution.py
@@ -21,6 +21,7 @@
 )
 W = 3
 RX = 8
+LEAD = 16
 LANES = 128
 F32 = jnp.float32
 BF16 = jnp.bfloat16
@@ -141,7 +142,7 @@
     u_ref[...] = full(k_ref[...], full(solved, s_ref[...])).reshape(u_ref.shape)
 
 
-def solve(source, scalars, scalar_z):
+def solve(source, sets, sets_z):
     local_z, local_x, local_y = source.shape
     nx, ny, nz = lax.axis_size("gx"), lax.axis_size("gy"), lax.axis_size("gz")
     total_x, total_z = local_x * nx, local_z * nz
@@ -183,17 +184,19 @@
     backward_z = jnp.asarray(cosine.T, F32)
 
     together = lax.optimization_barrier
-    source, scalar_z = together((source, scalar_z))
+    source, first_z = together((source, sets_z[0]))
+    sets_z = [first_z] + sets_z[1:]
     blocks = source.reshape(nx, layers, local_x, local_y)
-    scalar_x = x_halo((scalars,), *scalar_z)
     blocks = lax.all_to_all(blocks, "gx", 0, 0)
-    blocks, scalar_x = together((blocks, scalar_x))
+    blocks, sets_z = together((blocks, sets_z))
+    sets_x = [x_halo(a, *z) for a, z in zip(sets, sets_z)]
     sine_x = sine_half(total_x)
     blocks = x_lines(blocks, split_table(sine_x), group)
-    scalar_pack = y_pack((scalars,), *scalar_z, *scalar_x)
+    blocks, sets_x = together((blocks, sets_x))
+    packs = [y_pack(a, *z, *x) for a, z, x in zip(sets, sets_z, sets_x)]
     blocks = lax.all_to_all(blocks, ("gz", "gx"), 0, 0)
-    blocks, scalar_pack = together((blocks, scalar_pack))
-    scalar_y = shift_pair(*scalar_pack, "gy")
+    blocks, packs = together((blocks, packs))
+    sets_y = [shift_pair(*pack, "gy") for pack in packs]
     columns = blocks.reshape(total_z, part_x, local_y)
 
     cube = pl.BlockSpec((total_z, 8, local_y), lambda i: (0, i, 0))
@@ -260,10 +263,12 @@
 
     blocks = columns.reshape(group, layers, part_x, local_y)
     blocks = lax.all_to_all(blocks, ("gz", "gx"), 0, 0)
-    blocks, scalar_y = together((blocks, scalar_y))
+    blocks, sets_y = together((blocks, sets_y))
     blocks = x_lines(blocks, (jnp.asarray(sine_x.T, F32),), nx)
     blocks = lax.all_to_all(blocks, "gx", 0, 0)
-    return blocks.reshape(local_z, local_x, local_y), scalar_z + scalar_x + scalar_y
+    return blocks.reshape(local_z, local_x, local_y), [
+        tuple(z) + tuple(x) + tuple(y) for z, x, y in zip(sets_z, sets_x, sets_y)
+    ]
 
 
 def shift_pair(low_part, high_part, axis):
@@ -397,8 +402,8 @@
 def assemble(k, local_z, mains, halo, put):
     z_low, z_high, x_low, x_high, y_low, y_high = halo
     local_x, local_y = z_low.shape[2:]
-    every = slice(0, local_x + 2 * RX)
-    inner = slice(RX, RX + local_x)
+    every = slice(LEAD, LEAD + local_x + 2 * RX)
+    inner = slice(LEAD + RX, LEAD + RX + local_x)
     wide = slice(0, local_y)
     lane = lax.broadcasted_iota(jnp.int32, (1, LANES), 1)
     up = lax.rem(2 * LANES - W * k, LANES)
@@ -419,8 +424,8 @@
             def _():
                 put(field, inner, wide, z_high[field, 0])
 
-            put(field, slice(0, RX), wide, x_low[field, 0])
-            put(field, slice(RX + local_x, 2 * RX + local_x), wide, x_high[field, 0])
+            put(field, slice(LEAD, LEAD + RX), wide, x_low[field, 0])
+            put(field, slice(inner.stop, inner.stop + RX), wide, x_high[field, 0])
             put(
                 field,
                 every,
@@ -452,54 +457,108 @@
     return pltpu.roll(jnp.where(row == 7, before, value), 1, 0)
 
 
-def divergence_kernel(local_z, wind, opened, *refs):
-    halo, out, cell, face_z = refs[:6], refs[6], refs[7], refs[8]
-    k = pl.program_id(0) + W - 1
+def edge_kernel(span, first, last, wind, lo_ref, hi_ref):
+    step = pl.program_id(0)
+    lane = lax.broadcasted_iota(jnp.int32, (1, LANES), 1)
+
+    @pl.when(step == 0)
+    def _():
+        lo_ref[...] = jnp.zeros_like(lo_ref)
+        hi_ref[...] = jnp.zeros_like(hi_ref)
+
+    low, high = lo_ref[...], hi_ref[...]
+    for j in range(span):
+        k = step * span + j
+        keep = lane == k
+        low = jnp.where(keep, pltpu.roll(first[0, j], k, 1), low)
+        flux = wind[0, j] * last[0, j]
+        high = jnp.where(keep, pltpu.roll(flux, lax.rem(k + 1, LANES), 1), high)
+    lo_ref[...] = low
+    hi_ref[...] = high
+
+
+def face_edges(wind, opened):
+    local_z, local_x, local_y = wind.shape[1:]
+    span = 8
+    final = local_y // LANES - 1
+    block = (1, span, local_x, LANES)
+    shape = jax.ShapeDtypeStruct((local_x, LANES), F32)
+    first_y, last_y = pl.pallas_call(
+        functools.partial(edge_kernel, span),
+        grid=(local_z // span,),
+        in_specs=[
+            pl.BlockSpec(block, lambda k: (0, k, 0, 0)),
+            pl.BlockSpec(block, lambda k: (0, k, 0, final)),
+            pl.BlockSpec(block, lambda k: (1, k, 0, final)),
+        ],
+        out_specs=[pl.BlockSpec((local_x, LANES), lambda k: (0, 0))] * 2,
+        out_shape=[shape, shape],
+        compiler_params=params(),
+    )(opened, opened, wind)
+    z_pair = shift_pair(opened[0, 0], wind[2, -1] * opened[0, -1], "gz")
+    last_x = slice(local_x - 1, local_x)
+    x_pair = shift_pair(opened[0, :, :1], wind[0, :, last_x] * opened[0, :, last_x], "gx")
+    return z_pair + x_pair + shift_pair(first_y, last_y, "gy")
+
+
+def divergence_kernel(wind, opened, over, z_low, z_high, x_low, x_high, y_low, y_high, out, face_z):
+    k, depth = pl.program_id(0), pl.num_programs(0)
     local_x, local_y = out.shape[1:]
-    lanes = local_y + LANES
-    now, old = lax.rem(k, 2), lax.rem(k + 1, 2)
-
-    def put(field, rows, wide, value):
-        cell[now, field, rows, wide] = value
-
-    assemble(k, local_z, (wind, opened), halo, put)
-    count = local_x // 8 + 2
-    before = jnp.zeros((8, lanes), F32)
-    for i in range(count - 1):
-        here, after = slice(8 * i, 8 * i + 8), slice(8 * i + 8, 8 * i + 16)
-        open_cells = cell[old, 3, here, :]
-        flux_x = cell[old, 0, here, :] * (open_cells * next_x(open_cells, cell[old, 3, after, :]))
-        flux_y = cell[old, 1, here, :] * (open_cells * next_y(open_cells))
-        flux_z = cell[old, 2, here, :] * (open_cells * cell[now, 3, here, :])
-        if i > 0:
-            total = (flux_x - prev_x(flux_x, before)) + (flux_y - prev_y(flux_y))
-            total = total + (flux_z - face_z[here, :])
-            out[0, 8 * i - 8 : 8 * i, :] = total[:, :local_y]
-        face_z[here, :] = flux_z
+    lane = lax.broadcasted_iota(jnp.int32, (1, LANES), 1)
+    before = None
+    for i in range(local_x // 8):
+        rows = slice(8 * i, 8 * i + 8)
+        cells = opened[0, 0, rows, :]
+        if i < local_x // 8 - 1:
+            after = opened[0, 0, 8 * i + 8 : 8 * i + 16, :]
+        else:
+            after = jnp.broadcast_to(x_high[0], cells.shape)
+        if before is None:
+            before = jnp.broadcast_to(x_low[0] * cells[0:1], cells.shape)
+        flux_x = wind[0, 0, rows, :] * (cells * next_x(cells, after))
+        right = pltpu.roll(y_high[rows, :], lax.rem(2 * LANES - 1 - k, LANES), 1)
+        left = pltpu.roll(y_low[rows, :], lax.rem(LANES - k, LANES), 1)
+        beside = next_y(cells)
+        cut = local_y - LANES
+        tail = jnp.where(lane == LANES - 1, right, beside[:, cut:])
+        beside = tail if cut == 0 else jnp.concatenate([beside[:, :cut], tail], 1)
+        flux_y = wind[1, 0, rows, :] * (cells * beside)
+        back = prev_y(flux_y)
+        head = jnp.where(lane == 0, left * cells[:, :LANES], back[:, :LANES])
+        back = head if cut == 0 else jnp.concatenate([head, back[:, LANES:]], 1)
+        above = jnp.where(k == depth - 1, z_high[rows, :], over[0, 0, rows, :])
+        flux_z = wind[2, 0, rows, :] * (cells * above)
+        below = jnp.where(k == 0, z_low[rows, :] * cells, face_z[rows, :])
+        out[0, rows, :] = (flux_x - prev_x(flux_x, before)) + (flux_y - back) + (flux_z - below)
+        face_z[rows, :] = flux_z
         before = flux_x
 
 
-def divergence(wind, opened, wind_halo):
+def divergence(wind, opened, edges):
     local_z, local_x, local_y = wind.shape[1:]
-    plane_of = lambda k: k + W - 1
-    middle = lambda k: (0, jnp.clip(plane_of(k) - W, 0, local_z - 1), 0, 0)
-    lanes = local_y + LANES
-    rows = local_x + 2 * RX
+    plane = pl.BlockSpec((local_x, local_y), lambda k: (0, 0))
+    line = pl.BlockSpec((1, 1, local_y), lambda k: (k, 0, 0))
+    pack = pl.BlockSpec((local_x, LANES), lambda k: (0, 0))
+    one = (1, 1, local_x, local_y)
     return pl.pallas_call(
-        functools.partial(divergence_kernel, local_z),
-        grid=(local_z + 2,),
+        divergence_kernel,
+        grid=(local_z,),
         in_specs=[
-            pl.BlockSpec((3, 1, local_x, local_y), middle),
-            pl.BlockSpec((1, 1, local_x, local_y), middle),
-        ]
-        + halo_specs(4, local_z, local_x, local_y, plane_of),
-        out_specs=pl.BlockSpec(
-            (1, local_x, local_y), lambda k: (jnp.clip(k - 2, 0, local_z - 1), 0, 0)
-        ),
+            pl.BlockSpec((3, 1, local_x, local_y), lambda k: (0, k, 0, 0)),
+            pl.BlockSpec(one, lambda k: (0, k, 0, 0)),
+            pl.BlockSpec(one, lambda k: (0, jnp.minimum(k + 1, local_z - 1), 0, 0)),
+            plane,
+            plane,
+            line,
+            line,
+            pack,
+            pack,
+        ],
+        out_specs=pl.BlockSpec((1, local_x, local_y), lambda k: (k, 0, 0)),
         out_shape=jax.ShapeDtypeStruct((local_z, local_x, local_y), F32),
-        scratch_shapes=[pltpu.VMEM((2, 4, rows, lanes), F32), pltpu.VMEM((rows, lanes), F32)],
+        scratch_shapes=[pltpu.VMEM((local_x, local_y), F32)],
         compiler_params=params(),
-    )(wind, opened, *wind_halo)
+    )(wind, opened, opened, *edges)
 
 
 def limiter(demand, supply):
@@ -520,11 +579,11 @@
     local_x, local_y = out.shape[2:]
     lanes = local_y + LANES
     count = local_x // 8 + 2
-    s0, s1, s2, s3 = (lax.rem(k + 4 - d, 4) for d in range(4))
+    s1, s2, s3 = (lax.rem(k + 3 - d, 3) for d in range(1, 4))
     now, old = lax.rem(k, 2), lax.rem(k + 1, 2)
 
     def put_scalar(field, rows, wide, value):
-        conc[field][s0, rows, wide] = value
+        conc[field][now, rows, wide] = value
 
     def put_wind(field, rows, wide, value):
         cell[now, field, rows, wide] = value
@@ -539,10 +598,27 @@
     def chunk(i):
         return pl.ds(pl.multiple_of(i * 8, 8), 8)
 
-    def column(i, _):
-        here = chunk(i)
-        after = chunk(jnp.minimum(i + 1, count - 1))
-        before = chunk(jnp.maximum(i - 1, 0))
+    def keep_ratios(s, mid, up_new, down_new):
+        ratio[s][now, 0, mid, :] = up_new
+        ratio[s][now, 1, mid, :] = down_new
+
+    def keep(s, here, antis, lows, t_new, u_new, l_new):
+        low_z[s][here, :] = lows[2]
+        edge[s][0] = lows[0]
+        trial[s][s1, here, :] = t_new
+        upper[s][s1, here, :] = u_new
+        lower[s][s1, here, :] = l_new
+        for d in range(3):
+            anti[s][s1, d, here, :] = antis[d]
+
+    def limit(a, up_here, down_here, up_next, down_next):
+        share = jnp.where(
+            a >= 0.0, jnp.minimum(up_next, down_here), jnp.minimum(up_here, down_next)
+        )
+        return share * a
+
+    def column(stages, i, _):
+        last, mid, here, after = (chunk(i + d) for d in range(4))
 
         cells, multiplier = cell[old, 3, here, :], cell[old, 4, here, :]
         neighbours = (
@@ -562,8 +638,8 @@
             speed[d, here, :] = speeds[d][:, :local_y]
 
         for s in range(scalar_count):
-            c = conc[s][s1, here, :]
-            downwind = (next_x(c, conc[s][s1, after, :]), next_y(c), conc[s][s0, here, :])
+            c = conc[s][old, here, :]
+            downwind = (next_x(c, conc[s][old, after, :]), next_y(c), conc[s][now, here, :])
             antis, lows = [], []
             for d in range(3):
                 a = sizes[d] * (downwind[d] - c)
@@ -573,75 +649,87 @@
             t_new = c - (change + (lows[2] - low_z[s][here, :]))
             u_new, l_new = jnp.maximum(c, t_new), jnp.minimum(c, t_new)
 
-            u, l = upper[s][s2, here, :], lower[s][s2, here, :]
+            new = (here, antis, lows, t_new, u_new, l_new)
+            if stages == 1:
+                keep(s, *new)
+                continue
+
+            u, l = upper[s][s2, mid, :], lower[s][s2, mid, :]
             ceiling = jnp.maximum(
-                jnp.maximum(u, u_new),
+                jnp.maximum(u, upper[s][s1, mid, :]),
                 jnp.maximum(
-                    next_x(u, upper[s][s2, after, :]), prev_x(u, upper[s][s2, before, :])
+                    next_x(u, upper[s][s2, here, :]), prev_x(u, upper[s][s2, last, :])
                 ),
             )
             ceiling = jnp.maximum(
-                jnp.maximum(ceiling, upper[s][s3, here, :]), jnp.maximum(next_y(u), prev_y(u))
+                jnp.maximum(ceiling, upper[s][s3, mid, :]), jnp.maximum(next_y(u), prev_y(u))
             )
             bottom = jnp.minimum(
-                jnp.minimum(l, l_new),
+                jnp.minimum(l, lower[s][s1, mid, :]),
                 jnp.minimum(
-                    next_x(l, lower[s][s2, after, :]), prev_x(l, lower[s][s2, before, :])
+                    next_x(l, lower[s][s2, here, :]), prev_x(l, lower[s][s2, last, :])
                 ),
             )
             bottom = jnp.minimum(
-                jnp.minimum(bottom, lower[s][s3, here, :]), jnp.minimum(next_y(l), prev_y(l))
+                jnp.minimum(bottom, lower[s][s3, mid, :]), jnp.minimum(next_y(l), prev_y(l))
             )
-            a_x, a_y, a_z = (anti[s][s2, d, here, :] for d in range(3))
+            a_x, a_y, a_z = (anti[s][s2, d, mid, :] for d in range(3))
             befores = (
-                prev_x(a_x, anti[s][s2, 0, before, :]),
+                prev_x(a_x, anti[s][s2, 0, last, :]),
                 prev_y(a_y),
-                anti[s][s3, 2, here, :],
+                anti[s][s3, 2, mid, :],
             )
             inflow, outflow = 0.0, 0.0
             for a, b in zip((a_x, a_y, a_z), befores):
                 inflow = inflow + (jnp.maximum(b, 0.0) - jnp.minimum(a, 0.0))
                 outflow = outflow + (jnp.maximum(a, 0.0) - jnp.minimum(b, 0.0))
-            t_mid = trial[s][s2, here, :]
+            t_mid = trial[s][s2, mid, :]
             up_new = limiter(inflow, ceiling - t_mid)
             down_new = limiter(outflow, t_mid - bottom)
 
-            r_up, r_down = ratio[s][old, 0, here, :], ratio[s][old, 1, here, :]
-            nexts = (
-                (
-                    next_x(r_up, ratio[s][old, 0, after, :]),
-                    next_x(r_down, ratio[s][old, 1, after, :]),
+            ratios = (mid, up_new, down_new)
+            if stages == 2:
+                keep(s, *new)
+                keep_ratios(s, *ratios)
+                continue
+
+            r_up, r_down = ratio[s][old, 0, last, :], ratio[s][old, 1, last, :]
+            own_up, own_down = r_up[:, :local_y], r_down[:, :local_y]
+            own = slice(0, local_y)
+            limited = (
+                limit(
+                    anti[s][s3, 0, last, own],
+                    own_up,
+                    own_down,
+                    next_x(own_up, ratio[s][old, 0, mid, own]),
+                    next_x(own_down, ratio[s][old, 1, mid, own]),
                 ),
-                (next_y(r_up), next_y(r_down)),
-                (up_new, down_new),
+                limit(anti[s][s3, 1, last, :], r_up, r_down, next_y(r_up), next_y(r_down)),
+                limit(
+                    anti[s][s3, 2, last, own],
+                    own_up,
+                    own_down,
+                    ratio[s][now, 0, last, own],
+                    ratio[s][now, 1, last, own],
+                ),
             )
-            limited = []
-            for d in range(3):
-                a = anti[s][s3, d, here, :]
-                share = jnp.where(
-                    a >= 0.0, jnp.minimum(nexts[d][0], r_down), jnp.minimum(r_up, nexts[d][1])
-                )
-                limited.append(share * a)
-            moved = limited[0] - prev_x(limited[0], edge[s][1])
-            moved = moved + (limited[1] - prev_y(limited[1])) + (limited[2] - lim_z[s][here, :])
-            final = trial[s][s3, here, :] - moved
-
-            result[s][here, :] = final[:, :local_y]
-            lim_z[s][here, :] = limited[2]
-            edge[s][1] = limited[0]
-            ratio[s][now, 0, here, :] = up_new
-            ratio[s][now, 1, here, :] = down_new
-            trial[s][s1, here, :] = t_new
-            upper[s][s1, here, :] = u_new
-            lower[s][s1, here, :] = l_new
-            low_z[s][here, :] = lows[2]
-            edge[s][0] = lows[0]
-            for d in range(3):
-                anti[s][s1, d, here, :] = antis[d]
+            moved = limited[0] - prev_x(limited[0], edge[s][1, :, own])
+            moved = moved + (limited[1] - prev_y(limited[1]))[:, :local_y]
+            moved = moved + (limited[2] - lim_z[s][last, :])
+            result[s][last, :] = trial[s][s3, last, own] - moved
+            lim_z[s][last, :] = limited[2]
+            edge[s][1, :, own] = limited[0]
+            keep_ratios(s, *ratios)
+            keep(s, *new)
         return 0
 
-    lax.fori_loop(0, count, column, 0)
-    inner = slice(RX, RX + local_x)
+    for stages, begin, end in ((1, 1, 4), (2, 4, 5), (3, 5, local_z + 2 * W)):
+
+        @pl.when((k >= begin) & (k < end))
+        def _():
+            lax.fori_loop(0, count + 1, functools.partial(column, stages), 0)
+
+    inner = slice(LEAD + RX, LEAD + RX + local_x)
 
     @pl.when((k > W) & (k <= W + local_z))
     def _():
@@ -664,7 +752,7 @@
     same = lambda k: k
     middle = lambda k: (0, jnp.clip(k - W, 0, local_z - 1), 0, 0)
     lanes = local_y + LANES
-    rows = local_x + 2 * RX
+    rows = local_x + 2 * RX + 2 * LEAD
     plane = (rows, lanes)
 
     def main(count):
@@ -700,14 +788,14 @@
         + [
             pltpu.VMEM(shape, F32)
             for shape in (
-                (4,) + plane,
-                (4,) + plane,
-                (4,) + plane,
-                (4,) + plane,
-                (4, 3) + plane,
+                (2,) + plane,
+                (3,) + plane,
+                (3,) + plane,
+                (3,) + plane,
+                (3, 3) + plane,
                 (2, 2) + plane,
                 plane,
-                plane,
+                (rows, local_y),
                 (2, 8, lanes),
                 (rows, local_y),
             )
@@ -728,13 +816,11 @@
 
 def body(initial_wind, building_mask, surface_flags, scalars):
     opened = (1.0 - building_mask.astype(F32))[None]
-    wind_z = z_halo((initial_wind, opened))
-    scalar_z = z_halo((scalars,), wind_z)
-    wind_x = x_halo((initial_wind, opened), *wind_z)
-    wind_y = shift_pair(*y_pack((initial_wind, opened), *wind_z, *wind_x), "gy")
-    wind_halo = wind_z + wind_x + wind_y
-    source = divergence(initial_wind, opened, wind_halo)
-    multiplier, scalar_halo = solve(source, scalars, scalar_z)
+    edges = face_edges(initial_wind, opened)
+    sets = [(initial_wind, opened), (scalars,)]
+    sets_z = [z_halo(arrays, edges[:2]) for arrays in sets]
+    source = divergence(initial_wind, opened, edges)
+    multiplier, (wind_halo, scalar_halo) = solve(source, sets, sets_z)
     multiplier = multiplier[None]
     mult_halo = halos((multiplier,))
     corrected, transported = transport(

time: 753 us -> 686 us (0.911)
  waiting for transfers between devices: 193 us -> 118 us
  Pallas kernels: 402 us -> 380 us
  starting transfers between devices: 64.2 us -> 83.8 us
  other arithmetic: 6.05 us -> 16.2 us
    ppermute x9 -> x12, waiting for transfers between devices: 93.2 us -> 40.4 us  [shift_pair(): lax.ppermute(high_part, axis, up)]
    all_to_all x2, waiting for transfers between devices: 64.6 us -> 43.7 us  [solve(): blocks = lax.all_to_all(blocks, ('gz', 'gx'), 0, 0)]
    pallas_call x1, Pallas kernels: 272 us -> 255 us  [transport(): pl.pallas_call(functools.partial(transport_kernel, local_z, n), grid=(loc...]
    ppermute x9 -> x12, starting transfers between devices: 22.1 us -> 33.5 us  [shift_pair(): lax.ppermute(high_part, axis, up)]
    ppermute x9 -> x12, starting transfers between devices: 22.5 us -> 30.1 us  [shift_pair(): lax.ppermute(low_part, axis, down)]
    ppermute x9 -> x12, waiting for transfers between devices: 35.2 us -> 28.7 us  [shift_pair(): lax.ppermute(low_part, axis, down)]
    pallas_call x1 -> x2, Pallas kernels: 32.4 us -> 28.2 us  [the longest x1 23.5 us: divergence(): pl.pallas_call(divergence_kernel, grid=(local_z,), in_specs=[pl.BlockSpec...]
  transfers between devices with their start and end apart: 21 -> 27, of which waited for: 17 -> 18; matrix products, arithmetic and copies ran while one was open for 2% -> 3% of each run, Pallas kernels for 8% -> 9%
where the time goes in v2:
time: 686 us; the launch traced here: 683 us
  Pallas kernels  380 us (55%)
  waiting for transfers between devices  118 us (17%)
  starting transfers between devices  83.8 us (12%)
  blocking collectives  64.3 us (9%)
  local copies, waits for them, and re-layouts  19.8 us (3%)
  other arithmetic  16.2 us (2%)
    pallas_call x1, Pallas kernels, transport(): pl.pallas_call(functools.partial(transport_kernel, local_z, n), grid=(loc...  255 us
    all_to_all x1, blocking collectives, solve(): blocks = lax.all_to_all(blocks, 'gx', 0, 0)  53.6 us
    all_to_all x2, waiting for transfers between devices, solve(): blocks = lax.all_to_all(blocks, ('gz', 'gx'), 0, 0)  43.7 us
    ppermute x12, waiting for transfers between devices, shift_pair(): lax.ppermute(high_part, axis, up)  40.4 us
    ppermute x12, starting transfers between devices, shift_pair(): lax.ppermute(high_part, axis, up)  33.5 us
    ppermute x12, starting transfers between devices, shift_pair(): lax.ppermute(low_part, axis, down)  30.1 us
    pallas_call x3, Pallas kernels, y_pack(): pl.pallas_call(functools.partial(pack_kernel, groups, span), grid=(local_...  29.6 us
    pallas_call x1, Pallas kernels, solve(): pl.pallas_call(backward_kernel, grid=(tiles,), in_specs=[cube, small, tab...  28.8 us
  transfers between devices with their start and end apart: 27, of which 18 were waited for; matrix products, arithmetic and copies ran while one was open for 3% of the time, Pallas kernels for 9%

profile of v2, /device:TPU:5, one launch (start us, length us, event | category | flops | bytes accessed | tf_op | source)
XLA Modules:
  0.0 683.4 jit_solution(15809862494839278195)
XLA Ops:
  0.6 2.6 subtract_bitcast_fusion.first.last.opened.over.refs_1_.refs_3_.refs_8_
  8.9 2.0 pad_maximum_fusion
  13.2 4.2 collective-permute-start.7
  18.4 4.0 collective-permute-start.3
  22.4 4.6 shard_map.293
  27.1 4.0 collective-permute-start.4
  32.4 3.3 collective-permute-start.2
  38.0 23.5 %shard_map.294 = f32[32,128,256]{2,1,0:T(8,128)} custom-call(f32[3,32,128,256]{3,2,1,0:T(8,128)} %refs_7_.1, f32[1,32,128,256]{3,2,1,0:T(8,128)} %copy-done, f32[1,32,128,256]{3,2,1,0:T(8,128)} %copy-done, f32[128,256]{1,0:T(8,128)} %copy-done.20, f32[128,256]{1,0:T(8,128)} %copy-done.19, f32[32,1,256]{2,1,0:T(1,128)} %copy-done.27, ...), custom_call_target="tpu_custom_call" | custom-call | tf_op jit(solution)/shard_map/pallas_call | solution.py:543
  61.6 5.2 all-to-all-start
  66.8 2.2 fusion.35
  70.3 6.3 collective-permute-start.9
  78.4 2.7 fusion.36
  81.1 3.0 fusion.34
  84.1 22.8 %collective-permute-done.8.refs_2_.refs_3_.refs_1_ = f32[4,3,128,256]{3,2,1,0:T(8,128)} collective-permute-done((f32[4,3,128,256]{3,2,1,0:T(8,128)S(1)}, f32[4,3,128,256]{3,2,1,0:T(8,128)}, u32[]{:S(2)}, u32[]{:S(2)}) %collective-permute-start.8) | collective-permute-done | bytes 1572896 | tf_op jit(solution)/shard_map/ppermute | solution.py:278
  106.9 1.9 collective-permute-done.9.refs_4_.refs_5_.refs_2_
  108.9 4.8 all-to-all-done.x_ref
  116.9 3.4 collective-permute-start.10
  121.5 2.0 collective-permute-start.11
  124.6 3.6 collective-permute-start.12
  131.4 8.9 %shard_map.295 = f32[8,8,64,256]{3,2,1,0:T(8,128)} custom-call(f32[4,8,128,256]{3,2,1,0:T(8,128)} %all-to-all-done.x_ref, bf16[512,512]{1,0:T(8,128)(2,1)} %constant.120.clone.refs_0_, bf16[512,512]{1,0:T(8,128)(2,1)} %constant.121.clone.refs_1_), custom_call_target="tpu_custom_call" | custom-call | tf_op jit(solution)/shard_map/pallas_call | solution.py:103
  140.3 7.5 %collective-permute-done.12.refs_6_.refs_7_.refs_3_ = f32[4,38,8,256]{3,2,1,0:T(8,128)} collective-permute-done((f32[4,38,8,256]{3,2,1,0:T(8,128)}, f32[4,38,8,256]{3,2,1,0:T(8,128)}, u32[]{:S(2)}, u32[]{:S(2)}) %collective-permute-start.12) | collective-permute-done | bytes 1245216 | tf_op jit(solution)/shard_map/ppermute | solution.py:278
  147.8 5.7 collective-permute-done.13.refs_8_.refs_9_.refs_4_
  153.5 4.6 all-to-all-start.1
  159.0 2.0 copy.50.lam_ref
  160.9 12.3 %shard_map.297 = (f32[4,144,128]{2,1,0:T(8,128)}, f32[4,144,128]{2,1,0:T(8,128)}) custom-call(f32[4,32,128,256]{3,2,1,0:T(8,128)} %refs_0_.7, f32[4,32,128,256]{3,2,1,0:T(8,128)} %refs_0_.7, f32[4,3,128,256]{3,2,1,0:T(8,128)} %collective-permute-done.8.refs_2_.refs_3_.refs_1_, f32[4,3,128,256]{3,2,1,0:T(8,128)} %collective-permute-done.8.refs_2_.refs_3_.refs_1_, ...), custom_call_target="tpu_custom_call" | custom-call | tf_op jit(solution)/shard_map/pallas_call | solution.py:370
  173.2 12.2 %shard_map.296 = (f32[4,144,128]{2,1,0:T(8,128)}, f32[4,144,128]{2,1,0:T(8,128)}) custom-call(f32[3,32,128,256]{3,2,1,0:T(8,128)} %refs_7_.1, f32[1,32,128,256]{3,2,1,0:T(8,128)} %copy-done, f32[3,32,128,256]{3,2,1,0:T(8,128)} %refs_7_.1, f32[1,32,128,256]{3,2,1,0:T(8,128)} %copy-done, f32[4,3,128,256]{3,2,1,0:T(8,128)} %copy-done.2, ...), custom_call_target="tpu_custom_call" | custom-call | tf_op jit(solution)/shard_map/pallas_call | solution.py:370
  185.4 17.5 %all-to-all-done.1 = f32[8,8,64,256]{3,2,1,0:T(8,128)} async-done(((f32[8,8,64,256]{3,2,1,0:T(8,128)}), f32[8,8,64,256]{3,2,1,0:T(8,128)}, u32[]{:S(2)}, u32[]{:S(2)}) %all-to-all-start.1) | async-done | bytes 4194336 | tf_op jit(solution)/shard_map/all_to_all | solution.py:197
  202.9 18.4 %shard_map.298 = (f32[64,64,256]{2,1,0:T(8,128)}, f32[8,8,512]{2,1,0:T(8,128)}) custom-call(f32[64,64,256]{2,1,0:T(8,128)} %bitcast.6.x_ref, bf16[256,256]{1,0:T(8,128)(2,1)} %constant.115.clone.s_high, bf16[256,256]{1,0:T(8,128)(2,1)} %constant.116.clone.s_low, bf16[512,512]{1,0:T(8,128)(2,1)} %constant.117.clone.k_high, ...), custom_call_target="tpu_custom_call" | custom-call | tf_op jit(solution)/shard_map/pallas_call | solution.py:213
  222.3 10.7 %all-gather = f32[32,2,512]{2,1,0:T(2,128)S(1)} all-gather(f32[8,2,512]{2,1,0:T(2,128)S(1)} %slice.155), channel_id=2, replica_groups=mesh['gx'=4,'gy'=4,'gz'=2] {'gy'}, dimensions={0}, use_global_device_ids=true | all-gather | bytes 163840 | tf_op jit(solution)/shard_map/all_gather | solution.py:225
  236.8 28.8 %shard_map.299 = f32[64,64,256]{2,1,0:T(8,128)} custom-call(f32[64,64,256]{2,1,0:T(8,128)} %get-tuple-element.63.b_ref, f32[8,8,512]{2,1,0:T(8,128)} %maximum_maximum_fusion.ab_ref, f32[256,256]{1,0:T(8,128)} %constant.132.clone.s_ref, f32[512,512]{1,0:T(8,128)} %constant.119.clone.k_ref, f32[8,512,1]{2,1,0:T(8,128)} %copy.50.lam_ref, ...), custom_call_target="tpu_custom_call" | custom-call | tf_op jit(solution)/shard_map/pallas_call | solution.py:255
  265.5 10.5 %all-to-all-start.2 = ((f32[8,8,64,256]{3,2,1,0:T(8,128)}), f32[8,8,64,256]{3,2,1,0:T(8,128)}, u32[]{:S(2)}, u32[]{:S(2)}) async-start(f32[8,8,64,256]{3,2,1,0:T(8,128)} %bitcast.104), calls=%async_computation.2 | async-start | bytes 8388608 | tf_op jit(solution)/shard_map/all_to_all | solution.py:265
  276.0 2.7 collective-permute-start.14
  280.1 4.0 collective-permute-start.16
  285.4 3.2 collective-permute-done.15.refs_14_
  288.6 2.5 collective-permute-done.16.refs_5_
  291.1 4.1 collective-permute-done.17.refs_6_
  295.2 26.2 %all-to-all-done.2.x_ref = f32[8,8,64,256]{3,2,1,0:T(8,128)} async-done(((f32[8,8,64,256]{3,2,1,0:T(8,128)}), f32[8,8,64,256]{3,2,1,0:T(8,128)}, u32[]{:S(2)}, u32[]{:S(2)}) %all-to-all-start.2) | async-done | bytes 4194336 | tf_op jit(solution)/shard_map/all_to_all | solution.py:265
  321.4 11.4 %shard_map.300 = f32[4,8,128,256]{3,2,1,0:T(8,128)} custom-call(f32[8,8,64,256]{3,2,1,0:T(8,128)} %all-to-all-done.2.x_ref, f32[512,512]{1,0:T(8,128)} %constant.133.clone.refs_0_), custom_call_target="tpu_custom_call" | custom-call | tf_op jit(solution)/shard_map/pallas_call | solution.py:103
  332.9 53.6 %all_to_all.20 = f32[4,8,128,256]{3,2,1,0:T(8,128)S(1)} all-to-all(f32[4,8,128,256]{3,2,1,0:T(8,128)} %shard_map.300), channel_id=1, replica_groups=mesh['gx'=4,'gy'=4,'gz'=2] {'gx'}, dimensions={0} | all-to-all | bytes 8388608 | tf_op jit(solution)/shard_map/all_to_all | solution.py:268
  386.6 3.3 collective-permute-start.19
  391.2 6.0 collective-permute-done.19.refs_4_.refs_5_.refs_17_
  397.2 3.8 collective-permute-done.18.refs_2_.refs_3_.refs_16_
  401.1 4.5 collective-permute-start.20
  409.5 4.4 collective-permute-done.21.refs_8_.refs_9_.refs_19_
  414.6 5.1 shard_map.301
  419.7 2.7 collective-permute-start.22
  424.8 2.9 collective-permute-done.23.refs_21_
  428.3 254.9 %shard_map.302 = (f32[3,32,128,256]{3,2,1,0:T(8,128)}, f32[4,32,128,256]{3,2,1,0:T(8,128)}) custom-call(f32[4,32,128,256]{3,2,1,0:T(8,128)} %refs_0_.7, f32[4,3,128,256]{3,2,1,0:T(8,128)} %collective-permute-done.8.refs_2_.refs_3_.refs_1_, f32[4,3,128,256]{3,2,1,0:T(8,128)} %collective-permute-done.9.refs_4_.refs_5_.refs_2_, ...), custom_call_target="tpu_custom_call" | custom-call | tf_op jit(solution)/shard_map/pallas_call | solution.py:764
  (127 shorter events, 41.2 us)
Async XLA Ops:
  3.2 14.2 %copy-start = (f32[1,32,128,256]{3,2,1,0:T(8,128)}, f32[1,32,128,256]{3,2,1,0:T(8,128)S(1)}, u32[]{:S(2)}) copy-start(f32[1,32,128,256]{3,2,1,0:T(8,128)S(1)} %subtract_bitcast_fusion.first.last.opened.over.refs_1_.refs_3_.refs_8_) | copy-start | bytes 12582916
  4.3 6.6 collective-permute-start.1
  5.7 6.3 collective-permute-start
  10.9 16.2 %copy-start.19 = (f32[128,256]{1,0:T(8,128)}, f32[128,256]{1,0:T(8,128)S(1)}, u32[]{:S(2)}) copy-start(f32[128,256]{1,0:T(8,128)S(1)} %collective-permute-done.1.z_high) | copy-start | bytes 393220
  11.9 15.2 %copy-start.20 = (f32[128,256]{1,0:T(8,128)}, f32[128,256]{1,0:T(8,128)S(1)}, u32[]{:S(2)}) copy-start(f32[128,256]{1,0:T(8,128)S(1)} %collective-permute-done.z_low) | copy-start | bytes 393220
  11.9 49.6 %collective-permute-start.6 = (f32[4,3,128,256]{3,2,1,0:T(8,128)}, f32[4,3,128,256]{3,2,1,0:T(8,128)S(1)}, u32[]{:S(2)}, u32[]{:S(2)}) collective-permute-start(f32[4,3,128,256]{3,2,1,0:T(8,128)} %get-tuple-element.41), channel_id=1, source_target_pairs={{0,1},{2,3},{4,5},{6,7},{8,9},{10,11},{12,13},{14,15},{16,17},{18,... | collective-permute-start | bytes 4718600 | tf_op jit(solution)/shard_map/ppermute | solution.py:278
  13.2 48.4 %collective-permute-start.7 = (f32[4,3,128,256]{3,2,1,0:T(8,128)}, f32[4,3,128,256]{3,2,1,0:T(8,128)S(1)}, u32[]{:S(2)}, u32[]{:S(2)}) collective-permute-start(f32[4,3,128,256]{3,2,1,0:T(8,128)} %get-tuple-element.42), channel_id=1, source_target_pairs={{1,0},{3,2},{5,4},{7,6},{9,8},{11,10},{13,12},{15,14},{17,16},{19,... | collective-permute-start | bytes 4718600 | tf_op jit(solution)/shard_map/ppermute | solution.py:278
  18.4 14.0 %collective-permute-start.3 = (f32[32,1,256]{2,1,0:T(1,128)S(1)}, f32[32,1,256]{2,1,0:T(1,128)S(1)}, u32[]{:S(2)}, u32[]{:S(2)}) collective-permute-start(f32[32,1,256]{2,1,0:T(1,128)S(1)} %get-tuple-element.100), channel_id=1, source_target_pairs={{8,0},{16,8},{24,16},{9,1},{17,9},{25,17},{10,2},{18,10},{26,18},{... | collective-permute-start | bytes 98312 | tf_op jit(solution)/shard_map/ppermute | solution.py:278
  27.1 9.7 %collective-permute-start.4 = (f32[128,128]{1,0:T(8,128)}, f32[128,128]{1,0:T(8,128)S(1)}, u32[]{:S(2)}, u32[]{:S(2)}) collective-permute-start(f32[128,128]{1,0:T(8,128)} %get-tuple-element.39), channel_id=1, source_target_pairs={{0,2},{2,4},{4,6},{1,3},{3,5},{5,7},{8,10},{10,12},{12,14},{9,11},... | collective-permute-start | bytes 196616 | tf_op jit(solution)/shard_map/ppermute | solution.py:278
  31.1 6.1 collective-permute-start.5
  32.4 4.3 collective-permute-start.2
  61.6 54.1 %copy-start.2 = (f32[4,3,128,256]{3,2,1,0:T(8,128)}, f32[4,3,128,256]{3,2,1,0:T(8,128)S(1)}, u32[]{:S(2)}) copy-start(f32[4,3,128,256]{3,2,1,0:T(8,128)S(1)} %collective-permute-done.6.refs_4_.refs_5_.refs_9_) | copy-start | bytes 4718596
  61.6 54.2 %copy-start.3 = (f32[4,3,128,256]{3,2,1,0:T(8,128)}, f32[4,3,128,256]{3,2,1,0:T(8,128)S(1)}, u32[]{:S(2)}) copy-start(f32[4,3,128,256]{3,2,1,0:T(8,128)S(1)} %collective-permute-done.7.refs_6_.refs_7_.refs_10_) | copy-start | bytes 4718596
  61.6 52.1 %all-to-all-start = ((f32[4,8,128,256]{3,2,1,0:T(8,128)}), f32[4,8,128,256]{3,2,1,0:T(8,128)}, u32[]{:S(2)}, u32[]{:S(2)}) async-start(f32[4,8,128,256]{3,2,1,0:T(8,128)} %bitcast.103), calls=%async_computation | async-start | bytes 8388608 | tf_op jit(solution)/shard_map/all_to_all | solution.py:190
  69.0 38.0 %collective-permute-start.8 = (f32[4,3,128,256]{3,2,1,0:T(8,128)S(1)}, f32[4,3,128,256]{3,2,1,0:T(8,128)}, u32[]{:S(2)}, u32[]{:S(2)}) collective-permute-start(f32[4,3,128,256]{3,2,1,0:T(8,128)S(1)} %get-tuple-element.46), channel_id=1, source_target_pairs={{0,1},{2,3},{4,5},{6,7},{8,9},{10,11},{12,13},{14,15},{16,17},{18,... | collective-permute-start | bytes 4718600 | tf_op jit(solution)/shard_map/ppermute | solution.py:278
  70.3 38.6 %collective-permute-start.9 = (f32[4,3,128,256]{3,2,1,0:T(8,128)S(1)}, f32[4,3,128,256]{3,2,1,0:T(8,128)}, u32[]{:S(2)}, u32[]{:S(2)}) collective-permute-start(f32[4,3,128,256]{3,2,1,0:T(8,128)S(1)} %get-tuple-element.47), channel_id=1, source_target_pairs={{1,0},{3,2},{5,4},{7,6},{9,8},{11,10},{13,12},{15,14},{17,16},{19,... | collective-permute-start | bytes 4718600 | tf_op jit(solution)/shard_map/ppermute | solution.py:278
  116.9 23.4 %collective-permute-start.10 = (f32[4,38,8,256]{3,2,1,0:T(8,128)}, f32[4,38,8,256]{3,2,1,0:T(8,128)S(1)}, u32[]{:S(2)}, u32[]{:S(2)}) collective-permute-start(f32[4,38,8,256]{3,2,1,0:T(8,128)} %pad_maximum_fusion.2), channel_id=1, source_target_pairs={{0,8},{8,16},{16,24},{1,9},{9,17},{17,25},{2,10},{10,18},{18,26},{... | collective-permute-start | bytes 3735560 | tf_op jit(solution)/shard_map/ppermute | solution.py:278
  121.5 18.8 %collective-permute-start.11 = (f32[4,38,8,256]{3,2,1,0:T(8,128)}, f32[4,38,8,256]{3,2,1,0:T(8,128)S(1)}, u32[]{:S(2)}, u32[]{:S(2)}) collective-permute-start(f32[4,38,8,256]{3,2,1,0:T(8,128)} %pad_maximum_fusion.3), channel_id=1, source_target_pairs={{8,0},{16,8},{24,16},{9,1},{17,9},{25,17},{10,2},{18,10},{26,18},{... | collective-permute-start | bytes 3735560 | tf_op jit(solution)/shard_map/ppermute | solution.py:278
  124.6 23.1 %collective-permute-start.12 = (f32[4,38,8,256]{3,2,1,0:T(8,128)}, f32[4,38,8,256]{3,2,1,0:T(8,128)}, u32[]{:S(2)}, u32[]{:S(2)}) collective-permute-start(f32[4,38,8,256]{3,2,1,0:T(8,128)} %pad_maximum_fusion.4), channel_id=1, source_target_pairs={{0,8},{8,16},{16,24},{1,9},{9,17},{17,25},{2,10},{10,18},{18,26},{... | collective-permute-start | bytes 3735560 | tf_op jit(solution)/shard_map/ppermute | solution.py:278
  129.4 24.0 %collective-permute-start.13 = (f32[4,38,8,256]{3,2,1,0:T(8,128)}, f32[4,38,8,256]{3,2,1,0:T(8,128)}, u32[]{:S(2)}, u32[]{:S(2)}) collective-permute-start(f32[4,38,8,256]{3,2,1,0:T(8,128)} %pad_maximum_fusion.5), channel_id=1, source_target_pairs={{8,0},{16,8},{24,16},{9,1},{17,9},{25,17},{10,2},{18,10},{26,18},{... | collective-permute-start | bytes 3735560 | tf_op jit(solution)/shard_map/ppermute | solution.py:278
  140.3 13.2 %copy-start.4 = (f32[4,38,8,256]{3,2,1,0:T(8,128)}, f32[4,38,8,256]{3,2,1,0:T(8,128)S(1)}, u32[]{:S(2)}) copy-start(f32[4,38,8,256]{3,2,1,0:T(8,128)S(1)} %collective-permute-done.10.refs_8_.refs_9_.refs_11_) | copy-start | bytes 3735556
  140.3 13.2 %copy-start.5 = (f32[4,38,8,256]{3,2,1,0:T(8,128)}, f32[4,38,8,256]{3,2,1,0:T(8,128)S(1)}, u32[]{:S(2)}) copy-start(f32[4,38,8,256]{3,2,1,0:T(8,128)S(1)} %collective-permute-done.11.refs_10_.refs_11_.refs_12_) | copy-start | bytes 3735556
  153.5 49.4 %all-to-all-start.1 = ((f32[8,8,64,256]{3,2,1,0:T(8,128)}), f32[8,8,64,256]{3,2,1,0:T(8,128)}, u32[]{:S(2)}, u32[]{:S(2)}) async-start(f32[8,8,64,256]{3,2,1,0:T(8,128)} %shard_map.295), calls=%async_computation.1 | async-start | bytes 8388608 | tf_op jit(solution)/shard_map/all_to_all | solution.py:197
  265.5 13.2 %copy-start.34 = (f32[4,144,128]{2,1,0:T(8,128)S(1)}, f32[4,144,128]{2,1,0:T(8,128)}, u32[]{:S(2)}) copy-start(f32[4,144,128]{2,1,0:T(8,128)} %get-tuple-element.66) | copy-start | bytes 884740
  265.5 14.5 %copy-start.33 = (f32[4,144,128]{2,1,0:T(8,128)S(1)}, f32[4,144,128]{2,1,0:T(8,128)}, u32[]{:S(2)}) copy-start(f32[4,144,128]{2,1,0:T(8,128)} %get-tuple-element.67) | copy-start | bytes 884740
  265.5 18.6 %copy-start.32 = (f32[4,144,128]{2,1,0:T(8,128)S(1)}, f32[4,144,128]{2,1,0:T(8,128)}, u32[]{:S(2)}) copy-start(f32[4,144,128]{2,1,0:T(8,128)} %get-tuple-element.68) | copy-start | bytes 884740
  265.5 55.9 %all-to-all-start.2 = ((f32[8,8,64,256]{3,2,1,0:T(8,128)}), f32[8,8,64,256]{3,2,1,0:T(8,128)}, u32[]{:S(2)}, u32[]{:S(2)}) async-start(f32[8,8,64,256]{3,2,1,0:T(8,128)} %bitcast.104), calls=%async_computation.2 | async-start | bytes 8388608 | tf_op jit(solution)/shard_map/all_to_all | solution.py:265
  276.0 9.4 %collective-permute-start.14 = (f32[4,144,128]{2,1,0:T(8,128)S(1)}, f32[4,144,128]{2,1,0:T(8,128)S(1)}, u32[]{:S(2)}, u32[]{:S(2)}) collective-permute-start(f32[4,144,128]{2,1,0:T(8,128)S(1)} %copy-done.35), channel_id=1, source_target_pairs={{0,2},{2,4},{4,6},{1,3},{3,5},{5,7},{8,10},{10,12},{12,14},{9,11},... | collective-permute-start | bytes 884744 | tf_op jit(solution)/shard_map/ppermute | solution.py:278
  278.8 9.8 %collective-permute-start.15 = (f32[4,144,128]{2,1,0:T(8,128)S(1)}, f32[4,144,128]{2,1,0:T(8,128)S(1)}, u32[]{:S(2)}, u32[]{:S(2)}) collective-permute-start(f32[4,144,128]{2,1,0:T(8,128)S(1)} %copy-done.34), channel_id=1, source_target_pairs={{2,0},{4,2},{6,4},{3,1},{5,3},{7,5},{10,8},{12,10},{14,12},{11,9},... | collective-permute-start | bytes 884744 | tf_op jit(solution)/shard_map/ppermute | solution.py:278
  280.1 11.0 %collective-permute-start.16 = (f32[4,144,128]{2,1,0:T(8,128)S(1)}, f32[4,144,128]{2,1,0:T(8,128)S(1)}, u32[]{:S(2)}, u32[]{:S(2)}) collective-permute-start(f32[4,144,128]{2,1,0:T(8,128)S(1)} %copy-done.33), channel_id=1, source_target_pairs={{0,2},{2,4},{4,6},{1,3},{3,5},{5,7},{8,10},{10,12},{12,14},{9,11},... | collective-permute-start | bytes 884744 | tf_op jit(solution)/shard_map/ppermute | solution.py:278
  284.1 11.1 %collective-permute-start.17 = (f32[4,144,128]{2,1,0:T(8,128)S(1)}, f32[4,144,128]{2,1,0:T(8,128)S(1)}, u32[]{:S(2)}, u32[]{:S(2)}) collective-permute-start(f32[4,144,128]{2,1,0:T(8,128)S(1)} %copy-done.32), channel_id=1, source_target_pairs={{2,0},{4,2},{6,4},{3,1},{5,3},{7,5},{10,8},{12,10},{14,12},{11,9},... | collective-permute-start | bytes 884744 | tf_op jit(solution)/shard_map/ppermute | solution.py:278
  285.4 47.4 %copy-start.15 = (f32[4,144,128]{2,1,0:T(8,128)}, f32[4,144,128]{2,1,0:T(8,128)S(1)}, u32[]{:S(2)}) copy-start(f32[4,144,128]{2,1,0:T(8,128)S(1)} %collective-permute-done.14.refs_13_) | copy-start | bytes 884740
  288.6 44.3 %copy-start.16 = (f32[4,144,128]{2,1,0:T(8,128)}, f32[4,144,128]{2,1,0:T(8,128)S(1)}, u32[]{:S(2)}) copy-start(f32[4,144,128]{2,1,0:T(8,128)S(1)} %collective-permute-done.15.refs_14_) | copy-start | bytes 884740
  291.1 41.8 %copy-start.17 = (f32[4,144,128]{2,1,0:T(8,128)}, f32[4,144,128]{2,1,0:T(8,128)S(1)}, u32[]{:S(2)}) copy-start(f32[4,144,128]{2,1,0:T(8,128)S(1)} %collective-permute-done.16.refs_5_) | copy-start | bytes 884740
  295.2 37.7 %copy-start.18 = (f32[4,144,128]{2,1,0:T(8,128)}, f32[4,144,128]{2,1,0:T(8,128)S(1)}, u32[]{:S(2)}) copy-start(f32[4,144,128]{2,1,0:T(8,128)S(1)} %collective-permute-done.17.refs_6_) | copy-start | bytes 884740
  386.6 21.0 %copy-start.21 = (s32[128,256]{1,0:T(8,128)S(1)}, s32[128,256]{1,0:T(8,128)}, u32[]{:S(2)}) copy-start(s32[128,256]{1,0:T(8,128)} %param.32) | copy-start | bytes 393220
  386.6 10.6 %collective-permute-start.19 = (f32[1,3,128,256]{3,2,1,0:T(8,128)S(1)}, f32[1,3,128,256]{3,2,1,0:T(8,128)S(1)}, u32[]{:S(2)}, u32[]{:S(2)}) collective-permute-start(f32[1,3,128,256]{3,2,1,0:T(8,128)S(1)} %get-tuple-element.94), channel_id=1, source_target_pairs={{1,0},{3,2},{5,4},{7,6},{9,8},{11,10},{13,12},{15,14},{17,16},{19,... | collective-permute-start | bytes 1179656 | tf_op jit(solution)/shard_map/ppermute | solution.py:278
  389.9 11.2 %collective-permute-start.18 = (f32[1,3,128,256]{3,2,1,0:T(8,128)S(1)}, f32[1,3,128,256]{3,2,1,0:T(8,128)S(1)}, u32[]{:S(2)}, u32[]{:S(2)}) collective-permute-start(f32[1,3,128,256]{3,2,1,0:T(8,128)S(1)} %get-tuple-element.95), channel_id=1, source_target_pairs={{0,1},{2,3},{4,5},{6,7},{8,9},{10,11},{12,13},{14,15},{16,17},{18,... | collective-permute-start | bytes 1179656 | tf_op jit(solution)/shard_map/ppermute | solution.py:278
  397.2 16.7 %copy-start.8 = (f32[1,3,128,256]{3,2,1,0:T(8,128)}, f32[1,3,128,256]{3,2,1,0:T(8,128)S(1)}, u32[]{:S(2)}) copy-start(f32[1,3,128,256]{3,2,1,0:T(8,128)S(1)} %collective-permute-done.19.refs_4_.refs_5_.refs_17_) | copy-start | bytes 1179652
  401.0 12.8 %copy-start.9 = (f32[1,3,128,256]{3,2,1,0:T(8,128)}, f32[1,3,128,256]{3,2,1,0:T(8,128)S(1)}, u32[]{:S(2)}) copy-start(f32[1,3,128,256]{3,2,1,0:T(8,128)S(1)} %collective-permute-done.18.refs_2_.refs_3_.refs_16_) | copy-start | bytes 1179652
  401.1 8.4 %collective-permute-start.20 = (f32[1,38,8,256]{3,2,1,0:T(8,128)S(1)}, f32[1,38,8,256]{3,2,1,0:T(8,128)S(1)}, u32[]{:S(2)}, u32[]{:S(2)}) collective-permute-start(f32[1,38,8,256]{3,2,1,0:T(8,128)S(1)} %pad_maximum_fusion.6), channel_id=1, source_target_pairs={{0,8},{8,16},{16,24},{1,9},{9,17},{17,25},{2,10},{10,18},{18,26},{... | collective-permute-start | bytes 933896 | tf_op jit(solution)/shard_map/ppermute | solution.py:278
  405.7 8.2 %collective-permute-start.21 = (f32[1,38,8,256]{3,2,1,0:T(8,128)S(1)}, f32[1,38,8,256]{3,2,1,0:T(8,128)S(1)}, u32[]{:S(2)}, u32[]{:S(2)}) collective-permute-start(f32[1,38,8,256]{3,2,1,0:T(8,128)S(1)} %pad_maximum_fusion.7), channel_id=1, source_target_pairs={{8,0},{16,8},{24,16},{9,1},{17,9},{25,17},{10,2},{18,10},{26,18},{... | collective-permute-start | bytes 933896 | tf_op jit(solution)/shard_map/ppermute | solution.py:278
  407.7 16.0 %copy-start.28 = (f32[4]{0:T(128)S(1)}, f32[4]{0:T(128)}, u32[]{:S(2)}) copy-start(f32[4]{0:T(128)} %constant.137.clone) | copy-start | bytes 52
  407.7 16.0 %copy-start.29 = (f32[4]{0:T(128)S(1)}, f32[4]{0:T(128)}, u32[]{:S(2)}) copy-start(f32[4]{0:T(128)} %constant.136.clone) | copy-start | bytes 52
  407.7 16.0 %copy-start.30 = (f32[4]{0:T(128)S(1)}, f32[4]{0:T(128)}, u32[]{:S(2)}) copy-start(f32[4]{0:T(128)} %constant.135.clone) | copy-start | bytes 52
  407.7 16.0 %copy-start.31 = (f32[4]{0:T(128)S(1)}, f32[4]{0:T(128)}, u32[]{:S(2)}) copy-start(f32[4]{0:T(128)} %constant.134.clone) | copy-start | bytes 52
  419.7 5.1 collective-permute-start.22
  422.4 5.3 collective-permute-start.23
  (15 other events, 52.7 us)

commit v3 on v2

--- a/solution.py
+++ b/solution.py
@@ -502,51 +502,61 @@
 
 
 def divergence_kernel(wind, opened, over, z_low, z_high, x_low, x_high, y_low, y_high, out, face_z):
-    k, depth = pl.program_id(0), pl.num_programs(0)
-    local_x, local_y = out.shape[1:]
+    step, steps = pl.program_id(0), pl.num_programs(0)
+    span, local_x, local_y = out.shape
     lane = lax.broadcasted_iota(jnp.int32, (1, LANES), 1)
-    before = None
-    for i in range(local_x // 8):
-        rows = slice(8 * i, 8 * i + 8)
-        cells = opened[0, 0, rows, :]
-        if i < local_x // 8 - 1:
-            after = opened[0, 0, 8 * i + 8 : 8 * i + 16, :]
-        else:
-            after = jnp.broadcast_to(x_high[0], cells.shape)
-        if before is None:
-            before = jnp.broadcast_to(x_low[0] * cells[0:1], cells.shape)
-        flux_x = wind[0, 0, rows, :] * (cells * next_x(cells, after))
-        right = pltpu.roll(y_high[rows, :], lax.rem(2 * LANES - 1 - k, LANES), 1)
-        left = pltpu.roll(y_low[rows, :], lax.rem(LANES - k, LANES), 1)
-        beside = next_y(cells)
-        cut = local_y - LANES
-        tail = jnp.where(lane == LANES - 1, right, beside[:, cut:])
-        beside = tail if cut == 0 else jnp.concatenate([beside[:, :cut], tail], 1)
-        flux_y = wind[1, 0, rows, :] * (cells * beside)
-        back = prev_y(flux_y)
-        head = jnp.where(lane == 0, left * cells[:, :LANES], back[:, :LANES])
-        back = head if cut == 0 else jnp.concatenate([head, back[:, LANES:]], 1)
-        above = jnp.where(k == depth - 1, z_high[rows, :], over[0, 0, rows, :])
-        flux_z = wind[2, 0, rows, :] * (cells * above)
-        below = jnp.where(k == 0, z_low[rows, :] * cells, face_z[rows, :])
-        out[0, rows, :] = (flux_x - prev_x(flux_x, before)) + (flux_y - back) + (flux_z - below)
-        face_z[rows, :] = flux_z
-        before = flux_x
+    for j in range(span):
+        k = step * span + j
+        before = None
+        for i in range(local_x // 8):
+            rows = slice(8 * i, 8 * i + 8)
+            cells = opened[0, j, rows, :]
+            if i < local_x // 8 - 1:
+                after = opened[0, j, 8 * i + 8 : 8 * i + 16, :]
+            else:
+                after = jnp.broadcast_to(x_high[j], cells.shape)
+            if before is None:
+                before = jnp.broadcast_to(x_low[j] * cells[0:1], cells.shape)
+            flux_x = wind[0, j, rows, :] * (cells * next_x(cells, after))
+            right = pltpu.roll(y_high[rows, :], lax.rem(2 * LANES - 1 - k, LANES), 1)
+            left = pltpu.roll(y_low[rows, :], lax.rem(LANES - k, LANES), 1)
+            beside = next_y(cells)
+            cut = local_y - LANES
+            tail = jnp.where(lane == LANES - 1, right, beside[:, cut:])
+            beside = tail if cut == 0 else jnp.concatenate([beside[:, :cut], tail], 1)
+            flux_y = wind[1, j, rows, :] * (cells * beside)
+            back = prev_y(flux_y)
+            head = jnp.where(lane == 0, left * cells[:, :LANES], back[:, :LANES])
+            back = head if cut == 0 else jnp.concatenate([head, back[:, LANES:]], 1)
+            if j < span - 1:
+                above = opened[0, j + 1, rows, :]
+            else:
+                above = jnp.where(step == steps - 1, z_high[rows, :], over[0, 0, rows, :])
+            flux_z = wind[2, j, rows, :] * (cells * above)
+            below = face_z[rows, :]
+            if j == 0:
+                below = jnp.where(step == 0, z_low[rows, :] * cells, below)
+            out[j, rows, :] = (flux_x - prev_x(flux_x, before)) + (flux_y - back) + (flux_z - below)
+            face_z[rows, :] = flux_z
+            before = flux_x
 
 
 def divergence(wind, opened, edges):
     local_z, local_x, local_y = wind.shape[1:]
     plane = pl.BlockSpec((local_x, local_y), lambda k: (0, 0))
-    line = pl.BlockSpec((1, 1, local_y), lambda k: (k, 0, 0))
+    span = 4
+    line = pl.BlockSpec((span, 1, local_y), lambda k: (k, 0, 0))
     pack = pl.BlockSpec((local_x, LANES), lambda k: (0, 0))
-    one = (1, 1, local_x, local_y)
     return pl.pallas_call(
         divergence_kernel,
-        grid=(local_z,),
+        grid=(local_z // span,),
         in_specs=[
-            pl.BlockSpec((3, 1, local_x, local_y), lambda k: (0, k, 0, 0)),
-            pl.BlockSpec(one, lambda k: (0, k, 0, 0)),
-            pl.BlockSpec(one, lambda k: (0, jnp.minimum(k + 1, local_z - 1), 0, 0)),
+            pl.BlockSpec((3, span, local_x, local_y), lambda k: (0, k, 0, 0)),
+            pl.BlockSpec((1, span, local_x, local_y), lambda k: (0, k, 0, 0)),
+            pl.BlockSpec(
+                (1, 1, local_x, local_y),
+                lambda k: (0, jnp.minimum(k * span + span, local_z - 1), 0, 0),
+            ),
             plane,
             plane,
             line,
@@ -554,7 +564,7 @@
             pack,
             pack,
         ],
-        out_specs=pl.BlockSpec((1, local_x, local_y), lambda k: (k, 0, 0)),
+        out_specs=pl.BlockSpec((span, local_x, local_y), lambda k: (k, 0, 0)),
         out_shape=jax.ShapeDtypeStruct((local_z, local_x, local_y), F32),
         scratch_shapes=[pltpu.VMEM((local_x, local_y), F32)],
         compiler_params=params(),

time: 686 us -> 691 us (level)
  transfers between devices with their start and end apart: 27 -> 27, of which waited for: 18 -> 18; matrix products, arithmetic and copies ran while one was open for 3% -> 3% of each run, Pallas kernels for 9% -> 10%
where the time goes in v3:
time: 691 us; the launch traced here: 689 us
  Pallas kernels  386 us (56%)
  waiting for transfers between devices  118 us (17%)
  starting transfers between devices  83.8 us (12%)
  blocking collectives  64.3 us (9%)
  local copies, waits for them, and re-layouts  19.8 us (3%)
  other arithmetic  16.2 us (2%)
    pallas_call x1, Pallas kernels, transport(): pl.pallas_call(functools.partial(transport_kernel, local_z, n), grid=(loc...  255 us
    all_to_all x1, blocking collectives, solve(): blocks = lax.all_to_all(blocks, 'gx', 0, 0)  53.6 us
    all_to_all x2, waiting for transfers between devices, solve(): blocks = lax.all_to_all(blocks, ('gz', 'gx'), 0, 0)  43.7 us
    ppermute x12, waiting for transfers between devices, shift_pair(): lax.ppermute(high_part, axis, up)  40.3 us
    ppermute x12, starting transfers between devices, shift_pair(): lax.ppermute(high_part, axis, up)  33.4 us
    ppermute x12, starting transfers between devices, shift_pair(): lax.ppermute(low_part, axis, down)  30.1 us
    pallas_call x3, Pallas kernels, y_pack(): pl.pallas_call(functools.partial(pack_kernel, groups, span), grid=(local_...  29.6 us
    pallas_call x1, Pallas kernels, divergence(): pl.pallas_call(divergence_kernel, grid=(local_z // span,), in_specs=[pl.B...  29.4 us
  transfers between devices with their start and end apart: 27, of which 18 were waited for; matrix products, arithmetic and copies ran while one was open for 3% of the time, Pallas kernels for 10%

profile of v3, /device:TPU:5, one launch (start us, length us, event | category | flops | bytes accessed | tf_op | source)
XLA Modules:
  0.0 689.2 jit_solution(7748674750312338047)
XLA Ops:
  0.6 2.6 subtract_bitcast_fusion.first.last.opened.over.refs_1_.refs_3_.refs_8_
  8.9 2.0 pad_maximum_fusion
  13.2 4.2 collective-permute-start.7
  18.4 4.0 collective-permute-start.3
  22.4 4.6 shard_map.293
  27.1 4.0 collective-permute-start.4
  32.4 3.3 collective-permute-start.2
  38.0 29.4 %shard_map.294 = f32[32,128,256]{2,1,0:T(8,128)} custom-call(f32[3,32,128,256]{3,2,1,0:T(8,128)} %refs_7_.1, f32[1,32,128,256]{3,2,1,0:T(8,128)} %copy-done, f32[1,32,128,256]{3,2,1,0:T(8,128)} %copy-done, f32[128,256]{1,0:T(8,128)} %copy-done.20, f32[128,256]{1,0:T(8,128)} %copy-done.19, f32[32,1,256]{2,1,0:T(1,128)} %copy-done.27, ...), custom_call_target="tpu_custom_call" | custom-call | tf_op jit(solution)/shard_map/pallas_call | solution.py:550
  67.4 5.2 all-to-all-start
  72.6 2.2 fusion.35
  76.1 6.3 collective-permute-start.9
  84.2 2.7 fusion.36
  86.9 3.0 fusion.34
  89.9 22.8 %collective-permute-done.8.refs_2_.refs_3_.refs_1_ = f32[4,3,128,256]{3,2,1,0:T(8,128)} collective-permute-done((f32[4,3,128,256]{3,2,1,0:T(8,128)S(1)}, f32[4,3,128,256]{3,2,1,0:T(8,128)}, u32[]{:S(2)}, u32[]{:S(2)}) %collective-permute-start.8) | collective-permute-done | bytes 1572896 | tf_op jit(solution)/shard_map/ppermute | solution.py:278
  112.8 1.9 collective-permute-done.9.refs_4_.refs_5_.refs_2_
  114.7 4.8 all-to-all-done.x_ref
  122.8 3.4 collective-permute-start.10
  127.3 2.0 collective-permute-start.11
  130.5 3.6 collective-permute-start.12
  137.2 8.9 %shard_map.295 = f32[8,8,64,256]{3,2,1,0:T(8,128)} custom-call(f32[4,8,128,256]{3,2,1,0:T(8,128)} %all-to-all-done.x_ref, bf16[512,512]{1,0:T(8,128)(2,1)} %constant.120.clone.refs_0_, bf16[512,512]{1,0:T(8,128)(2,1)} %constant.121.clone.refs_1_), custom_call_target="tpu_custom_call" | custom-call | tf_op jit(solution)/shard_map/pallas_call | solution.py:103
  146.1 7.5 %collective-permute-done.12.refs_6_.refs_7_.refs_3_ = f32[4,38,8,256]{3,2,1,0:T(8,128)} collective-permute-done((f32[4,38,8,256]{3,2,1,0:T(8,128)}, f32[4,38,8,256]{3,2,1,0:T(8,128)}, u32[]{:S(2)}, u32[]{:S(2)}) %collective-permute-start.12) | collective-permute-done | bytes 1245216 | tf_op jit(solution)/shard_map/ppermute | solution.py:278
  153.6 5.7 collective-permute-done.13.refs_8_.refs_9_.refs_4_
  159.3 4.6 all-to-all-start.1
  164.8 2.0 copy.50.lam_ref
  166.7 12.3 %shard_map.297 = (f32[4,144,128]{2,1,0:T(8,128)}, f32[4,144,128]{2,1,0:T(8,128)}) custom-call(f32[4,32,128,256]{3,2,1,0:T(8,128)} %refs_0_.7, f32[4,32,128,256]{3,2,1,0:T(8,128)} %refs_0_.7, f32[4,3,128,256]{3,2,1,0:T(8,128)} %collective-permute-done.8.refs_2_.refs_3_.refs_1_, f32[4,3,128,256]{3,2,1,0:T(8,128)} %collective-permute-done.8.refs_2_.refs_3_.refs_1_, ...), custom_call_target="tpu_custom_call" | custom-call | tf_op jit(solution)/shard_map/pallas_call | solution.py:370
  179.1 12.2 %shard_map.296 = (f32[4,144,128]{2,1,0:T(8,128)}, f32[4,144,128]{2,1,0:T(8,128)}) custom-call(f32[3,32,128,256]{3,2,1,0:T(8,128)} %refs_7_.1, f32[1,32,128,256]{3,2,1,0:T(8,128)} %copy-done, f32[3,32,128,256]{3,2,1,0:T(8,128)} %refs_7_.1, f32[1,32,128,256]{3,2,1,0:T(8,128)} %copy-done, f32[4,3,128,256]{3,2,1,0:T(8,128)} %copy-done.2, ...), custom_call_target="tpu_custom_call" | custom-call | tf_op jit(solution)/shard_map/pallas_call | solution.py:370
  191.3 17.5 %all-to-all-done.1 = f32[8,8,64,256]{3,2,1,0:T(8,128)} async-done(((f32[8,8,64,256]{3,2,1,0:T(8,128)}), f32[8,8,64,256]{3,2,1,0:T(8,128)}, u32[]{:S(2)}, u32[]{:S(2)}) %all-to-all-start.1) | async-done | bytes 4194336 | tf_op jit(solution)/shard_map/all_to_all | solution.py:197
  208.8 18.4 %shard_map.298 = (f32[64,64,256]{2,1,0:T(8,128)}, f32[8,8,512]{2,1,0:T(8,128)}) custom-call(f32[64,64,256]{2,1,0:T(8,128)} %bitcast.6.x_ref, bf16[256,256]{1,0:T(8,128)(2,1)} %constant.115.clone.s_high, bf16[256,256]{1,0:T(8,128)(2,1)} %constant.116.clone.s_low, bf16[512,512]{1,0:T(8,128)(2,1)} %constant.117.clone.k_high, ...), custom_call_target="tpu_custom_call" | custom-call | tf_op jit(solution)/shard_map/pallas_call | solution.py:213
  228.1 10.7 %all-gather = f32[32,2,512]{2,1,0:T(2,128)S(1)} all-gather(f32[8,2,512]{2,1,0:T(2,128)S(1)} %slice.155), channel_id=2, replica_groups=mesh['gx'=4,'gy'=4,'gz'=2] {'gy'}, dimensions={0}, use_global_device_ids=true | all-gather | bytes 163840 | tf_op jit(solution)/shard_map/all_gather | solution.py:225
  242.6 28.8 %shard_map.299 = f32[64,64,256]{2,1,0:T(8,128)} custom-call(f32[64,64,256]{2,1,0:T(8,128)} %get-tuple-element.63.b_ref, f32[8,8,512]{2,1,0:T(8,128)} %maximum_maximum_fusion.ab_ref, f32[256,256]{1,0:T(8,128)} %constant.132.clone.s_ref, f32[512,512]{1,0:T(8,128)} %constant.119.clone.k_ref, f32[8,512,1]{2,1,0:T(8,128)} %copy.50.lam_ref, ...), custom_call_target="tpu_custom_call" | custom-call | tf_op jit(solution)/shard_map/pallas_call | solution.py:255
  271.4 10.4 %all-to-all-start.2 = ((f32[8,8,64,256]{3,2,1,0:T(8,128)}), f32[8,8,64,256]{3,2,1,0:T(8,128)}, u32[]{:S(2)}, u32[]{:S(2)}) async-start(f32[8,8,64,256]{3,2,1,0:T(8,128)} %bitcast.104), calls=%async_computation.2 | async-start | bytes 8388608 | tf_op jit(solution)/shard_map/all_to_all | solution.py:265
  281.9 2.7 collective-permute-start.14
  285.9 4.0 collective-permute-start.16
  291.2 3.2 collective-permute-done.15.refs_14_
  294.4 2.5 collective-permute-done.16.refs_5_
  296.9 4.1 collective-permute-done.17.refs_6_
  301.0 26.2 %all-to-all-done.2.x_ref = f32[8,8,64,256]{3,2,1,0:T(8,128)} async-done(((f32[8,8,64,256]{3,2,1,0:T(8,128)}), f32[8,8,64,256]{3,2,1,0:T(8,128)}, u32[]{:S(2)}, u32[]{:S(2)}) %all-to-all-start.2) | async-done | bytes 4194336 | tf_op jit(solution)/shard_map/all_to_all | solution.py:265
  327.2 11.4 %shard_map.300 = f32[4,8,128,256]{3,2,1,0:T(8,128)} custom-call(f32[8,8,64,256]{3,2,1,0:T(8,128)} %all-to-all-done.2.x_ref, f32[512,512]{1,0:T(8,128)} %constant.133.clone.refs_0_), custom_call_target="tpu_custom_call" | custom-call | tf_op jit(solution)/shard_map/pallas_call | solution.py:103
  338.7 53.6 %all_to_all.20 = f32[4,8,128,256]{3,2,1,0:T(8,128)S(1)} all-to-all(f32[4,8,128,256]{3,2,1,0:T(8,128)} %shard_map.300), channel_id=1, replica_groups=mesh['gx'=4,'gy'=4,'gz'=2] {'gx'}, dimensions={0} | all-to-all | bytes 8388608 | tf_op jit(solution)/shard_map/all_to_all | solution.py:268
  392.4 3.3 collective-permute-start.19
  397.1 6.0 collective-permute-done.19.refs_4_.refs_5_.refs_17_
  403.0 3.8 collective-permute-done.18.refs_2_.refs_3_.refs_16_
  406.9 4.5 collective-permute-start.20
  415.3 4.4 collective-permute-done.21.refs_8_.refs_9_.refs_19_
  420.5 5.1 shard_map.301
  425.5 2.7 collective-permute-start.22
  430.6 2.9 collective-permute-done.23.refs_21_
  434.2 254.9 %shard_map.302 = (f32[3,32,128,256]{3,2,1,0:T(8,128)}, f32[4,32,128,256]{3,2,1,0:T(8,128)}) custom-call(f32[4,32,128,256]{3,2,1,0:T(8,128)} %refs_0_.7, f32[4,3,128,256]{3,2,1,0:T(8,128)} %collective-permute-done.8.refs_2_.refs_3_.refs_1_, f32[4,3,128,256]{3,2,1,0:T(8,128)} %collective-permute-done.9.refs_4_.refs_5_.refs_2_, ...), custom_call_target="tpu_custom_call" | custom-call | tf_op jit(solution)/shard_map/pallas_call | solution.py:774
  (127 shorter events, 41.2 us)
Async XLA Ops:
  3.2 14.2 %copy-start = (f32[1,32,128,256]{3,2,1,0:T(8,128)}, f32[1,32,128,256]{3,2,1,0:T(8,128)S(1)}, u32[]{:S(2)}) copy-start(f32[1,32,128,256]{3,2,1,0:T(8,128)S(1)} %subtract_bitcast_fusion.first.last.opened.over.refs_1_.refs_3_.refs_8_) | copy-start | bytes 12582916
  4.3 6.6 collective-permute-start.1
  5.7 6.3 collective-permute-start
  10.9 16.2 %copy-start.19 = (f32[128,256]{1,0:T(8,128)}, f32[128,256]{1,0:T(8,128)S(1)}, u32[]{:S(2)}) copy-start(f32[128,256]{1,0:T(8,128)S(1)} %collective-permute-done.1.z_high) | copy-start | bytes 393220
  11.9 15.2 %copy-start.20 = (f32[128,256]{1,0:T(8,128)}, f32[128,256]{1,0:T(8,128)S(1)}, u32[]{:S(2)}) copy-start(f32[128,256]{1,0:T(8,128)S(1)} %collective-permute-done.z_low) | copy-start | bytes 393220
  11.9 55.5 %collective-permute-start.6 = (f32[4,3,128,256]{3,2,1,0:T(8,128)}, f32[4,3,128,256]{3,2,1,0:T(8,128)S(1)}, u32[]{:S(2)}, u32[]{:S(2)}) collective-permute-start(f32[4,3,128,256]{3,2,1,0:T(8,128)} %get-tuple-element.41), channel_id=1, source_target_pairs={{0,1},{2,3},{4,5},{6,7},{8,9},{10,11},{12,13},{14,15},{16,17},{18,... | collective-permute-start | bytes 4718600 | tf_op jit(solution)/shard_map/ppermute | solution.py:278
  13.2 54.2 %collective-permute-start.7 = (f32[4,3,128,256]{3,2,1,0:T(8,128)}, f32[4,3,128,256]{3,2,1,0:T(8,128)S(1)}, u32[]{:S(2)}, u32[]{:S(2)}) collective-permute-start(f32[4,3,128,256]{3,2,1,0:T(8,128)} %get-tuple-element.42), channel_id=1, source_target_pairs={{1,0},{3,2},{5,4},{7,6},{9,8},{11,10},{13,12},{15,14},{17,16},{19,... | collective-permute-start | bytes 4718600 | tf_op jit(solution)/shard_map/ppermute | solution.py:278
  18.4 14.0 %collective-permute-start.3 = (f32[32,1,256]{2,1,0:T(1,128)S(1)}, f32[32,1,256]{2,1,0:T(1,128)S(1)}, u32[]{:S(2)}, u32[]{:S(2)}) collective-permute-start(f32[32,1,256]{2,1,0:T(1,128)S(1)} %get-tuple-element.100), channel_id=1, source_target_pairs={{8,0},{16,8},{24,16},{9,1},{17,9},{25,17},{10,2},{18,10},{26,18},{... | collective-permute-start | bytes 98312 | tf_op jit(solution)/shard_map/ppermute | solution.py:278
  27.1 9.7 %collective-permute-start.4 = (f32[128,128]{1,0:T(8,128)}, f32[128,128]{1,0:T(8,128)S(1)}, u32[]{:S(2)}, u32[]{:S(2)}) collective-permute-start(f32[128,128]{1,0:T(8,128)} %get-tuple-element.39), channel_id=1, source_target_pairs={{0,2},{2,4},{4,6},{1,3},{3,5},{5,7},{8,10},{10,12},{12,14},{9,11},... | collective-permute-start | bytes 196616 | tf_op jit(solution)/shard_map/ppermute | solution.py:278
  31.1 6.1 collective-permute-start.5
  32.4 4.3 collective-permute-start.2
  67.4 54.1 %copy-start.2 = (f32[4,3,128,256]{3,2,1,0:T(8,128)}, f32[4,3,128,256]{3,2,1,0:T(8,128)S(1)}, u32[]{:S(2)}) copy-start(f32[4,3,128,256]{3,2,1,0:T(8,128)S(1)} %collective-permute-done.6.refs_4_.refs_5_.refs_9_) | copy-start | bytes 4718596
  67.4 54.2 %copy-start.3 = (f32[4,3,128,256]{3,2,1,0:T(8,128)}, f32[4,3,128,256]{3,2,1,0:T(8,128)S(1)}, u32[]{:S(2)}) copy-start(f32[4,3,128,256]{3,2,1,0:T(8,128)S(1)} %collective-permute-done.7.refs_6_.refs_7_.refs_10_) | copy-start | bytes 4718596
  67.4 52.1 %all-to-all-start = ((f32[4,8,128,256]{3,2,1,0:T(8,128)}), f32[4,8,128,256]{3,2,1,0:T(8,128)}, u32[]{:S(2)}, u32[]{:S(2)}) async-start(f32[4,8,128,256]{3,2,1,0:T(8,128)} %bitcast.103), calls=%async_computation | async-start | bytes 8388608 | tf_op jit(solution)/shard_map/all_to_all | solution.py:190
  74.8 38.0 %collective-permute-start.8 = (f32[4,3,128,256]{3,2,1,0:T(8,128)S(1)}, f32[4,3,128,256]{3,2,1,0:T(8,128)}, u32[]{:S(2)}, u32[]{:S(2)}) collective-permute-start(f32[4,3,128,256]{3,2,1,0:T(8,128)S(1)} %get-tuple-element.46), channel_id=1, source_target_pairs={{0,1},{2,3},{4,5},{6,7},{8,9},{10,11},{12,13},{14,15},{16,17},{18,... | collective-permute-start | bytes 4718600 | tf_op jit(solution)/shard_map/ppermute | solution.py:278
  76.1 38.6 %collective-permute-start.9 = (f32[4,3,128,256]{3,2,1,0:T(8,128)S(1)}, f32[4,3,128,256]{3,2,1,0:T(8,128)}, u32[]{:S(2)}, u32[]{:S(2)}) collective-permute-start(f32[4,3,128,256]{3,2,1,0:T(8,128)S(1)} %get-tuple-element.47), channel_id=1, source_target_pairs={{1,0},{3,2},{5,4},{7,6},{9,8},{11,10},{13,12},{15,14},{17,16},{19,... | collective-permute-start | bytes 4718600 | tf_op jit(solution)/shard_map/ppermute | solution.py:278
  122.8 23.4 %collective-permute-start.10 = (f32[4,38,8,256]{3,2,1,0:T(8,128)}, f32[4,38,8,256]{3,2,1,0:T(8,128)S(1)}, u32[]{:S(2)}, u32[]{:S(2)}) collective-permute-start(f32[4,38,8,256]{3,2,1,0:T(8,128)} %pad_maximum_fusion.2), channel_id=1, source_target_pairs={{0,8},{8,16},{16,24},{1,9},{9,17},{17,25},{2,10},{10,18},{18,26},{... | collective-permute-start | bytes 3735560 | tf_op jit(solution)/shard_map/ppermute | solution.py:278
  127.3 18.8 %collective-permute-start.11 = (f32[4,38,8,256]{3,2,1,0:T(8,128)}, f32[4,38,8,256]{3,2,1,0:T(8,128)S(1)}, u32[]{:S(2)}, u32[]{:S(2)}) collective-permute-start(f32[4,38,8,256]{3,2,1,0:T(8,128)} %pad_maximum_fusion.3), channel_id=1, source_target_pairs={{8,0},{16,8},{24,16},{9,1},{17,9},{25,17},{10,2},{18,10},{26,18},{... | collective-permute-start | bytes 3735560 | tf_op jit(solution)/shard_map/ppermute | solution.py:278
  130.5 23.1 %collective-permute-start.12 = (f32[4,38,8,256]{3,2,1,0:T(8,128)}, f32[4,38,8,256]{3,2,1,0:T(8,128)}, u32[]{:S(2)}, u32[]{:S(2)}) collective-permute-start(f32[4,38,8,256]{3,2,1,0:T(8,128)} %pad_maximum_fusion.4), channel_id=1, source_target_pairs={{0,8},{8,16},{16,24},{1,9},{9,17},{17,25},{2,10},{10,18},{18,26},{... | collective-permute-start | bytes 3735560 | tf_op jit(solution)/shard_map/ppermute | solution.py:278
  135.3 24.0 %collective-permute-start.13 = (f32[4,38,8,256]{3,2,1,0:T(8,128)}, f32[4,38,8,256]{3,2,1,0:T(8,128)}, u32[]{:S(2)}, u32[]{:S(2)}) collective-permute-start(f32[4,38,8,256]{3,2,1,0:T(8,128)} %pad_maximum_fusion.5), channel_id=1, source_target_pairs={{8,0},{16,8},{24,16},{9,1},{17,9},{25,17},{10,2},{18,10},{26,18},{... | collective-permute-start | bytes 3735560 | tf_op jit(solution)/shard_map/ppermute | solution.py:278
  146.1 13.2 %copy-start.4 = (f32[4,38,8,256]{3,2,1,0:T(8,128)}, f32[4,38,8,256]{3,2,1,0:T(8,128)S(1)}, u32[]{:S(2)}) copy-start(f32[4,38,8,256]{3,2,1,0:T(8,128)S(1)} %collective-permute-done.10.refs_8_.refs_9_.refs_11_) | copy-start | bytes 3735556
  146.1 13.2 %copy-start.5 = (f32[4,38,8,256]{3,2,1,0:T(8,128)}, f32[4,38,8,256]{3,2,1,0:T(8,128)S(1)}, u32[]{:S(2)}) copy-start(f32[4,38,8,256]{3,2,1,0:T(8,128)S(1)} %collective-permute-done.11.refs_10_.refs_11_.refs_12_) | copy-start | bytes 3735556
  159.3 49.4 %all-to-all-start.1 = ((f32[8,8,64,256]{3,2,1,0:T(8,128)}), f32[8,8,64,256]{3,2,1,0:T(8,128)}, u32[]{:S(2)}, u32[]{:S(2)}) async-start(f32[8,8,64,256]{3,2,1,0:T(8,128)} %shard_map.295), calls=%async_computation.1 | async-start | bytes 8388608 | tf_op jit(solution)/shard_map/all_to_all | solution.py:197
  271.4 13.2 %copy-start.34 = (f32[4,144,128]{2,1,0:T(8,128)S(1)}, f32[4,144,128]{2,1,0:T(8,128)}, u32[]{:S(2)}) copy-start(f32[4,144,128]{2,1,0:T(8,128)} %get-tuple-element.66) | copy-start | bytes 884740
  271.4 14.5 %copy-start.33 = (f32[4,144,128]{2,1,0:T(8,128)S(1)}, f32[4,144,128]{2,1,0:T(8,128)}, u32[]{:S(2)}) copy-start(f32[4,144,128]{2,1,0:T(8,128)} %get-tuple-element.67) | copy-start | bytes 884740
  271.4 18.5 %copy-start.32 = (f32[4,144,128]{2,1,0:T(8,128)S(1)}, f32[4,144,128]{2,1,0:T(8,128)}, u32[]{:S(2)}) copy-start(f32[4,144,128]{2,1,0:T(8,128)} %get-tuple-element.68) | copy-start | bytes 884740
  271.4 55.8 %all-to-all-start.2 = ((f32[8,8,64,256]{3,2,1,0:T(8,128)}), f32[8,8,64,256]{3,2,1,0:T(8,128)}, u32[]{:S(2)}, u32[]{:S(2)}) async-start(f32[8,8,64,256]{3,2,1,0:T(8,128)} %bitcast.104), calls=%async_computation.2 | async-start | bytes 8388608 | tf_op jit(solution)/shard_map/all_to_all | solution.py:265
  281.9 9.4 %collective-permute-start.14 = (f32[4,144,128]{2,1,0:T(8,128)S(1)}, f32[4,144,128]{2,1,0:T(8,128)S(1)}, u32[]{:S(2)}, u32[]{:S(2)}) collective-permute-start(f32[4,144,128]{2,1,0:T(8,128)S(1)} %copy-done.35), channel_id=1, source_target_pairs={{0,2},{2,4},{4,6},{1,3},{3,5},{5,7},{8,10},{10,12},{12,14},{9,11},... | collective-permute-start | bytes 884744 | tf_op jit(solution)/shard_map/ppermute | solution.py:278
  284.6 9.8 %collective-permute-start.15 = (f32[4,144,128]{2,1,0:T(8,128)S(1)}, f32[4,144,128]{2,1,0:T(8,128)S(1)}, u32[]{:S(2)}, u32[]{:S(2)}) collective-permute-start(f32[4,144,128]{2,1,0:T(8,128)S(1)} %copy-done.34), channel_id=1, source_target_pairs={{2,0},{4,2},{6,4},{3,1},{5,3},{7,5},{10,8},{12,10},{14,12},{11,9},... | collective-permute-start | bytes 884744 | tf_op jit(solution)/shard_map/ppermute | solution.py:278
  285.9 11.0 %collective-permute-start.16 = (f32[4,144,128]{2,1,0:T(8,128)S(1)}, f32[4,144,128]{2,1,0:T(8,128)S(1)}, u32[]{:S(2)}, u32[]{:S(2)}) collective-permute-start(f32[4,144,128]{2,1,0:T(8,128)S(1)} %copy-done.33), channel_id=1, source_target_pairs={{0,2},{2,4},{4,6},{1,3},{3,5},{5,7},{8,10},{10,12},{12,14},{9,11},... | collective-permute-start | bytes 884744 | tf_op jit(solution)/shard_map/ppermute | solution.py:278
  289.9 11.1 %collective-permute-start.17 = (f32[4,144,128]{2,1,0:T(8,128)S(1)}, f32[4,144,128]{2,1,0:T(8,128)S(1)}, u32[]{:S(2)}, u32[]{:S(2)}) collective-permute-start(f32[4,144,128]{2,1,0:T(8,128)S(1)} %copy-done.32), channel_id=1, source_target_pairs={{2,0},{4,2},{6,4},{3,1},{5,3},{7,5},{10,8},{12,10},{14,12},{11,9},... | collective-permute-start | bytes 884744 | tf_op jit(solution)/shard_map/ppermute | solution.py:278
  291.2 47.4 %copy-start.15 = (f32[4,144,128]{2,1,0:T(8,128)}, f32[4,144,128]{2,1,0:T(8,128)S(1)}, u32[]{:S(2)}) copy-start(f32[4,144,128]{2,1,0:T(8,128)S(1)} %collective-permute-done.14.refs_13_) | copy-start | bytes 884740
  294.4 44.3 %copy-start.16 = (f32[4,144,128]{2,1,0:T(8,128)}, f32[4,144,128]{2,1,0:T(8,128)S(1)}, u32[]{:S(2)}) copy-start(f32[4,144,128]{2,1,0:T(8,128)S(1)} %collective-permute-done.15.refs_14_) | copy-start | bytes 884740
  296.9 41.8 %copy-start.17 = (f32[4,144,128]{2,1,0:T(8,128)}, f32[4,144,128]{2,1,0:T(8,128)S(1)}, u32[]{:S(2)}) copy-start(f32[4,144,128]{2,1,0:T(8,128)S(1)} %collective-permute-done.16.refs_5_) | copy-start | bytes 884740
  301.0 37.7 %copy-start.18 = (f32[4,144,128]{2,1,0:T(8,128)}, f32[4,144,128]{2,1,0:T(8,128)S(1)}, u32[]{:S(2)}) copy-start(f32[4,144,128]{2,1,0:T(8,128)S(1)} %collective-permute-done.17.refs_6_) | copy-start | bytes 884740
  392.4 21.0 %copy-start.21 = (s32[128,256]{1,0:T(8,128)S(1)}, s32[128,256]{1,0:T(8,128)}, u32[]{:S(2)}) copy-start(s32[128,256]{1,0:T(8,128)} %param.32) | copy-start | bytes 393220
  392.4 10.6 %collective-permute-start.19 = (f32[1,3,128,256]{3,2,1,0:T(8,128)S(1)}, f32[1,3,128,256]{3,2,1,0:T(8,128)S(1)}, u32[]{:S(2)}, u32[]{:S(2)}) collective-permute-start(f32[1,3,128,256]{3,2,1,0:T(8,128)S(1)} %get-tuple-element.94), channel_id=1, source_target_pairs={{1,0},{3,2},{5,4},{7,6},{9,8},{11,10},{13,12},{15,14},{17,16},{19,... | collective-permute-start | bytes 1179656 | tf_op jit(solution)/shard_map/ppermute | solution.py:278
  395.7 11.2 %collective-permute-start.18 = (f32[1,3,128,256]{3,2,1,0:T(8,128)S(1)}, f32[1,3,128,256]{3,2,1,0:T(8,128)S(1)}, u32[]{:S(2)}, u32[]{:S(2)}) collective-permute-start(f32[1,3,128,256]{3,2,1,0:T(8,128)S(1)} %get-tuple-element.95), channel_id=1, source_target_pairs={{0,1},{2,3},{4,5},{6,7},{8,9},{10,11},{12,13},{14,15},{16,17},{18,... | collective-permute-start | bytes 1179656 | tf_op jit(solution)/shard_map/ppermute | solution.py:278
  403.0 16.7 %copy-start.8 = (f32[1,3,128,256]{3,2,1,0:T(8,128)}, f32[1,3,128,256]{3,2,1,0:T(8,128)S(1)}, u32[]{:S(2)}) copy-start(f32[1,3,128,256]{3,2,1,0:T(8,128)S(1)} %collective-permute-done.19.refs_4_.refs_5_.refs_17_) | copy-start | bytes 1179652
  406.9 12.8 %copy-start.9 = (f32[1,3,128,256]{3,2,1,0:T(8,128)}, f32[1,3,128,256]{3,2,1,0:T(8,128)S(1)}, u32[]{:S(2)}) copy-start(f32[1,3,128,256]{3,2,1,0:T(8,128)S(1)} %collective-permute-done.18.refs_2_.refs_3_.refs_16_) | copy-start | bytes 1179652
  406.9 8.4 %collective-permute-start.20 = (f32[1,38,8,256]{3,2,1,0:T(8,128)S(1)}, f32[1,38,8,256]{3,2,1,0:T(8,128)S(1)}, u32[]{:S(2)}, u32[]{:S(2)}) collective-permute-start(f32[1,38,8,256]{3,2,1,0:T(8,128)S(1)} %pad_maximum_fusion.6), channel_id=1, source_target_pairs={{0,8},{8,16},{16,24},{1,9},{9,17},{17,25},{2,10},{10,18},{18,26},{... | collective-permute-start | bytes 933896 | tf_op jit(solution)/shard_map/ppermute | solution.py:278
  411.5 8.2 %collective-permute-start.21 = (f32[1,38,8,256]{3,2,1,0:T(8,128)S(1)}, f32[1,38,8,256]{3,2,1,0:T(8,128)S(1)}, u32[]{:S(2)}, u32[]{:S(2)}) collective-permute-start(f32[1,38,8,256]{3,2,1,0:T(8,128)S(1)} %pad_maximum_fusion.7), channel_id=1, source_target_pairs={{8,0},{16,8},{24,16},{9,1},{17,9},{25,17},{10,2},{18,10},{26,18},{... | collective-permute-start | bytes 933896 | tf_op jit(solution)/shard_map/ppermute | solution.py:278
  413.5 16.0 %copy-start.28 = (f32[4]{0:T(128)S(1)}, f32[4]{0:T(128)}, u32[]{:S(2)}) copy-start(f32[4]{0:T(128)} %constant.137.clone) | copy-start | bytes 52
  413.5 16.0 %copy-start.29 = (f32[4]{0:T(128)S(1)}, f32[4]{0:T(128)}, u32[]{:S(2)}) copy-start(f32[4]{0:T(128)} %constant.136.clone) | copy-start | bytes 52
  413.6 16.0 %copy-start.30 = (f32[4]{0:T(128)S(1)}, f32[4]{0:T(128)}, u32[]{:S(2)}) copy-start(f32[4]{0:T(128)} %constant.135.clone) | copy-start | bytes 52
  413.6 16.0 %copy-start.31 = (f32[4]{0:T(128)S(1)}, f32[4]{0:T(128)}, u32[]{:S(2)}) copy-start(f32[4]{0:T(128)} %constant.134.clone) | copy-start | bytes 52
  425.5 5.1 collective-permute-start.22
  428.2 5.3 collective-permute-start.23
  (15 other events, 52.7 us)
